TPU v7x, 512 devices: a whole 4x4x16 slice. The times are simulated.
512 devices in a mesh: date: 32 (over y_hi, z), row: 8 (over x, core), col: 2 (over y_lo).
Axes of the slice: x: 4, y: 4 (y_hi: 2, y_lo: 2; y = y_hi * 2 + y_lo), z: 16, core: 2. Of those that a mesh axis runs over, the one named last changes fastest.
Arguments:
- images: float32 [64, 2, 384, 1536], P('date', None, 'row', 'col'), may hold values from -8 to 8
- secondaries: int32 [64, 3], P('date'), may hold values from 0 to 63, as said below
Outputs:
- filtered: float32 [64, 3, 2, 192, 192], P('date', None, None, 'row', 'col')
- coherence: float32 [64, 3, 2, 192, 192], P('date', None, None, 'row', 'col')
Inputs may be any that keep to these rules, and one draw needn't show every extreme that they name: secondaries[k, l] = (k + o) mod 64 for 3 distinct offsets o of 1 to 4, rising with l; the offset 4 occurs in every draw.
All inputs are finite; a program needn't handle non-finite values.
Results may differ from a plain program's by a relative error of at most 0.00005.
Values sent between devices are 32-bit elements; how exact they have to be, the bound alone decides.
No kernel may reach another device: no remote copies, remote signals or barrier semaphores. Data moves between devices by JAX's collectives and lax.ppermute only.
A program may use at most 128 MiB of HBM per device.

v0:
```python
import math

import jax
import jax.numpy as jnp
from jax import lax
from jax.sharding import PartitionSpec as P

LOOK_R = 2
LOOK_C = 8
PATCH = 32
KEEP = 24
MARGIN = 4


def shifted(value, axis, steps):
    count = lax.axis_size(axis)
    pairs = [(source, (source + steps) % count) for source in range(count)]
    return lax.ppermute(value, axis, pairs)


def with_halo(block, sides, width):
    for axis, dim in sides:
        count = lax.axis_size(axis)
        forward = [(i, i + 1) for i in range(count - 1)]
        backward = [(target, source) for source, target in forward]
        low = lax.ppermute(
            lax.slice_in_dim(block, block.shape[dim] - width, None, axis=dim), axis, forward
        )
        high = lax.ppermute(lax.slice_in_dim(block, 0, width, axis=dim), axis, backward)
        block = jnp.concatenate([low, block, high], axis=dim)
    return block


def multilook(values):
    extent = values.shape
    blocks = values.reshape(
        extent[:-2] + (extent[-2] // LOOK_R, LOOK_R, extent[-1] // LOOK_C, LOOK_C)
    )
    return blocks.mean(axis=(-3, -1))


def window_last(grid_values, block_count):
    leading = grid_values.shape[:-1]
    head_part = grid_values[..., : block_count * KEEP].reshape(leading + (block_count, KEEP))
    widths = [(0, 0)] * (grid_values.ndim - 1) + [(0, 2 * KEEP - PATCH)]
    extended = jnp.pad(grid_values, widths)
    tail_part = extended[..., KEEP:].reshape(leading + (block_count, KEEP))[..., : PATCH - KEEP]
    return jnp.concatenate([head_part, tail_part], axis=-1)


def patches(grid_values, row_blocks, col_blocks):
    across = window_last(grid_values, col_blocks)
    turned = jnp.moveaxis(across, -3, -1)
    stacked = window_last(turned, row_blocks)
    return jnp.moveaxis(stacked, (-4, -3), (-2, -1))


def box_mean(padded, rows_out, cols_out):
    summed = jnp.zeros(padded.shape[:-2] + (rows_out, cols_out), padded.dtype)
    for row_step in (-1, 0, 1):
        for col_step in (-1, 0, 1):
            summed = (
                summed
                + padded[
                    ...,
                    MARGIN + row_step : MARGIN + row_step + rows_out,
                    MARGIN + col_step : MARGIN + col_step + cols_out,
                ]
            )
    return summed / 9.0


def coherence_from(real_pad, imag_pad, first_pad, second_pad, rows_out, cols_out):
    cross_real = box_mean(real_pad, rows_out, cols_out)
    cross_imag = box_mean(imag_pad, rows_out, cols_out)
    energy = box_mean(first_pad, rows_out, cols_out) * box_mean(second_pad, rows_out, cols_out)
    factor = lax.rsqrt(energy + 1e-06)
    return jnp.stack([cross_real * factor, cross_imag * factor], axis=-3)


def weights_of(power):
    smooth = jnp.zeros_like(power)
    for row_step in (-1, 0, 1):
        for col_step in (-1, 0, 1):
            smooth = smooth + jnp.roll(power, (row_step, col_step), axis=(-3, -1))
    smooth = smooth / 9.0
    level = jnp.mean(power, axis=(-3, -1), keepdims=True)
    weight = (smooth + level + 1e-06) ** 0.25
    return weight / jnp.mean(weight, axis=(-3, -1), keepdims=True)


def centre(values, row_blocks, col_blocks):
    kept = values[..., MARGIN : MARGIN + KEEP, :, MARGIN : MARGIN + KEEP]
    return kept.reshape(kept.shape[:-4] + (row_blocks * KEEP, col_blocks * KEEP))


def spectral(real_part, imag_part, sign):
    ticks = jnp.arange(PATCH, dtype=jnp.int32)
    angle = (ticks[:, None] * ticks[None, :] % PATCH).astype(jnp.float32) * (2.0 * math.pi / PATCH)
    cosine = jnp.cos(angle)
    sine = sign * jnp.sin(angle)
    highest = lax.Precision.HIGHEST

    def along_rows(table, values):
        return jnp.einsum("uy,...ybx->...ubx", table, values, precision=highest)

    def along_cols(table, values):
        return jnp.einsum("vx,...ybx->...ybv", table, values, precision=highest)

    middle_real = along_rows(cosine, real_part) - along_rows(sine, imag_part)
    middle_imag = along_rows(cosine, imag_part) + along_rows(sine, real_part)
    final_real = along_cols(cosine, middle_real) - along_cols(sine, middle_imag)
    final_imag = along_cols(cosine, middle_imag) + along_cols(sine, middle_real)
    return (final_real, final_imag)


def goldstein(real_pad, imag_pad, row_blocks, col_blocks):
    real_part = patches(real_pad, row_blocks, col_blocks)
    imag_part = patches(imag_pad, row_blocks, col_blocks)
    spec_real, spec_imag = spectral(real_part, imag_part, -1.0)
    weight = weights_of(spec_real * spec_real + spec_imag * spec_imag)
    back_real, back_imag = spectral(spec_real * weight, spec_imag * weight, 1.0)
    scale = 1.0 / (PATCH * PATCH)
    return jnp.stack(
        [
            centre(back_real * scale, row_blocks, col_blocks),
            centre(back_imag * scale, row_blocks, col_blocks),
        ],
        axis=-3,
    )


def body(images, secondaries):
    per_device = images.shape[0]
    links = secondaries.shape[1]
    tile_rows = images.shape[2]
    tile_cols = images.shape[3]
    look_rows = tile_rows // LOOK_R
    look_cols = tile_cols // LOOK_C
    first_date = lax.axis_index("date") * per_device
    total_dates = per_device * lax.axis_size("date")
    slots = (secondaries - first_date) % total_dates
    own_date = images[:, None]
    following = shifted(images, "date", -1)
    beyond = shifted(following, "date", -1)
    window = jnp.concatenate([images, following, beyond], axis=0)
    partners = jnp.take(window, slots.reshape(-1), axis=0).reshape(
        (per_device, links) + images.shape[1:]
    )
    pair_real = multilook(
        own_date[:, :, 0] * partners[:, :, 0] + own_date[:, :, 1] * partners[:, :, 1]
    )
    pair_imag = multilook(
        own_date[:, :, 1] * partners[:, :, 0] - own_date[:, :, 0] * partners[:, :, 1]
    )
    powers = multilook(window[:, 0] * window[:, 0] + window[:, 1] * window[:, 1])
    first_power = jnp.broadcast_to(
        powers[:per_device, None], (per_device, links, look_rows, look_cols)
    )
    second_power = jnp.take(powers, slots.reshape(-1), axis=0).reshape(
        per_device, links, look_rows, look_cols
    )
    planes = jnp.stack([pair_real, pair_imag, first_power, second_power], axis=2)
    padded = with_halo(planes, (("row", 3), ("col", 4)), MARGIN)
    real_pad = padded[:, :, 0]
    imag_pad = padded[:, :, 1]
    first_pad = padded[:, :, 2]
    second_pad = padded[:, :, 3]
    coherent = coherence_from(real_pad, imag_pad, first_pad, second_pad, look_rows, look_cols)
    filtered = goldstein(real_pad, imag_pad, look_rows // KEEP, look_cols // KEEP)
    return (filtered, coherent)


def solution(mesh):
    in_specs = (P("date", None, "row", "col"), P("date", None))
    out_specs = (P("date", None, None, "row", "col"), P("date", None, None, "row", "col"))
    return jax.shard_map(body, mesh=mesh, in_specs=in_specs, out_specs=out_specs, check_vma=False)
```

profile of v0, /device:TPU:1, one launch (start us, length us, event | category | flops | bytes accessed | tf_op | source)
XLA Modules:
  0.0 143.1 jit_solution(3506358894038190235)
XLA Ops:
  0.6 14.6 %collective-permute-start = (f32[2,2,48,768]{3,2,1,0:T(8,128)}, f32[2,2,48,768]{3,2,1,0:T(8,128)S(1)}, u32[]{:S(2)}, u32[]{:S(2)}) collective-permute-start(f32[2,2,48,768]{3,2,1,0:T(8,128)} %param.2), channel_id=1, source_target_pairs={{0,496},{16,0},{32,16},{48,32},{64,48},{80,64},{96,80},{112,96},{1... | collective-permute-start | bytes 1769480 | tf_op jit(solution)/shard_map/ppermute | solution.py:18
  16.0 1.1 fusion.184
  17.1 4.0 %mul.270 = f32[2,24,2,96,8]{4,3,2,1,0:T(8,128)} reshape(f32[2,1,1,48,768]{4,3,2,0,1:T(8,128)S(1)} %get-tuple-element.17) | data formatting | bytes 589824 | tf_op jit(solution)/shard_map/mul | solution.py:151
  21.1 4.0 %mul.266 = f32[2,24,2,96,8]{4,3,2,1,0:T(8,128)} reshape(f32[2,1,1,48,768]{4,3,2,0,1:T(8,128)S(1)} %get-tuple-element.16) | data formatting | bytes 589824 | tf_op jit(solution)/shard_map/mul | solution.py:151
  25.1 2.4 %collective-permute-done = f32[2,2,48,768]{3,2,1,0:T(8,128)S(1)} collective-permute-done((f32[2,2,48,768]{3,2,1,0:T(8,128)}, f32[2,2,48,768]{3,2,1,0:T(8,128)S(1)}, u32[]{:S(2)}, u32[]{:S(2)}) %collective-permute-start) | collective-permute-done | bytes 589856 | tf_op jit(solution)/shard_map/ppermute | solution.py:18
  27.5 7.6 %collective-permute-start.1 = (f32[2,2,48,768]{3,2,1,0:T(8,128)S(1)}, f32[2,2,48,768]{3,2,1,0:T(8,128)S(1)}, u32[]{:S(2)}, u32[]{:S(2)}) collective-permute-start(f32[2,2,48,768]{3,2,1,0:T(8,128)S(1)} %collective-permute-done), channel_id=1, source_target_pairs={{0,496},{16,0},{32,16},{48,32},{64,48},{80,64},{96,80},{112,96},{1... | collective-permute-start | bytes 1769480 | tf_op jit(solution)/shard_map/ppermute | solution.py:18
  35.3 10.9 %collective-permute-done.1 = f32[2,2,48,768]{3,2,1,0:T(8,128)S(1)} collective-permute-done((f32[2,2,48,768]{3,2,1,0:T(8,128)S(1)}, f32[2,2,48,768]{3,2,1,0:T(8,128)S(1)}, u32[]{:S(2)}, u32[]{:S(2)}) %collective-permute-start.1) | collective-permute-done | bytes 589856 | tf_op jit(solution)/shard_map/ppermute | solution.py:18
  46.3 9.5 %add.276 = f32[6,24,2,96,8]{4,3,2,1,0:T(8,128)} reshape(f32[6,1,48,768]{3,2,1,0:T(8,128)S(1)} %fusion.8) | data formatting | bytes 1769472 | tf_op jit(solution)/shard_map/add | solution.py:156
  55.9 7.5 %reduce_sum.47 = f32[6,24,96]{2,1,0:T(8,128)S(1)} reduce(f32[6,24,2,96,8]{4,3,2,1,0:T(8,128)} %add.276, f32[]{:T(128)} %constant.89.clone.1), dimensions={2,4}, to_apply=%region_2.3 | reduce | flops 207360 | bytes 940036 | tf_op jit(solution)/shard_map/reduce_sum | solution.py:39
  64.0 1.2 gather_fusion.1
  65.9 1.6 %broadcast_select_fusion = f32[2,3,1,24,96]{4,3,1,0,2:T(8,128)} fusion(f32[2,3,1,24,96]{4,3,1,0,2:T(8,128)} %bitcast.216, pred[2,3]{1,0:T(4,128)(4,1)S(1)} %get-tuple-element.12), kind=kLoop, calls=%fused_computation.139 | loop fusion | flops 13824 | bytes 110598 | tf_op jit(solution)/shard_map/jit(_take)/select_n | solution.py:160
  67.8 9.5 %squeeze.13 = f32[2,3,24,2,96,8]{5,4,3,2,1,0:T(8,128)} reshape(f32[2,3,1,48,768]{4,3,1,0,2:T(8,128)S(1)} %get-tuple-element.15) | data formatting | bytes 1769472 | tf_op jit(solution)/shard_map/squeeze | solution.py:151
  77.4 9.4 %squeeze.12 = f32[2,3,24,2,96,8]{5,4,3,2,1,0:T(8,128)} reshape(f32[2,3,1,48,768]{4,3,1,0,2:T(8,128)S(1)} %get-tuple-element.14) | data formatting | bytes 1769472 | tf_op jit(solution)/shard_map/squeeze | solution.py:151
  86.8 13.6 %add_reduce_fusion = (f32[2,3,24,96]{3,2,1,0:T(8,128)S(1)}, f32[2,3,24,96]{3,2,1,0:T(8,128)S(1)}) fusion(f32[2,3,24,2,96,8]{5,4,3,2,1,0:T(8,128)} %squeeze.13, f32[2,3,24,2,96,8]{5,4,3,2,1,0:T(8,128)} %squeeze.12, f32[2,24,2,96,8]{4,3,2,1,0:T(8,128)} %mul.270, f32[2,24,2,96,8]{4,3,2,1,0:T(8,128)} %mul.266), kind=kLoop, calls=%fused_computation.3 | loop fusion | flops 1741824 | bytes 2469888 | tf_op jit(solution)/shard_map/reduce_sum | solution.py:39
  100.5 4.4 %collective-permute-start.3 = (f32[2,3,4,4,96]{4,3,1,0,2:T(4,128)S(1)}, f32[2,3,4,4,96]{4,3,1,0,2:T(4,128)S(1)}, u32[]{:S(2)}, u32[]{:S(2)}) collective-permute-start(f32[2,3,4,4,96]{4,3,1,0,2:T(4,128)S(1)} %get-tuple-element.49), channel_id=1, source_target_pairs={{2,0},{4,2},{6,4},{8,6},{10,8},{12,10},{14,12},{3,1},{5,3},{7,5},{... | collective-permute-start | bytes 110600 | tf_op jit(solution)/shard_map/ppermute | solution.py:29
  104.9 3.0 %collective-permute-start.2 = (f32[2,3,4,4,96]{4,3,1,0,2:T(4,128)S(1)}, f32[2,3,4,4,96]{4,3,1,0,2:T(4,128)S(1)}, u32[]{:S(2)}, u32[]{:S(2)}) collective-permute-start(f32[2,3,4,4,96]{4,3,1,0,2:T(4,128)S(1)} %get-tuple-element.48), channel_id=1, source_target_pairs={{0,2},{2,4},{4,6},{6,8},{8,10},{10,12},{12,14},{1,3},{3,5},{5,7},{... | collective-permute-start | bytes 110600 | tf_op jit(solution)/shard_map/ppermute | solution.py:26
  107.9 1.1 collective-permute-done.2
  109.3 1.3 collective-permute-start.5
  110.6 4.2 %collective-permute-start.4 = (f32[2,3,4,32,4]{4,3,1,0,2:T(8,128)S(1)}, f32[2,3,4,32,4]{4,3,1,0,2:T(8,128)S(1)}, u32[]{:S(2)}, u32[]{:S(2)}) collective-permute-start(f32[2,3,4,32,4]{4,3,1,0,2:T(8,128)S(1)} %get-tuple-element.46), channel_id=1, source_target_pairs={{0,1},{2,3},{4,5},{6,7},{8,9},{10,11},{12,13},{14,15},{16,17},{18,... | collective-permute-start | bytes 36872 | tf_op jit(solution)/shard_map/ppermute | solution.py:26
  114.8 6.8 %collective-permute-done.5 = f32[2,3,4,32,4]{4,3,1,0,2:T(8,128)S(1)} collective-permute-done((f32[2,3,4,32,4]{4,3,1,0,2:T(8,128)S(1)}, f32[2,3,4,32,4]{4,3,1,0,2:T(8,128)S(1)}, u32[]{:S(2)}, u32[]{:S(2)}) %collective-permute-start.5) | collective-permute-done | bytes 12320 | tf_op jit(solution)/shard_map/ppermute | solution.py:29
  121.6 1.8 %collective-permute-done.4 = f32[2,3,4,32,4]{4,3,1,0,2:T(8,128)S(1)} collective-permute-done((f32[2,3,4,32,4]{4,3,1,0,2:T(8,128)S(1)}, f32[2,3,4,32,4]{4,3,1,0,2:T(8,128)S(1)}, u32[]{:S(2)}, u32[]{:S(2)}) %collective-permute-start.4) | collective-permute-done | bytes 12320 | tf_op jit(solution)/shard_map/ppermute | solution.py:26
  126.8 0.8 fusion.73
  128.2 0.8 fusion.70
  129.8 0.9 fusion.182
  132.1 1.1 fusion.180
  133.2 0.9 fusion.38
  134.0 0.9 fusion.34
  134.9 0.9 fusion
  135.8 1.0 fusion.64
  136.8 0.9 fusion.1
  138.5 0.8 fusion.7
  139.7 0.8 fusion.5
  (66 shorter events, 12.6 us)
Async XLA Ops:
  0.6 26.9 %collective-permute-start = (f32[2,2,48,768]{3,2,1,0:T(8,128)}, f32[2,2,48,768]{3,2,1,0:T(8,128)S(1)}, u32[]{:S(2)}, u32[]{:S(2)}) collective-permute-start(f32[2,2,48,768]{3,2,1,0:T(8,128)} %param.2), channel_id=1, source_target_pairs={{0,496},{16,0},{32,16},{48,32},{64,48},{80,64},{96,80},{112,96},{1... | collective-permute-start | bytes 1769480 | tf_op jit(solution)/shard_map/ppermute | solution.py:18
  21.1 14.1 %copy-start = (f32[2,2,48,768]{3,2,1,0:T(8,128)S(1)}, f32[2,2,48,768]{3,2,1,0:T(8,128)}, u32[]{:S(2)}) copy-start(f32[2,2,48,768]{3,2,1,0:T(8,128)} %param.2) | copy-start | bytes 1769476
  27.5 18.7 %collective-permute-start.1 = (f32[2,2,48,768]{3,2,1,0:T(8,128)S(1)}, f32[2,2,48,768]{3,2,1,0:T(8,128)S(1)}, u32[]{:S(2)}, u32[]{:S(2)}) collective-permute-start(f32[2,2,48,768]{3,2,1,0:T(8,128)S(1)} %collective-permute-done), channel_id=1, source_target_pairs={{0,496},{16,0},{32,16},{48,32},{64,48},{80,64},{96,80},{112,96},{1... | collective-permute-start | bytes 1769480 | tf_op jit(solution)/shard_map/ppermute | solution.py:18
  86.8 13.7 %copy-start.2 = (f32[2,24,96]{2,1,0:T(8,128)S(1)}, f32[2,24,96]{2,1,0:T(8,128)}, u32[]{:S(2)}) copy-start(f32[2,24,96]{2,1,0:T(8,128)} %slice.372) | copy-start | bytes 55300
  86.8 13.7 %copy-start.1 = (f32[2,3,1,24,96]{4,3,1,0,2:T(8,128)S(1)}, f32[2,3,1,24,96]{4,3,1,0,2:T(8,128)}, u32[]{:S(2)}) copy-start(f32[2,3,1,24,96]{4,3,1,0,2:T(8,128)} %broadcast_select_fusion) | copy-start | bytes 165892
  100.5 7.4 %collective-permute-start.3 = (f32[2,3,4,4,96]{4,3,1,0,2:T(4,128)S(1)}, f32[2,3,4,4,96]{4,3,1,0,2:T(4,128)S(1)}, u32[]{:S(2)}, u32[]{:S(2)}) collective-permute-start(f32[2,3,4,4,96]{4,3,1,0,2:T(4,128)S(1)} %get-tuple-element.49), channel_id=1, source_target_pairs={{2,0},{4,2},{6,4},{8,6},{10,8},{12,10},{14,12},{3,1},{5,3},{7,5},{... | collective-permute-start | bytes 110600 | tf_op jit(solution)/shard_map/ppermute | solution.py:29
  104.9 4.2 %collective-permute-start.2 = (f32[2,3,4,4,96]{4,3,1,0,2:T(4,128)S(1)}, f32[2,3,4,4,96]{4,3,1,0,2:T(4,128)S(1)}, u32[]{:S(2)}, u32[]{:S(2)}) collective-permute-start(f32[2,3,4,4,96]{4,3,1,0,2:T(4,128)S(1)} %get-tuple-element.48), channel_id=1, source_target_pairs={{0,2},{2,4},{4,6},{6,8},{8,10},{10,12},{12,14},{1,3},{3,5},{5,7},{... | collective-permute-start | bytes 110600 | tf_op jit(solution)/shard_map/ppermute | solution.py:26
  109.3 12.3 %collective-permute-start.5 = (f32[2,3,4,32,4]{4,3,1,0,2:T(8,128)S(1)}, f32[2,3,4,32,4]{4,3,1,0,2:T(8,128)S(1)}, u32[]{:S(2)}, u32[]{:S(2)}) collective-permute-start(f32[2,3,4,32,4]{4,3,1,0,2:T(8,128)S(1)} %get-tuple-element.47), channel_id=1, source_target_pairs={{1,0},{3,2},{5,4},{7,6},{9,8},{11,10},{13,12},{15,14},{17,16},{19,... | collective-permute-start | bytes 36872 | tf_op jit(solution)/shard_map/ppermute | solution.py:29
  110.6 12.8 %collective-permute-start.4 = (f32[2,3,4,32,4]{4,3,1,0,2:T(8,128)S(1)}, f32[2,3,4,32,4]{4,3,1,0,2:T(8,128)S(1)}, u32[]{:S(2)}, u32[]{:S(2)}) collective-permute-start(f32[2,3,4,32,4]{4,3,1,0,2:T(8,128)S(1)} %get-tuple-element.46), channel_id=1, source_target_pairs={{0,1},{2,3},{4,5},{6,7},{8,9},{10,11},{12,13},{14,15},{16,17},{18,... | collective-permute-start | bytes 36872 | tf_op jit(solution)/shard_map/ppermute | solution.py:26
where the time goes:
time: 143 us
  local copies, waits for them, and re-layouts  43.7 us (31%)
  starting transfers between devices  35.1 us (25%)
  other arithmetic  27.8 us (19%)
  waiting for transfers between devices  23.1 us (16%)
  matrix products  12.4 us (9%)
    ppermute x2, starting transfers between devices, shifted(): return lax.ppermute(value, axis, pairs)  22.2 us
    reduce_sum x2, other arithmetic, multilook(): return blocks.mean(axis=(-3, -1))  21.1 us
    ppermute x2, waiting for transfers between devices, shifted(): return lax.ppermute(value, axis, pairs)  13.3 us
    squeeze x1, local copies, waits for them, and re-layouts, body(): partners[:, :, 1]  9.54 us
    add x1, local copies, waits for them, and re-layouts, body(): window[:, 0] * window[:, 0] + window[:, 1] * window[:, 1]  9.54 us
    squeeze x1, local copies, waits for them, and re-layouts, body(): partners[:, :, 0]  9.4 us
    ppermute x2, starting transfers between devices, with_halo(): lax.ppermute(lax.slice_in_dim(block, block.shape[dim] - width, None, axis...  7.23 us
    ppermute x2, waiting for transfers between devices, with_halo(): lax.ppermute(lax.slice_in_dim(block, 0, width, axis=dim), axis, backward)  6.78 us
  transfers between devices with their start and end apart: 6, of which 5 were waited for; matrix products, arithmetic and copies ran while one was open for 7% of the time, Pallas kernels for 0%

commit v1 on v0

v1 whole, which is shorter than its diff:
```python
import functools
import math

import jax
import jax.numpy as jnp
import numpy as np
from jax import lax
from jax.experimental import pallas as pl
from jax.experimental.pallas import tpu as pltpu
from jax.sharding import PartitionSpec as P

KEEP = 24
PATCH = 32
MARGIN = 4
LANES = 128
STRIP = 32
LINKS = 3
F32 = jnp.float32
BF16 = jnp.bfloat16

HELD = ((0, 1), (0, 2), (0, 3), (1, 2), (1, 3))
SENT = ((-2, 2), (-1, 2), (-1, 3))


def vmem():
    return pl.BlockSpec(memory_space=pltpu.VMEM)


def smem():
    return pl.BlockSpec(memory_space=pltpu.SMEM)


def call(kernel, outs, count, scratch=(), specs=None, flops=1e6, moved=1e6):
    return pl.pallas_call(
        kernel,
        out_shape=outs,
        in_specs=specs or [vmem()] * count,
        out_specs=jax.tree.map(lambda _: vmem(), outs),
        scratch_shapes=list(scratch),
        compiler_params=pltpu.CompilerParams(vmem_limit_bytes=32 * 1024 * 1024),
        cost_estimate=pl.CostEstimate(flops=int(flops), bytes_accessed=int(moved), transcendentals=0),
    )


def lane_index(shape):
    return lax.broadcasted_iota(jnp.int32, shape, len(shape) - 1)


def edge_kernel(first_ref, last_ref, out_ref):
    at_left = lax.axis_index("col") == 0
    lanes = lane_index(first_ref.shape[2:])
    for part in range(2):
        pieces = []
        for date in range(2):
            left = first_ref[date, part]
            right = pltpu.roll(last_ref[date, part], STRIP, 1)
            pieces.append(jnp.where(at_left, right, left))
        zero, one = pieces
        value = jnp.where(lanes < STRIP, zero, pltpu.roll(one, STRIP, 1))
        value = jnp.where(lanes < 2 * STRIP, value, pltpu.roll(zero, 2 * STRIP, 1))
        value = jnp.where(lanes < 3 * STRIP, value, pltpu.roll(one, 3 * STRIP, 1))
        out_ref[part] = value


def edge_of(images):
    rows, cols = images.shape[2:]
    spec = lambda index: pl.BlockSpec((2, 2, rows, LANES), lambda i: (0, 0, 0, index))
    return pl.pallas_call(
        edge_kernel,
        grid=(1,),
        out_shape=jax.ShapeDtypeStruct((2, rows, LANES), F32),
        in_specs=[spec(0), spec(cols // LANES - 1)],
        out_specs=pl.BlockSpec((2, rows, LANES), lambda i: (0, 0, 0)),
    )(images, images)


def looks_table(cols, at_left):
    shape = (cols, LANES)
    source = lax.broadcasted_iota(jnp.int32, shape, 0)
    target = lax.broadcasted_iota(jnp.int32, shape, 1)
    main = jnp.where((source >> 3) + MARGIN == target, 1.0 / 16.0, 0.0)
    shape = (LANES, LANES)
    source = lax.broadcasted_iota(jnp.int32, shape, 0)
    target = lax.broadcasted_iota(jnp.int32, shape, 1)
    place = jnp.where(at_left, MARGIN + cols // 8, 0)
    edge = jnp.where(((source & (STRIP - 1)) >> 3) + place == target, 1.0 / 16.0, 0.0)
    return jnp.concatenate([main, edge], axis=0).astype(BF16)


def split_dot(values, table):
    high = values.astype(BF16)
    rest = values - high.astype(F32)
    middle = rest.astype(BF16)
    low = (rest - middle.astype(F32)).astype(BF16)
    dot = lambda v: jnp.dot(v, table, preferred_element_type=F32)
    return dot(high) + (dot(middle) + dot(low))


def pairs_kernel(*refs):
    own_edge, after_edge, before_edge, held, sent, stage = refs[-6:]
    tiles = (len(refs) - 6) // 3
    own, after, before = refs[:tiles], refs[tiles : 2 * tiles], refs[2 * tiles : 3 * tiles]
    cols = tiles * LANES
    half = own_edge.shape[1] // 2
    at_left = lax.axis_index("col") == 0
    holders = {-2: (before, 0), -1: (before, 1), 0: (own, 0), 1: (own, 1), 2: (after, 0), 3: (after, 1)}

    def image(slot, tile):
        refs, date = holders[slot]
        return [
            [refs[tile][date, part, pl.ds(parity, half, stride=2), :] for parity in range(2)]
            for part in range(2)
        ]

    def edge(ref):
        return [[ref[part, pl.ds(parity, half, stride=2), :] for parity in range(2)] for part in range(2)]

    def product(a, b):
        (ar, ai), (br, bi) = a, b
        real = (ar[0] * br[0] + ai[0] * bi[0]) + (ar[1] * br[1] + ai[1] * bi[1])
        imag = (ai[0] * br[0] - ar[0] * bi[0]) + (ai[1] * br[1] - ar[1] * bi[1])
        return real, imag

    def power(a):
        ar, ai = a
        return (ar[0] * ar[0] + ai[0] * ai[0]) + (ar[1] * ar[1] + ai[1] * ai[1])

    pairs = HELD + SENT
    planes = 2 * len(pairs)
    for tile in range(tiles):
        lanes = pl.ds(tile * LANES, LANES)
        loaded = {slot: image(slot, tile) for slot in holders}
        for n, (a, b) in enumerate(pairs):
            real, imag = product(loaded[a], loaded[b])
            stage[pl.ds(2 * n * half, half), lanes] = real
            stage[pl.ds((2 * n + 1) * half, half), lanes] = imag
        for slot in range(4):
            stage[pl.ds((planes + slot) * half, half), lanes] = power(loaded[slot])

    lanes = pl.ds(cols, LANES)
    block = lane_index((half, LANES)) >> 5

    def only(value, wanted):
        return jnp.where(block == wanted, value, 0.0)

    turned = lambda a: [[pltpu.roll(v, STRIP, 1) for v in part] for part in a]
    mine, theirs, earlier = edge(own_edge), edge(after_edge), edge(before_edge)
    crossed = [
        [jnp.where(block < 2, v, w) for v, w in zip(p, q)] for p, q in zip(theirs, turned(theirs))
    ]
    local = product(mine, turned(mine))
    ahead = product(mine, crossed)
    met = product(earlier, crossed)
    where = {
        (0, 1): (local, 0),
        (0, 2): (ahead, 0),
        (1, 3): (ahead, 1),
        (0, 3): (ahead, 2),
        (1, 2): (ahead, 3),
        (-2, 2): (met, 0),
        (-1, 3): (met, 1),
        (-1, 2): (met, 3),
    }
    for n, pair in enumerate(pairs):
        (real, imag), wanted = where[pair]
        stage[pl.ds(2 * n * half, half), lanes] = only(real, wanted)
        stage[pl.ds((2 * n + 1) * half, half), lanes] = only(imag, wanted)
    own_power, after_power = power(mine), power(theirs)
    for slot in range(4):
        value = own_power if slot < 2 else after_power
        stage[pl.ds((planes + slot) * half, half), lanes] = only(value, slot % 2)

    means = split_dot(stage[...], looks_table(cols, at_left))
    split = 2 * len(HELD) * half
    end = planes * half
    held[pl.ds(0, split), :] = means[:split]
    held[pl.ds(split, 4 * half), :] = means[end:]
    sent[pl.ds(0, end - split), :] = means[split:end]
    sent[pl.ds(end - split, 2 * half), :] = means[end + 2 * half :]


def pairs_of(own, after, before, own_edge, after_edge, before_edge):
    rows, cols = own.shape[2:]
    half, tiles = rows // 2, cols // LANES
    tile = lambda index: pl.BlockSpec((2, 2, rows, LANES), lambda i: (0, 0, 0, index))
    edge = pl.BlockSpec((2, rows, LANES), lambda i: (0, 0, 0))
    plane = lambda count: jax.ShapeDtypeStruct((count * half, LANES), F32)
    whole = lambda out: pl.BlockSpec(out.shape, lambda i: (0, 0))
    total = 2 * len(HELD + SENT) + 4
    outs = (plane(2 * len(HELD) + 4), plane(2 * len(SENT) + 2))
    return pl.pallas_call(
        pairs_kernel,
        grid=(1,),
        out_shape=outs,
        in_specs=[tile(index) for index in range(tiles)] * 3 + [edge] * 3,
        out_specs=tuple(whole(out) for out in outs),
        scratch_shapes=[pltpu.VMEM((total * half, cols + LANES), F32)],
        compiler_params=pltpu.CompilerParams(vmem_limit_bytes=32 * 1024 * 1024),
    )(*[own] * tiles, *[after] * tiles, *[before] * tiles, own_edge, after_edge, before_edge)


def chosen(secondaries, held, back, all_planes):
    size = KEEP
    order = [("h", 0), ("h", 1), ("h", 2), ("b", 0), ("h", 3), ("h", 4), ("b", 1), ("b", 2)]
    for n, (which, index) in enumerate(order):
        ref = held if which == "h" else back
        all_planes[pl.ds(2 * n * size, 2 * size), :] = ref[pl.ds(2 * index * size, 2 * size), :]
    base = 2 * len(order) * size
    all_planes[pl.ds(base, 4 * size), :] = held[pl.ds(2 * len(HELD) * size, 4 * size), :]
    all_planes[pl.ds(base + 4 * size, 2 * size), :] = back[pl.ds(2 * len(SENT) * size, 2 * size), :]
    first = 2 * lax.axis_index("date")
    dates = 2 * lax.axis_size("date")

    def planes(date, link):
        slot = (secondaries[date, link] - first + dates) % dates
        pair = 4 * date + slot - 1 - date
        starts = (2 * pair, 2 * pair + 1, 16 + date, 16 + slot)
        return [pl.multiple_of(s * size, 8) if not isinstance(s, int) else s * size for s in starts]

    return planes


def rims_kernel(secondaries, held, back, chip, across, all_planes):
    planes = chosen(secondaries, held, back, all_planes)
    even = lax.axis_index("row") % 2 == 0
    n = 0
    for date in range(2):
        for link in range(LINKS):
            for start in planes(date, link):
                top = all_planes[pl.ds(start, 8), :]
                bottom = pltpu.roll(all_planes[pl.ds(start + KEEP - 8, 8), :], 4, 0)
                chip[pl.ds(4 * n, 4), :] = jnp.where(even, bottom, top)[:4]
                across[pl.ds(4 * n, 4), :] = jnp.where(even, top, bottom)[:4]
                n += 1


@functools.lru_cache(None)
def tables():
    blocks = LANES // PATCH
    n = np.arange(PATCH)
    angle = 2.0 * np.pi * (np.outer(n, n) % PATCH) / PATCH
    cosine, sine = np.cos(angle), np.sin(angle)
    forward = np.zeros((LANES, 2 * LANES))
    spread = np.zeros((LANES, 2 * LANES))
    inverse = np.zeros((LANES, 2 * LANES))
    for b in range(blocks):
        f = slice(b * PATCH, (b + 1) * PATCH)
        x = slice(b * KEEP, b * KEEP + PATCH)
        o = slice(b * KEEP, (b + 1) * KEEP)
        kept = slice(MARGIN, MARGIN + KEEP)
        forward[x, f] = cosine
        forward[x, LANES + b * PATCH : LANES + (b + 1) * PATCH] = -sine
        inverse[f, o] = cosine[:, kept] / PATCH
        inverse[f, LANES + b * KEEP : LANES + (b + 1) * KEEP] = sine[:, kept] / PATCH
        near = (n[:, None] - n[None, :]) % PATCH
        spread[f, f] = (near == 0) | (near == 1) | (near == PATCH - 1)
        spread[f, LANES + b * PATCH : LANES + (b + 1) * PATCH] = 1.0
    down = np.block([[cosine, sine], [-sine, cosine]])
    kept = slice(MARGIN, MARGIN + KEEP)
    up = np.block([[cosine[kept], -sine[kept]], [sine[kept], cosine[kept]]]) / PATCH
    return [np.asarray(t, np.float32) for t in (forward, spread, inverse, down, up)]


def exact_dot(a, b):
    return jnp.dot(a, b, preferred_element_type=F32, precision=lax.Precision.HIGHEST)


def filter_kernel(
    secondaries, held, back, chip, across, forward, spread, inverse, down, up, filtered, coherent, all_planes, pad
):
    planes = chosen(secondaries, held, back, all_planes)
    even = lax.axis_index("row") % 2 == 0
    pairs = 2 * LINKS
    n = 0
    for date in range(2):
        for link in range(LINKS):
            for start in planes(date, link):
                near, far = chip[pl.ds(4 * n, 4), :], across[pl.ds(4 * n, 4), :]
                pad[n, pl.ds(0, 4), :] = jnp.where(even, far, near)
                pad[n, pl.ds(4, KEEP), :] = all_planes[pl.ds(start, KEEP), :]
                pad[n, pl.ds(4 + KEEP, 4), :] = jnp.where(even, near, far)
                n += 1

    def box(value):
        rows = value[3 : 3 + KEEP] + value[4 : 4 + KEEP] + value[5 : 5 + KEEP]
        total = pltpu.roll(rows, LANES - 3, 1) + pltpu.roll(rows, LANES - 4, 1) + pltpu.roll(rows, LANES - 5, 1)
        return total * (1.0 / 9.0)

    wide = coherent.shape[-1]
    for p in range(pairs):
        real, imag, first, second = [box(pad[4 * p + k]) for k in range(4)]
        factor = lax.rsqrt(first * second + 1e-06)
        coherent[p // LINKS, p % LINKS, 0] = (real * factor)[:, :wide]
        coherent[p // LINKS, p % LINKS, 1] = (imag * factor)[:, :wide]

    reals = jnp.concatenate([pad[4 * p] for p in range(pairs)], axis=0)
    imags = jnp.concatenate([pad[4 * p + 1] for p in range(pairs)], axis=0)
    size = pairs * PATCH
    across_cols = exact_dot(jnp.concatenate([reals, imags], axis=0), forward[...])
    col_real = across_cols[:size, :LANES] - across_cols[size:, LANES:]
    col_imag = across_cols[size:, :LANES] + across_cols[:size, LANES:]
    rows_of = lambda v, p, count: v[p * count : (p + 1) * count]
    stacked = jnp.concatenate(
        [
            jnp.concatenate([rows_of(col_real, p, PATCH), rows_of(col_imag, p, PATCH)], axis=0)
            for p in range(pairs)
        ],
        axis=1,
    )
    spectrum = exact_dot(down[...], stacked)
    real, imag = spectrum[:PATCH], spectrum[PATCH:]
    power = real * real + imag * imag
    lanes_of = lambda v, p: v[:, p * LANES : (p + 1) * LANES]
    tall = lambda v: jnp.concatenate([lanes_of(v, p) for p in range(pairs)], axis=0)
    sums = exact_dot(tall(power), spread[...])
    weights = []
    for p in range(pairs):
        near = rows_of(sums, p, PATCH)[:, :LANES]
        level = jnp.sum(rows_of(sums, p, PATCH)[:, LANES:], axis=0, keepdims=True) * (1.0 / (PATCH * PATCH))
        smooth = (near + pltpu.roll(near, 1, 0) + pltpu.roll(near, PATCH - 1, 0)) * (1.0 / 9.0)
        weights.append(jnp.sqrt(jnp.sqrt(smooth + level + 1e-06)))
    totals = exact_dot(jnp.concatenate(weights, axis=0), spread[:, LANES:])
    scaled = []
    for p in range(pairs):
        total = jnp.sum(rows_of(totals, p, PATCH), axis=0, keepdims=True)
        scaled.append(weights[p] * ((PATCH * PATCH) / total))
    weight = jnp.concatenate(scaled, axis=1)
    lifted = exact_dot(up[...], jnp.concatenate([real * weight, imag * weight], axis=0))
    low, high = lifted[:KEEP], lifted[KEEP:]
    size = pairs * KEEP
    result = exact_dot(jnp.concatenate([tall(low), tall(high)], axis=0), inverse[...])
    out_real = result[:size, :LANES] - result[size:, LANES:]
    out_imag = result[size:, :LANES] + result[:size, LANES:]
    for p in range(pairs):
        filtered[p // LINKS, p % LINKS, 0] = rows_of(out_real, p, KEEP)[:, :wide]
        filtered[p // LINKS, p % LINKS, 1] = rows_of(out_imag, p, KEEP)[:, :wide]


def shifted(value, axis, steps):
    count = lax.axis_size(axis)
    pairs = [(source, (source + steps) % count) for source in range(count)]
    return lax.ppermute(value, axis, pairs)


def body(images, secondaries):
    rows, cols = images.shape[2:]
    cells_down, cells_along = rows // 2, cols // 8
    rim = jax.ShapeDtypeStruct((2 * LINKS * 4 * MARGIN, LANES), F32)
    count = lax.axis_size("row")
    inside = [(i, i ^ 1) for i in range(count)]
    outside = [(i, ((i + 1) ^ 1) - 1) for i in range(1, count - 1)]

    after = shifted(images, "date", -1)
    before = shifted(images, "date", 1)
    edge = lax.ppermute(edge_of(images), "col", [(0, 1), (1, 0)])
    after_edge = shifted(edge, "date", -1)
    before_edge = shifted(edge, "date", 1)

    held, sent = pairs_of(images, after, before, edge, after_edge, before_edge)
    back = shifted(sent, "date", -1)

    every = pltpu.VMEM((22 * cells_down, LANES), F32)
    chip, across = call(rims_kernel, (rim, rim), 3, [every], [smem(), vmem(), vmem()])(secondaries, held, back)
    chip = lax.ppermute(chip, "row", inside)
    across = lax.ppermute(across, "row", outside)
    out = jax.ShapeDtypeStruct((2, LINKS, 2, cells_down, cells_along), F32)
    return call(
        filter_kernel,
        (out, out),
        10,
        [every, pltpu.VMEM((8 * LINKS, PATCH, LANES), F32)],
        [smem()] + [vmem()] * 9,
    )(secondaries, held, back, chip, across, *tables())


def solution(mesh):
    in_specs = (P("date", None, "row", "col"), P("date", None))
    out_specs = (P("date", None, None, "row", "col"), P("date", None, None, "row", "col"))
    return jax.shard_map(body, mesh=mesh, in_specs=in_specs, out_specs=out_specs, check_vma=False)
```

time: 143 us -> 66.2 us (0.46)
  local copies, waits for them, and re-layouts: 43.7 us -> 0.04 us
  other arithmetic: 27.8 us -> 0 us
  matrix products: 12.4 us -> 0 us
  waiting for transfers between devices: 23.1 us -> 12.6 us
  starting transfers between devices: 35.1 us -> 45.1 us
  Pallas kernels: 0 us -> 7.43 us
    reduce_sum x3 -> x0, other arithmetic: 22.2 us -> none  [the longest x2 21.1 us: multilook(): return blocks.mean(axis=(-3, -1))]
    squeeze x3 -> x0, local copies, waits for them, and re-layouts: 19 us -> none  [the longest x1 9.54 us: body(): partners[:, :, 1]]
    ppermute x2 -> x5, starting transfers between devices: 22.2 us -> 35.3 us  [shifted(): return lax.ppermute(value, axis, pairs)]
    dot_general x16 -> x0, matrix products: 12.4 us -> none  [the longest x8 6.68 us: along_cols(): return jnp.einsum('vx,...ybx->...ybv', table, values, precision=highest)]
    ppermute x2 -> x5, waiting for transfers between devices: 13.3 us -> 2.77 us  [shifted(): return lax.ppermute(value, axis, pairs)]
    add x1 -> x0, local copies, waits for them, and re-layouts: 9.54 us -> none  [body(): window[:, 0] * window[:, 0] + window[:, 1] * window[:, 1]]
    mul x2 -> x0, local copies, waits for them, and re-layouts: 8.03 us -> none  [the longest x1 4.04 us: body(): own_date[:, :, 0] * partners[:, :, 0]]
    pallas_call x0 -> x4, Pallas kernels: none -> 7.43 us  [the longest x1 3.79 us: body(): call(filter_kernel, (out, out), 10, [every, pltpu.VMEM((8 * LINKS, PATCH,...]
  transfers between devices with their start and end apart: 6 -> 8, of which waited for: 5 -> 4; matrix products, arithmetic and copies ran while one was open for 7% -> 0% of each run, Pallas kernels for 0% -> 3%
where the time goes in v1:
time: 66.2 us; the launch traced here: 65.9 us
  starting transfers between devices  45.1 us (68%)
  waiting for transfers between devices  12.6 us (19%)
  Pallas kernels  7.43 us (11%)
  between operations  0.79 us (1%)
    ppermute x5, starting transfers between devices, shifted(): return lax.ppermute(value, axis, pairs)  35.3 us
    ppermute x1, waiting for transfers between devices, body(): edge = lax.ppermute(edge_of(images), 'col', [(0, 1), (1, 0)])  7.45 us
    ppermute x1, starting transfers between devices, body(): chip = lax.ppermute(chip, 'row', inside)  4.4 us
    pallas_call x1, Pallas kernels, body(): call(filter_kernel, (out, out), 10, [every, pltpu.VMEM((8 * LINKS, PATCH,...  3.79 us
    ppermute x1, starting transfers between devices, body(): across = lax.ppermute(across, 'row', outside)  3.02 us
    ppermute x5, waiting for transfers between devices, shifted(): return lax.ppermute(value, axis, pairs)  2.77 us
    ppermute x1, waiting for transfers between devices, body(): across = lax.ppermute(across, 'row', outside)  2.37 us
    ppermute x1, starting transfers between devices, body(): edge = lax.ppermute(edge_of(images), 'col', [(0, 1), (1, 0)])  2.29 us
  transfers between devices with their start and end apart: 8, of which 4 were waited for; matrix products, arithmetic and copies ran while one was open for 0% of the time, Pallas kernels for 3%

profile of v1, /device:TPU:1, one launch (start us, length us, event | category | flops | bytes accessed | tf_op | source)
XLA Modules:
  0.0 65.9 jit_solution(2256240540607960419)
XLA Ops:
  0.6 0.0 copy-start
  0.6 4.5 %collective-permute-start.1 = (f32[2,2,48,768]{3,2,1,0:T(8,128)}, f32[2,2,48,768]{3,2,1,0:T(8,128)S(1)}, u32[]{:S(2)}, u32[]{:S(2)}) collective-permute-start(f32[2,2,48,768]{3,2,1,0:T(8,128)} %refs_5_.1), channel_id=1, source_target_pairs={{0,16},{16,32},{32,48},{48,64},{64,80},{80,96},{96,112},{112,128},... | collective-permute-start | bytes 1769480 | tf_op jit(solution)/shard_map/ppermute | solution.py:342
  5.2 12.1 %collective-permute-start = (f32[2,2,48,768]{3,2,1,0:T(8,128)}, f32[2,2,48,768]{3,2,1,0:T(8,128)S(1)}, u32[]{:S(2)}, u32[]{:S(2)}) collective-permute-start(f32[2,2,48,768]{3,2,1,0:T(8,128)} %refs_5_.1), channel_id=1, source_target_pairs={{0,496},{16,0},{32,16},{48,32},{64,48},{80,64},{96,80},{112,96},{1... | collective-permute-start | bytes 1769480 | tf_op jit(solution)/shard_map/ppermute | solution.py:342
  17.3 1.7 %shard_map.86 = f32[2,48,128]{2,1,0:T(8,128)} custom-call(f32[2,2,48,768]{3,2,1,0:T(8,128)} %refs_5_.1, f32[2,2,48,768]{3,2,1,0:T(8,128)} %refs_5_.1), custom_call_target="tpu_custom_call" | custom-call | tf_op jit(solution)/shard_map/pallas_call | solution.py:68
  19.0 2.3 %collective-permute-start.2 = (f32[2,48,128]{2,1,0:T(8,128)}, f32[2,48,128]{2,1,0:T(8,128)S(1)}, u32[]{:S(2)}, u32[]{:S(2)}) collective-permute-start(f32[2,48,128]{2,1,0:T(8,128)} %shard_map.86), channel_id=1, source_target_pairs={{0,1},{1,0},{2,3},{3,2},{4,5},{5,4},{6,7},{7,6},{8,9},{9,8},{10,11... | collective-permute-start | bytes 147464 | tf_op jit(solution)/shard_map/ppermute | solution.py:355
  21.3 7.5 %collective-permute-done.2.refs_18_ = f32[2,48,128]{2,1,0:T(8,128)S(1)} collective-permute-done((f32[2,48,128]{2,1,0:T(8,128)}, f32[2,48,128]{2,1,0:T(8,128)S(1)}, u32[]{:S(2)}, u32[]{:S(2)}) %collective-permute-start.2) | collective-permute-done | bytes 49184 | tf_op jit(solution)/shard_map/ppermute | solution.py:355
  28.8 1.9 %collective-permute-start.4 = (f32[2,48,128]{2,1,0:T(8,128)S(1)}, f32[2,48,128]{2,1,0:T(8,128)S(1)}, u32[]{:S(2)}, u32[]{:S(2)}) collective-permute-start(f32[2,48,128]{2,1,0:T(8,128)S(1)} %collective-permute-done.2.refs_18_), channel_id=1, source_target_pairs={{0,16},{16,32},{32,48},{48,64},{64,80},{80,96},{96,112},{112,128},... | collective-permute-start | bytes 147464 | tf_op jit(solution)/shard_map/ppermute | solution.py:342
  30.7 9.5 %collective-permute-start.3 = (f32[2,48,128]{2,1,0:T(8,128)S(1)}, f32[2,48,128]{2,1,0:T(8,128)S(1)}, u32[]{:S(2)}, u32[]{:S(2)}) collective-permute-start(f32[2,48,128]{2,1,0:T(8,128)S(1)} %collective-permute-done.2.refs_18_), channel_id=1, source_target_pairs={{0,496},{16,0},{32,16},{48,32},{64,48},{80,64},{96,80},{112,96},{1... | collective-permute-start | bytes 147464 | tf_op jit(solution)/shard_map/ppermute | solution.py:342
  40.2 0.0 collective-permute-done.4.refs_20_
  40.2 1.1 %collective-permute-done.3.refs_19_ = f32[2,48,128]{2,1,0:T(8,128)S(1)} collective-permute-done((f32[2,48,128]{2,1,0:T(8,128)S(1)}, f32[2,48,128]{2,1,0:T(8,128)S(1)}, u32[]{:S(2)}, u32[]{:S(2)}) %collective-permute-start.3) | collective-permute-done | bytes 49184 | tf_op jit(solution)/shard_map/ppermute | solution.py:342
  41.4 0.0 collective-permute-done.1.refs_12_.refs_13_.refs_14_.refs_15_.refs_16_.refs_17_
  41.4 0.0 collective-permute-done.refs_6_.refs_7_.refs_8_.refs_9_.refs_10_.refs_11_
  41.4 0.0 copy-done
  41.4 0.0 copy-start.3
  41.4 0.0 copy-start.4
  41.4 0.0 copy-start.5
  41.4 1.3 %shard_map.87 = (f32[336,128]{1,0:T(8,128)S(1)}, f32[192,128]{1,0:T(8,128)S(1)}) custom-call(f32[2,2,48,768]{3,2,1,0:T(8,128)S(1)} %copy-done, f32[2,2,48,768]{3,2,1,0:T(8,128)S(1)} %copy-done, f32[2,2,48,768]{3,2,1,0:T(8,128)S(1)} %copy-done, f32[2,2,48,768]{3,2,1,0:T(8,128)S(1)} %copy-done, f32[2,2,48,768]{3,2,1,0:T(8,128)S(1)} %copy-done, ...), custom_call_target="tpu_custom_call" | custom-call | tf_op jit(solution)/shard_map/pallas_call | solution.py:191
  42.7 0.0 copy-start.6
  42.7 7.3 %collective-permute-start.5 = (f32[192,128]{1,0:T(8,128)S(1)}, f32[192,128]{1,0:T(8,128)S(1)}, u32[]{:S(2)}, u32[]{:S(2)}) collective-permute-start(f32[192,128]{1,0:T(8,128)S(1)} %get-tuple-element.7), channel_id=1, source_target_pairs={{0,496},{16,0},{32,16},{48,32},{64,48},{80,64},{96,80},{112,96},{1... | collective-permute-start | bytes 294920 | tf_op jit(solution)/shard_map/ppermute | solution.py:342
  50.0 1.6 %collective-permute-done.5.back = f32[192,128]{1,0:T(8,128)S(1)} collective-permute-done((f32[192,128]{1,0:T(8,128)S(1)}, f32[192,128]{1,0:T(8,128)S(1)}, u32[]{:S(2)}, u32[]{:S(2)}) %collective-permute-start.5) | collective-permute-done | bytes 98336 | tf_op jit(solution)/shard_map/ppermute | solution.py:342
  51.7 0.0 copy-done.6
  51.7 0.6 shard_map.88
  52.3 4.4 %collective-permute-start.6 = (f32[96,128]{1,0:T(8,128)S(1)}, f32[96,128]{1,0:T(8,128)S(1)}, u32[]{:S(2)}, u32[]{:S(2)}) collective-permute-start(f32[96,128]{1,0:T(8,128)S(1)} %get-tuple-element.8), channel_id=1, source_target_pairs={{0,2},{2,0},{4,6},{6,4},{8,10},{10,8},{12,14},{14,12},{1,3},{3,1},... | collective-permute-start | bytes 147464 | tf_op jit(solution)/shard_map/ppermute | solution.py:364
  56.7 3.0 %collective-permute-start.7 = (f32[96,128]{1,0:T(8,128)S(1)}, f32[96,128]{1,0:T(8,128)S(1)}, u32[]{:S(2)}, u32[]{:S(2)}) collective-permute-start(f32[96,128]{1,0:T(8,128)S(1)} %get-tuple-element.9), channel_id=1, source_target_pairs={{2,4},{4,2},{6,8},{8,6},{10,12},{12,10},{3,5},{5,3},{7,9},{9,7},{1... | collective-permute-start | bytes 147464 | tf_op jit(solution)/shard_map/ppermute | solution.py:365
  59.7 0.0 collective-permute-done.6.chip
  59.7 2.4 %collective-permute-done.7.across = f32[96,128]{1,0:T(8,128)S(1)} collective-permute-done((f32[96,128]{1,0:T(8,128)S(1)}, f32[96,128]{1,0:T(8,128)S(1)}, u32[]{:S(2)}, u32[]{:S(2)}) %collective-permute-start.7) | collective-permute-done | bytes 49184 | tf_op jit(solution)/shard_map/ppermute | solution.py:365
  62.1 0.0 copy-done.3
  62.1 0.0 copy-done.4
  62.1 0.0 copy-done.5
  62.1 0.0 copy-done.1
  62.1 0.0 copy-done.2
  62.1 3.8 %shard_map.89 = (f32[2,3,2,24,96]{4,3,2,1,0:T(8,128)}, f32[2,3,2,24,96]{4,3,2,1,0:T(8,128)}) custom-call(s32[2,3]{1,0:T(2,128)S(1)} %copy-done.6, f32[336,128]{1,0:T(8,128)S(1)} %get-tuple-element.6.held, f32[192,128]{1,0:T(8,128)S(1)} %collective-permute-done.5.back, f32[96,128]{1,0:T(8,128)S(1)} %collective-permute-done.6.chip, ...), custom_call_target="tpu_custom_call" | custom-call | flops 1000000 | bytes 1000000 | tf_op jit(solution)/shard_map/pallas_call | solution.py:367
  (2 shorter events, 0.0 us)
Async XLA Ops:
  0.6 40.8 %copy-start = (f32[2,2,48,768]{3,2,1,0:T(8,128)S(1)}, f32[2,2,48,768]{3,2,1,0:T(8,128)}, u32[]{:S(2)}) copy-start(f32[2,2,48,768]{3,2,1,0:T(8,128)} %refs_5_.1) | copy-start | bytes 1769476
  0.6 40.7 %collective-permute-start.1 = (f32[2,2,48,768]{3,2,1,0:T(8,128)}, f32[2,2,48,768]{3,2,1,0:T(8,128)S(1)}, u32[]{:S(2)}, u32[]{:S(2)}) collective-permute-start(f32[2,2,48,768]{3,2,1,0:T(8,128)} %refs_5_.1), channel_id=1, source_target_pairs={{0,16},{16,32},{32,48},{48,64},{64,80},{80,96},{96,112},{112,128},... | collective-permute-start | bytes 1769480 | tf_op jit(solution)/shard_map/ppermute | solution.py:342
  5.2 36.2 %collective-permute-start = (f32[2,2,48,768]{3,2,1,0:T(8,128)}, f32[2,2,48,768]{3,2,1,0:T(8,128)S(1)}, u32[]{:S(2)}, u32[]{:S(2)}) collective-permute-start(f32[2,2,48,768]{3,2,1,0:T(8,128)} %refs_5_.1), channel_id=1, source_target_pairs={{0,496},{16,0},{32,16},{48,32},{64,48},{80,64},{96,80},{112,96},{1... | collective-permute-start | bytes 1769480 | tf_op jit(solution)/shard_map/ppermute | solution.py:342
  19.0 9.8 %collective-permute-start.2 = (f32[2,48,128]{2,1,0:T(8,128)}, f32[2,48,128]{2,1,0:T(8,128)S(1)}, u32[]{:S(2)}, u32[]{:S(2)}) collective-permute-start(f32[2,48,128]{2,1,0:T(8,128)} %shard_map.86), channel_id=1, source_target_pairs={{0,1},{1,0},{2,3},{3,2},{4,5},{5,4},{6,7},{7,6},{8,9},{9,8},{10,11... | collective-permute-start | bytes 147464 | tf_op jit(solution)/shard_map/ppermute | solution.py:355
  28.8 11.4 %collective-permute-start.4 = (f32[2,48,128]{2,1,0:T(8,128)S(1)}, f32[2,48,128]{2,1,0:T(8,128)S(1)}, u32[]{:S(2)}, u32[]{:S(2)}) collective-permute-start(f32[2,48,128]{2,1,0:T(8,128)S(1)} %collective-permute-done.2.refs_18_), channel_id=1, source_target_pairs={{0,16},{16,32},{32,48},{48,64},{64,80},{80,96},{96,112},{112,128},... | collective-permute-start | bytes 147464 | tf_op jit(solution)/shard_map/ppermute | solution.py:342
  30.7 10.7 %collective-permute-start.3 = (f32[2,48,128]{2,1,0:T(8,128)S(1)}, f32[2,48,128]{2,1,0:T(8,128)S(1)}, u32[]{:S(2)}, u32[]{:S(2)}) collective-permute-start(f32[2,48,128]{2,1,0:T(8,128)S(1)} %collective-permute-done.2.refs_18_), channel_id=1, source_target_pairs={{0,496},{16,0},{32,16},{48,32},{64,48},{80,64},{96,80},{112,96},{1... | collective-permute-start | bytes 147464 | tf_op jit(solution)/shard_map/ppermute | solution.py:342
  41.4 20.7 %copy-start.3 = (f32[128,256]{1,0:T(8,128)S(1)}, f32[128,256]{1,0:T(8,128)}, u32[]{:S(2)}) copy-start(f32[128,256]{1,0:T(8,128)} %constant.10.clone.forward) | copy-start | bytes 393220
  41.4 20.7 %copy-start.4 = (f32[64,64]{1,0:T(8,128)S(1)}, f32[64,64]{1,0:T(8,128)}, u32[]{:S(2)}) copy-start(f32[64,64]{1,0:T(8,128)} %constant.13.clone.down) | copy-start | bytes 49156
  41.4 20.7 %copy-start.5 = (f32[48,64]{1,0:T(8,128)S(1)}, f32[48,64]{1,0:T(8,128)}, u32[]{:S(2)}) copy-start(f32[48,64]{1,0:T(8,128)} %constant.14.clone.up) | copy-start | bytes 36868
  42.7 8.9 %copy-start.6 = (s32[2,3]{1,0:T(2,128)S(1)}, s32[2,3]{1,0:T(2,128)}, u32[]{:S(2)}) copy-start(s32[2,3]{1,0:T(2,128)} %secondaries.3) | copy-start | bytes 76
  42.7 8.9 %collective-permute-start.5 = (f32[192,128]{1,0:T(8,128)S(1)}, f32[192,128]{1,0:T(8,128)S(1)}, u32[]{:S(2)}, u32[]{:S(2)}) collective-permute-start(f32[192,128]{1,0:T(8,128)S(1)} %get-tuple-element.7), channel_id=1, source_target_pairs={{0,496},{16,0},{32,16},{48,32},{64,48},{80,64},{96,80},{112,96},{1... | collective-permute-start | bytes 294920 | tf_op jit(solution)/shard_map/ppermute | solution.py:342
  51.7 10.4 %copy-start.1 = (f32[128,256]{1,0:T(8,128)S(1)}, f32[128,256]{1,0:T(8,128)}, u32[]{:S(2)}) copy-start(f32[128,256]{1,0:T(8,128)} %constant.12.clone.inverse) | copy-start | bytes 393220
  51.7 10.4 %copy-start.2 = (f32[128,256]{1,0:T(8,128)S(1)}, f32[128,256]{1,0:T(8,128)}, u32[]{:S(2)}) copy-start(f32[128,256]{1,0:T(8,128)} %constant.11.clone.spread) | copy-start | bytes 393220
  52.3 7.4 %collective-permute-start.6 = (f32[96,128]{1,0:T(8,128)S(1)}, f32[96,128]{1,0:T(8,128)S(1)}, u32[]{:S(2)}, u32[]{:S(2)}) collective-permute-start(f32[96,128]{1,0:T(8,128)S(1)} %get-tuple-element.8), channel_id=1, source_target_pairs={{0,2},{2,0},{4,6},{6,4},{8,10},{10,8},{12,14},{14,12},{1,3},{3,1},... | collective-permute-start | bytes 147464 | tf_op jit(solution)/shard_map/ppermute | solution.py:364
  56.7 5.4 %collective-permute-start.7 = (f32[96,128]{1,0:T(8,128)S(1)}, f32[96,128]{1,0:T(8,128)S(1)}, u32[]{:S(2)}, u32[]{:S(2)}) collective-permute-start(f32[96,128]{1,0:T(8,128)S(1)} %get-tuple-element.9), channel_id=1, source_target_pairs={{2,4},{4,2},{6,8},{8,6},{10,12},{12,10},{3,5},{5,3},{7,9},{9,7},{1... | collective-permute-start | bytes 147464 | tf_op jit(solution)/shard_map/ppermute | solution.py:365

commit v2 on v1

v2 whole, which is shorter than its diff:
```python
import functools
import math

import jax
import jax.numpy as jnp
import numpy as np
from jax import lax
from jax.experimental import pallas as pl
from jax.experimental.pallas import tpu as pltpu
from jax.sharding import PartitionSpec as P

KEEP = 24
PATCH = 32
MARGIN = 4
LANES = 128
STRIP = 32
RIGHT = 100
LINKS = 3
RUN = 16
F32 = jnp.float32
BF16 = jnp.bfloat16

HELD = ((0, 1), (0, 2), (0, 3), (1, 2), (1, 3))
SENT = ((-2, 2), (-1, 2), (-1, 3))
CANDIDATES = tuple((a - 2, b - 2) for a in range(2) for b in range(a + 1, a + 5))
PLANES = 2 * len(CANDIDATES) + 6


def vmem():
    return pl.BlockSpec(memory_space=pltpu.VMEM)


def smem():
    return pl.BlockSpec(memory_space=pltpu.SMEM)


def call(kernel, outs, count, scratch=(), specs=None, flops=1e6, moved=1e6):
    return pl.pallas_call(
        kernel,
        out_shape=outs,
        in_specs=specs or [vmem()] * count,
        out_specs=jax.tree.map(lambda _: vmem(), outs),
        scratch_shapes=list(scratch),
        compiler_params=pltpu.CompilerParams(vmem_limit_bytes=32 * 1024 * 1024),
        cost_estimate=pl.CostEstimate(flops=int(flops), bytes_accessed=int(moved), transcendentals=0),
    )


def lane_index(shape):
    return lax.broadcasted_iota(jnp.int32, shape, len(shape) - 1)


def looks_table(cols):
    source = lax.broadcasted_iota(jnp.int32, (cols, LANES), 0)
    target = lax.broadcasted_iota(jnp.int32, (cols, LANES), 1)
    return jnp.where((source >> 3) + MARGIN == target, 1.0 / 16.0, 0.0).astype(BF16)


def split_dot(values, table):
    high = values.astype(BF16)
    rest = values - high.astype(F32)
    middle = rest.astype(BF16)
    low = (rest - middle.astype(F32)).astype(BF16)
    dot = lambda v: jnp.dot(v, table, preferred_element_type=F32)
    return dot(high) + (dot(middle) + dot(low))


def tiled(images):
    rows, cols = images.shape[2:]
    spec = lambda index: pl.BlockSpec((2, 2, rows, LANES), lambda i: (0, 0, 0, index))
    return [spec(index) for index in range(cols // LANES)]


def keep_kernel(source, target, arrived):
    copies = [
        pltpu.make_async_copy(
            source.at[:, :, :, pl.ds(tile * LANES, LANES)], target.at[tile], arrived.at[tile]
        )
        for tile in range(target.shape[0])
    ]
    for copy in copies:
        copy.start()
    for copy in copies:
        copy.wait()


def kept(images):
    tiles = images.shape[3] // LANES
    return pl.pallas_call(
        keep_kernel,
        out_shape=pltpu.VMEM((tiles,) + images.shape[:3] + (LANES,), F32),
        in_specs=[pl.BlockSpec(memory_space=pl.ANY)],
        out_specs=vmem(),
        scratch_shapes=[pltpu.SemaphoreType.DMA((tiles,))],
    )(images)


def product(a, b):
    (ar, ai), (br, bi) = a, b
    real = (ar[0] * br[0] + ai[0] * bi[0]) + (ar[1] * br[1] + ai[1] * bi[1])
    imag = (ai[0] * br[0] - ar[0] * bi[0]) + (ai[1] * br[1] - ar[1] * bi[1])
    return real, imag


def power(a):
    ar, ai = a
    return (ar[0] * ar[0] + ai[0] * ai[0]) + (ar[1] * ar[1] + ai[1] * ai[1])


def reader(own, others):
    half = own.shape[3] // 2

    def image(slot, tile):
        def value(part, parity):
            rows = pl.ds(parity, half, stride=2)
            if 0 <= slot < 2:
                return own[tile, slot, part, rows, :]
            here, there, turn = others[slot // 2]
            first = here[tile][slot % 2, part, rows, :]
            return first if there is None else jnp.where(turn, there[tile][slot % 2, part, rows, :], first)

        return [[value(part, parity) for parity in range(2)] for part in range(2)]

    return image


def fill(stage, image, tiles, half, pairs, slots):
    for tile in range(tiles):
        lanes = pl.ds(tile * LANES, LANES)
        loaded = {slot: image(slot, tile) for slot in {s for pair in pairs for s in pair} | set(slots)}
        values = [v for a, b in pairs for v in product(loaded[a], loaded[b])]
        values += [power(loaded[slot]) for slot in slots]
        for n, value in enumerate(values):
            stage[pl.ds(n * half, half), lanes] = value


def meet(stage, image, tiles, half, sent, side):
    fill(stage, image, tiles, half, SENT, (2, 3))
    at_left = lax.axis_index("col") == 0

    def border(slot):
        here, there = image(slot, tiles - 1), image(slot, 0)
        return [
            [jnp.where(at_left, pltpu.roll(v, STRIP, 1), w) for v, w in zip(p, q)]
            for p, q in zip(here, there)
        ]

    bordered = {slot: border(slot) for slot in range(-2, 4)}
    values = [v for a, b in CANDIDATES for v in product(bordered[a], bordered[b])]
    values += [power(bordered[slot]) for slot in range(-2, 4)]
    block = lane_index((half, LANES)) >> 5
    rows = pl.ds((2 * len(SENT) + 2) * half, half)
    for tile in range(tiles):
        row = jnp.zeros((half, LANES), F32)
        for k, value in enumerate(values[4 * tile : 4 * tile + 4]):
            row = jnp.where(block == k, pltpu.roll(value, STRIP * k, 1) if k else value, row)
        stage[rows, pl.ds(tile * LANES, LANES)] = row
    means = split_dot(stage[...], looks_table(tiles * LANES))
    end = (2 * len(SENT) + 2) * half
    sent[...] = means[:end]
    side[...] = means[end:]


def meet_kernel(*refs):
    own, (sent, side, stage) = refs[0], refs[-3:]
    tiles, half = own.shape[0], own.shape[3] // 2
    before, before_wrap, after = [refs[1 + n * tiles : 1 + (n + 1) * tiles] for n in range(3)]
    first = lax.axis_index("date") % RUN == 0
    image = reader(own, {-1: (before, before_wrap, first), 1: (after, None, None)})
    meet(stage, image, tiles, half, sent, side)


def held_kernel(*refs):
    own, (held, sent, side, stage, second) = refs[0], refs[-5:]
    tiles, half = own.shape[0], own.shape[3] // 2
    after, after_wrap, before = [refs[1 + n * tiles : 1 + (n + 1) * tiles] for n in range(3)]
    last = lax.axis_index("date") % RUN == RUN - 1
    fill(stage, reader(own, {1: (after, after_wrap, last)}), tiles, half, HELD, range(4))
    held[...] = split_dot(stage[...], looks_table(tiles * LANES))

    @pl.when(last)
    def _():
        image = reader(own, {-1: (before, None, None), 1: (after_wrap, None, None)})
        meet(second, image, tiles, half, sent, side)


def on_tiles(kernel, counts, stages, own, *images, behind=()):
    rows, cols = images[0].shape[2:]
    half = rows // 2
    whole = lambda shape: pl.BlockSpec(shape, lambda i: (0,) * len(shape))
    return pl.pallas_call(
        kernel,
        grid=(1,),
        out_shape=tuple(jax.ShapeDtypeStruct((count * half, LANES), F32) for count in counts),
        in_specs=[whole(own.shape)] + [spec for image in images for spec in tiled(image)]
        + [whole(value.shape) for value in behind],
        out_specs=tuple(whole((count * half, LANES)) for count in counts),
        scratch_shapes=[pltpu.VMEM((count * half, cols), F32) for count in stages],
        compiler_params=pltpu.CompilerParams(vmem_limit_bytes=32 * 1024 * 1024),
    )(own, *[image for image in images for _ in range(cols // LANES)], *behind)


def rims_kernel(secondaries, held, side, back, late_side, late_back, picked, chip, across, every):
    at_left = lax.axis_index("col") == 0
    lanes = lane_index((KEEP, LANES))
    place = jnp.where(at_left, RIGHT, 0)
    margin = (lanes >= place) & (lanes < place + MARGIN)
    late = lax.axis_index("date") % RUN == RUN - 2
    columns = jnp.where(late, late_side[...], side[...])
    held_at, back_at = 0, 0
    for n in range(PLANES):
        pair = n // 2
        from_back = pair in (3, 6, 7) or n >= PLANES - 2
        if from_back:
            rows = pl.ds(back_at * KEEP, KEEP)
            value, back_at = jnp.where(late, late_back[rows, :], back[rows, :]), back_at + 1
        else:
            value, held_at = held[pl.ds(held_at * KEEP, KEEP), :], held_at + 1
        here = MARGIN + MARGIN * n
        right = pltpu.roll(columns, (RIGHT - here) % LANES, 1)
        left = pltpu.roll(columns, -here % LANES, 1)
        every[pl.ds(n * KEEP, KEEP), :] = jnp.where(margin, jnp.where(at_left, right, left), value)

    first = 2 * lax.axis_index("date")
    dates = 2 * lax.axis_size("date")
    even = lax.axis_index("row") % 2 == 0
    starts = []
    for date in range(2):
        for link in range(LINKS):
            slot = (secondaries[date, link] - first + dates) % dates
            pair = 3 * date + slot - 1
            starts += [2 * pair, 2 * pair + 1, PLANES - 6 + slot]
    starts += [PLANES - 6 + date for date in range(2)]
    for n, start in enumerate(starts):
        at = start * KEEP if isinstance(start, int) else pl.multiple_of(start * KEEP, 8)
        value = every[pl.ds(at, KEEP), :]
        picked[pl.ds(n * KEEP, KEEP), :] = value
        top, bottom = value[:MARGIN], value[KEEP - MARGIN :]
        chip[pl.ds(MARGIN * n, MARGIN), :] = jnp.where(even, bottom, top)
        across[pl.ds(MARGIN * n, MARGIN), :] = jnp.where(even, top, bottom)


@functools.lru_cache(None)
def tables():
    blocks = LANES // PATCH
    n = np.arange(PATCH)
    angle = 2.0 * np.pi * (np.outer(n, n) % PATCH) / PATCH
    cosine, sine = np.cos(angle), np.sin(angle)
    forward = np.zeros((LANES, 2 * LANES))
    spread = np.zeros((LANES, 2 * LANES))
    inverse = np.zeros((LANES, 2 * LANES))
    for b in range(blocks):
        f = slice(b * PATCH, (b + 1) * PATCH)
        x = slice(b * KEEP, b * KEEP + PATCH)
        o = slice(b * KEEP, (b + 1) * KEEP)
        kept = slice(MARGIN, MARGIN + KEEP)
        forward[x, f] = cosine
        forward[x, LANES + b * PATCH : LANES + (b + 1) * PATCH] = -sine
        inverse[f, o] = cosine[:, kept] / PATCH
        inverse[f, LANES + b * KEEP : LANES + (b + 1) * KEEP] = sine[:, kept] / PATCH
        near = (n[:, None] - n[None, :]) % PATCH
        spread[f, f] = (near == 0) | (near == 1) | (near == PATCH - 1)
        spread[f, LANES + b * PATCH : LANES + (b + 1) * PATCH] = 1.0
    down = np.block([[cosine, sine], [-sine, cosine]])
    kept = slice(MARGIN, MARGIN + KEEP)
    up = np.block([[cosine[kept], -sine[kept]], [sine[kept], cosine[kept]]]) / PATCH
    return [np.asarray(t, np.float32) for t in (forward, spread, inverse, down, up)]


def exact_dot(a, b):
    return jnp.dot(a, b, preferred_element_type=F32, precision=lax.Precision.HIGHEST)


def filter_kernel(picked, across, chip, forward, spread, inverse, down, up, filtered, coherent, pad):
    even = lax.axis_index("row") % 2 == 0
    pairs = 2 * LINKS
    for n in range(3 * pairs + 2):
        near, far = chip[pl.ds(MARGIN * n, MARGIN), :], across[pl.ds(MARGIN * n, MARGIN), :]
        pad[n, pl.ds(0, MARGIN), :] = jnp.where(even, far, near)
        pad[n, pl.ds(MARGIN, KEEP), :] = picked[pl.ds(n * KEEP, KEEP), :]
        pad[n, pl.ds(MARGIN + KEEP, MARGIN), :] = jnp.where(even, near, far)

    def box(value):
        rows = value[3 : 3 + KEEP] + value[4 : 4 + KEEP] + value[5 : 5 + KEEP]
        total = pltpu.roll(rows, LANES - 3, 1) + pltpu.roll(rows, LANES - 4, 1) + pltpu.roll(rows, LANES - 5, 1)
        return total * (1.0 / 9.0)

    wide = coherent.shape[-1]
    firsts = [box(pad[3 * pairs + date]) for date in range(2)]
    for p in range(pairs):
        real, imag, second = [box(pad[3 * p + k]) for k in range(3)]
        factor = lax.rsqrt(firsts[p // LINKS] * second + 1e-06)
        coherent[p // LINKS, p % LINKS, 0] = (real * factor)[:, :wide]
        coherent[p // LINKS, p % LINKS, 1] = (imag * factor)[:, :wide]

    reals = jnp.concatenate([pad[3 * p] for p in range(pairs)], axis=0)
    imags = jnp.concatenate([pad[3 * p + 1] for p in range(pairs)], axis=0)
    size = pairs * PATCH
    across_cols = exact_dot(jnp.concatenate([reals, imags], axis=0), forward[...])
    col_real = across_cols[:size, :LANES] - across_cols[size:, LANES:]
    col_imag = across_cols[size:, :LANES] + across_cols[:size, LANES:]
    rows_of = lambda v, p, count: v[p * count : (p + 1) * count]
    stacked = jnp.concatenate(
        [
            jnp.concatenate([rows_of(col_real, p, PATCH), rows_of(col_imag, p, PATCH)], axis=0)
            for p in range(pairs)
        ],
        axis=1,
    )
    spectrum = exact_dot(down[...], stacked)
    real, imag = spectrum[:PATCH], spectrum[PATCH:]
    power = real * real + imag * imag
    lanes_of = lambda v, p: v[:, p * LANES : (p + 1) * LANES]
    tall = lambda v: jnp.concatenate([lanes_of(v, p) for p in range(pairs)], axis=0)
    sums = exact_dot(tall(power), spread[...])
    weights = []
    for p in range(pairs):
        near = rows_of(sums, p, PATCH)[:, :LANES]
        level = jnp.sum(rows_of(sums, p, PATCH)[:, LANES:], axis=0, keepdims=True) * (1.0 / (PATCH * PATCH))
        smooth = (near + pltpu.roll(near, 1, 0) + pltpu.roll(near, PATCH - 1, 0)) * (1.0 / 9.0)
        weights.append(jnp.sqrt(jnp.sqrt(smooth + level + 1e-06)))
    totals = exact_dot(jnp.concatenate(weights, axis=0), spread[:, LANES:])
    scaled = []
    for p in range(pairs):
        total = jnp.sum(rows_of(totals, p, PATCH), axis=0, keepdims=True)
        scaled.append(weights[p] * ((PATCH * PATCH) / total))
    weight = jnp.concatenate(scaled, axis=1)
    lifted = exact_dot(up[...], jnp.concatenate([real * weight, imag * weight], axis=0))
    low, high = lifted[:KEEP], lifted[KEEP:]
    size = pairs * KEEP
    result = exact_dot(jnp.concatenate([tall(low), tall(high)], axis=0), inverse[...])
    out_real = result[:size, :LANES] - result[size:, LANES:]
    out_imag = result[size:, :LANES] + result[:size, LANES:]
    for p in range(pairs):
        filtered[p // LINKS, p % LINKS, 0] = rows_of(out_real, p, KEEP)[:, :wide]
        filtered[p // LINKS, p % LINKS, 1] = rows_of(out_imag, p, KEEP)[:, :wide]


def body(images, secondaries):
    rows, cols = images.shape[2:]
    cells_down, cells_along = rows // 2, cols // 8
    dates, count = lax.axis_size("date"), lax.axis_size("row")
    inner = lambda steps: [(d, d + steps) for d in range(dates) if 0 <= d % RUN + steps < RUN]
    outer = lambda steps: [(d, (d + steps) % dates) for d in range(dates) if not 0 <= d % RUN + steps < RUN]
    along = lambda value, pairs: lax.ppermute(value, "date", pairs)
    across = lambda value, pairs: lax.ppermute(
        value, ("date", "col"), [(2 * d + c, 2 * e + (c ^ 1)) for d, e in pairs for c in range(2)]
    )
    after, before = along(images, inner(-1)), along(images, inner(1))
    after_wrap, before_wrap = along(images, outer(-1)), along(images, outer(1))
    own = kept(images)
    total = 2 * len(SENT) + 2
    sent, side = on_tiles(meet_kernel, (total, 1), (total + 1,), own, before, before_wrap, after)
    soon = [(d, (d - 1) % dates) for d in range(dates) if d % RUN < RUN - 1]
    late = [(d, d - 1) for d in range(dates) if d % RUN == RUN - 1]
    side, back = across(side, soon), along(sent, soon)
    keeps = 2 * len(HELD) + 4
    held, late_sent, late_side = on_tiles(
        held_kernel, (keeps, total, 1), (keeps, total + 1), own, after, after_wrap, before, behind=(side, back)
    )
    late_side, late_back = across(late_side, late), along(late_sent, late)

    planes = 3 * 2 * LINKS + 2
    rim = jax.ShapeDtypeStruct((planes * MARGIN, LANES), F32)
    every = pltpu.VMEM((PLANES * cells_down, LANES), F32)
    picked = jax.ShapeDtypeStruct((planes * cells_down, LANES), F32)
    picked, chip, across = call(rims_kernel, (picked, rim, rim), 6, [every], [smem()] + [vmem()] * 5)(
        secondaries, held, side, back, late_side, late_back
    )
    chip = lax.ppermute(chip, "row", [(i, i ^ 1) for i in range(count)])
    across = lax.ppermute(across, "row", [(i, ((i + 1) ^ 1) - 1) for i in range(1, count - 1)])
    out = jax.ShapeDtypeStruct((2, LINKS, 2, cells_down, cells_along), F32)
    return call(filter_kernel, (out, out), 8, [pltpu.VMEM((planes, PATCH, LANES), F32)])(
        picked, across, chip, *tables()
    )


def solution(mesh):
    in_specs = (P("date", None, "row", "col"), P("date", None))
    out_specs = (P("date", None, None, "row", "col"), P("date", None, None, "row", "col"))
    return jax.shard_map(body, mesh=mesh, in_specs=in_specs, out_specs=out_specs, check_vma=False)
```

time: 66.2 us -> 56.2 us (0.85)
  starting transfers between devices: 45.1 us -> 34.9 us
    ppermute x8 -> x10, starting transfers between devices: 45.1 us -> 34.9 us  [the longest x6 24.1 us: body(): along = lambda value, pairs: lax.ppermute(value, 'date', pairs)]
    ppermute x8 -> x10, waiting for transfers between devices: 12.6 us -> 13.1 us  [the longest x6 8.54 us: body(): along = lambda value, pairs: lax.ppermute(value, 'date', pairs)]
    pallas_call x4 -> x5, Pallas kernels: 7.43 us -> 6.93 us  [the longest x1 3.22 us: body(): call(filter_kernel, (out, out), 8, [pltpu.VMEM((planes, PATCH, LANES), F3...]
  transfers between devices with their start and end apart: 8 -> 10, of which waited for: 4 -> 3; matrix products, arithmetic and copies ran while one was open for 0% -> 0% of each run, Pallas kernels for 3% -> 4%
where the time goes in v2:
time: 56.2 us; the launch traced here: 55.9 us
  starting transfers between devices  34.9 us (62%)
  waiting for transfers between devices  13.1 us (23%)
  Pallas kernels  6.93 us (12%)
  between operations  0.84 us (1%)
    ppermute x6, starting transfers between devices, body(): along = lambda value, pairs: lax.ppermute(value, 'date', pairs)  24.1 us
    ppermute x6, waiting for transfers between devices, body(): along = lambda value, pairs: lax.ppermute(value, 'date', pairs)  8.54 us
    ppermute x1, starting transfers between devices, body(): lax.ppermute(across, 'row', [(i, (i + 1 ^ 1) - 1) for i in range(1, count...  6.3 us
    ppermute x2, waiting for transfers between devices, body(): lax.ppermute(value, ('date', 'col'), [(2 * d + c, 2 * e + (c ^ 1)) for d,...  3.4 us
    pallas_call x1, Pallas kernels, body(): call(filter_kernel, (out, out), 8, [pltpu.VMEM((planes, PATCH, LANES), F3...  3.22 us
    ppermute x2, starting transfers between devices, body(): lax.ppermute(value, ('date', 'col'), [(2 * d + c, 2 * e + (c ^ 1)) for d,...  2.58 us
    ppermute x1, starting transfers between devices, body(): chip = lax.ppermute(chip, 'row', [(i, i ^ 1) for i in range(count)])  1.92 us
    pallas_call x2, Pallas kernels, on_tiles(): pl.pallas_call(kernel, grid=(1,), out_shape=tuple((jax.ShapeDtypeStruct((...  1.77 us
  transfers between devices with their start and end apart: 10, of which 3 were waited for; matrix products, arithmetic and copies ran while one was open for 0% of the time, Pallas kernels for 4%

profile of v2, /device:TPU:1, one launch (start us, length us, event | category | flops | bytes accessed | tf_op | source)
XLA Modules:
  0.0 55.9 jit_solution(2026668480772629370)
XLA Ops:
  0.6 1.3 %collective-permute-start = (f32[2,2,48,768]{3,2,1,0:T(8,128)}, f32[2,2,48,768]{3,2,1,0:T(8,128)S(1)}, u32[]{:S(2)}, u32[]{:S(2)}) collective-permute-start(f32[2,2,48,768]{3,2,1,0:T(8,128)} %source.1), channel_id=1, source_target_pairs={{16,0},{32,16},{48,32},{64,48},{80,64},{96,80},{112,96},{128,112},... | collective-permute-start | bytes 1769480 | tf_op jit(solution)/shard_map/ppermute | solution.py:345
  1.9 5.0 %collective-permute-start.2 = (f32[2,2,48,768]{3,2,1,0:T(8,128)}, f32[2,2,48,768]{3,2,1,0:T(8,128)S(1)}, u32[]{:S(2)}, u32[]{:S(2)}) collective-permute-start(f32[2,2,48,768]{3,2,1,0:T(8,128)} %source.1), channel_id=1, source_target_pairs={{0,16},{16,32},{32,48},{48,64},{64,80},{80,96},{96,112},{112,128},... | collective-permute-start | bytes 1769480 | tf_op jit(solution)/shard_map/ppermute | solution.py:345
  7.0 1.3 %collective-permute-start.3 = (f32[2,2,48,768]{3,2,1,0:T(8,128)}, f32[2,2,48,768]{3,2,1,0:T(8,128)S(1)}, u32[]{:S(2)}, u32[]{:S(2)}) collective-permute-start(f32[2,2,48,768]{3,2,1,0:T(8,128)} %source.1), channel_id=1, source_target_pairs={{240,256},{496,0},{241,257},{497,1},{242,258},{498,2},{243,259},{4... | collective-permute-start | bytes 1769480 | tf_op jit(solution)/shard_map/ppermute | solution.py:345
  8.3 12.3 %collective-permute-start.1 = (f32[2,2,48,768]{3,2,1,0:T(8,128)}, f32[2,2,48,768]{3,2,1,0:T(8,128)S(1)}, u32[]{:S(2)}, u32[]{:S(2)}) collective-permute-start(f32[2,2,48,768]{3,2,1,0:T(8,128)} %source.1), channel_id=1, source_target_pairs={{0,496},{256,240},{1,497},{257,241},{2,498},{258,242},{3,499},{259... | collective-permute-start | bytes 1769480 | tf_op jit(solution)/shard_map/ppermute | solution.py:345
  20.6 1.2 %shard_map.86.refs_0_ = f32[6,2,2,48,128]{4,3,2,1,0:T(8,128)S(1)} custom-call(f32[2,2,48,768]{3,2,1,0:T(8,128)} %source.1), custom_call_target="tpu_custom_call" | custom-call | tf_op jit(solution)/shard_map/pallas_call | solution.py:89
  21.8 0.0 collective-permute-done.refs_13_.refs_14_.refs_15_.refs_16_.refs_17_.refs_18_.refs_1_.refs_2_.refs_3_.refs_4_.refs_5_.refs_6_
  21.8 0.0 collective-permute-done.2.refs_1_.refs_2_.refs_3_.refs_4_.refs_5_.refs_6_.refs_13_.refs_14_.refs_15_.refs_16_.refs_17_.refs_18_
  21.8 8.5 %collective-permute-done.3.refs_7_.refs_8_.refs_9_.refs_10_.refs_11_.refs_12_ = f32[2,2,48,768]{3,2,1,0:T(8,128)S(1)} collective-permute-done((f32[2,2,48,768]{3,2,1,0:T(8,128)}, f32[2,2,48,768]{3,2,1,0:T(8,128)S(1)}, u32[]{:S(2)}, u32[]{:S(2)}) %collective-permute-start.3) | collective-permute-done | bytes 589856 | tf_op jit(solution)/shard_map/ppermute | solution.py:345
  30.3 0.9 %shard_map.87 = (f32[192,128]{1,0:T(8,128)S(1)}, f32[24,128]{1,0:T(8,128)S(1)}) custom-call(f32[6,2,2,48,128]{4,3,2,1,0:T(8,128)S(1)} %shard_map.86.refs_0_, f32[2,2,48,768]{3,2,1,0:T(8,128)S(1)} %collective-permute-done.2.refs_1_.refs_2_.refs_3_.refs_4_.refs_5_.refs_6_.refs_13_.refs_14_.refs_15_.refs_16_.refs_17_.refs_18_, ...), custom_call_target="tpu_custom_call" | custom-call | tf_op jit(solution)/shard_map/pallas_call | solution.py:191
  31.2 3.6 %collective-permute-start.5 = (f32[192,128]{1,0:T(8,128)S(1)}, f32[192,128]{1,0:T(8,128)S(1)}, u32[]{:S(2)}, u32[]{:S(2)}) collective-permute-start(f32[192,128]{1,0:T(8,128)S(1)} %get-tuple-element.11), channel_id=1, source_target_pairs={{0,496},{16,0},{32,16},{48,32},{64,48},{80,64},{96,80},{112,96},{1... | collective-permute-start | bytes 294920 | tf_op jit(solution)/shard_map/ppermute | solution.py:345
  34.7 1.9 %collective-permute-start.4 = (f32[24,128]{1,0:T(8,128)S(1)}, f32[24,128]{1,0:T(8,128)S(1)}, u32[]{:S(2)}, u32[]{:S(2)}) collective-permute-start(f32[24,128]{1,0:T(8,128)S(1)} %get-tuple-element.10), channel_id=1, source_target_pairs={{0,497},{1,496},{16,1},{17,0},{32,17},{33,16},{48,33},{49,32},{64,... | collective-permute-start | bytes 36872 | tf_op jit(solution)/shard_map/ppermute | solution.py:346
  36.7 0.0 collective-permute-done.1.refs_7_.refs_8_.refs_9_.refs_10_.refs_11_.refs_12_
  36.7 3.4 %collective-permute-done.4.refs_19_.side = f32[24,128]{1,0:T(8,128)S(1)} collective-permute-done((f32[24,128]{1,0:T(8,128)S(1)}, f32[24,128]{1,0:T(8,128)S(1)}, u32[]{:S(2)}, u32[]{:S(2)}) %collective-permute-start.4) | collective-permute-done | bytes 12320 | tf_op jit(solution)/shard_map/ppermute | solution.py:346
  40.1 0.0 collective-permute-done.5.refs_20_.back
  40.1 0.9 %shard_map.88 = (f32[336,128]{1,0:T(8,128)S(1)}, f32[192,128]{1,0:T(8,128)S(1)}, f32[24,128]{1,0:T(8,128)S(1)}) custom-call(f32[6,2,2,48,128]{4,3,2,1,0:T(8,128)S(1)} %shard_map.86.refs_0_, f32[2,2,48,768]{3,2,1,0:T(8,128)S(1)} %collective-permute-done.refs_13_.refs_14_.refs_15_.refs_16_.refs_17_.refs_18_.refs_1_.refs_2_.refs_3_.refs_4_.refs_5_.refs_6_, ...), custom_call_target="tpu_custom_call" | custom-call | tf_op jit(solution)/shard_map/pallas_call | solution.py:191
  41.0 0.7 %collective-permute-start.7 = (f32[192,128]{1,0:T(8,128)S(1)}, f32[192,128]{1,0:T(8,128)S(1)}, u32[]{:S(2)}, u32[]{:S(2)}) collective-permute-start(f32[192,128]{1,0:T(8,128)S(1)} %get-tuple-element.14), channel_id=1, source_target_pairs={{240,224},{496,480},{241,225},{497,481},{242,226},{498,482},{243,2... | collective-permute-start | bytes 294920 | tf_op jit(solution)/shard_map/ppermute | solution.py:345
  41.7 0.0 copy-start.5
  41.7 0.7 %collective-permute-start.6 = (f32[24,128]{1,0:T(8,128)S(1)}, f32[24,128]{1,0:T(8,128)S(1)}, u32[]{:S(2)}, u32[]{:S(2)}) collective-permute-start(f32[24,128]{1,0:T(8,128)S(1)} %get-tuple-element.13), channel_id=1, source_target_pairs={{240,225},{241,224},{496,481},{497,480},{242,227},{243,226},{498,4... | collective-permute-start | bytes 36872 | tf_op jit(solution)/shard_map/ppermute | solution.py:346
  42.4 0.0 collective-permute-done.6.late_side
  42.4 0.0 collective-permute-done.7.late_back
  42.4 0.0 copy-start
  42.4 0.0 copy-start.1
  42.4 0.0 copy-start.2
  42.4 0.8 %shard_map.89 = (f32[480,128]{1,0:T(8,128)S(1)}, f32[80,128]{1,0:T(8,128)S(1)}, f32[80,128]{1,0:T(8,128)S(1)}) custom-call(s32[2,3]{1,0:T(2,128)S(1)} %copy-done.5, f32[336,128]{1,0:T(8,128)S(1)} %get-tuple-element.12.held, f32[24,128]{1,0:T(8,128)S(1)} %collective-permute-done.4.refs_19_.side, f32[192,128]{1,0:T(8,128)S(1)} %collective-permute-done.5.refs_20_.back, ...), custom_call_target="tpu_custom_call" | custom-call | flops 1000000 | bytes 1000000 | tf_op jit(solution)/shard_map/pallas_call | solution.py:367
  43.2 6.3 %collective-permute-start.8 = (f32[80,128]{1,0:T(8,128)S(1)}, f32[80,128]{1,0:T(8,128)S(1)}, u32[]{:S(2)}, u32[]{:S(2)}) collective-permute-start(f32[80,128]{1,0:T(8,128)S(1)} %get-tuple-element.16), channel_id=1, source_target_pairs={{2,4},{4,2},{6,8},{8,6},{10,12},{12,10},{3,5},{5,3},{7,9},{9,7},{1... | collective-permute-start | bytes 122888 | tf_op jit(solution)/shard_map/ppermute | solution.py:371
  49.5 1.9 %collective-permute-start.9 = (f32[80,128]{1,0:T(8,128)S(1)}, f32[80,128]{1,0:T(8,128)S(1)}, u32[]{:S(2)}, u32[]{:S(2)}) collective-permute-start(f32[80,128]{1,0:T(8,128)S(1)} %get-tuple-element.17), channel_id=1, source_target_pairs={{0,2},{2,0},{4,6},{6,4},{8,10},{10,8},{12,14},{14,12},{1,3},{3,1},... | collective-permute-start | bytes 122888 | tf_op jit(solution)/shard_map/ppermute | solution.py:370
  51.4 0.0 collective-permute-done.8.across
  51.4 1.2 %collective-permute-done.9.chip = f32[80,128]{1,0:T(8,128)S(1)} collective-permute-done((f32[80,128]{1,0:T(8,128)S(1)}, f32[80,128]{1,0:T(8,128)S(1)}, u32[]{:S(2)}, u32[]{:S(2)}) %collective-permute-start.9) | collective-permute-done | bytes 40992 | tf_op jit(solution)/shard_map/ppermute | solution.py:370
  52.6 0.0 copy-done
  52.6 0.0 copy-done.1
  52.6 0.0 copy-done.2
  52.6 3.2 %shard_map.90 = (f32[2,3,2,24,96]{4,3,2,1,0:T(8,128)}, f32[2,3,2,24,96]{4,3,2,1,0:T(8,128)}) custom-call(f32[480,128]{1,0:T(8,128)S(1)} %get-tuple-element.15.picked, f32[80,128]{1,0:T(8,128)S(1)} %collective-permute-done.8.across, f32[80,128]{1,0:T(8,128)S(1)} %collective-permute-done.9.chip, f32[128,256]{1,0:T(8,128)S(1)} %copy-done, ...), custom_call_target="tpu_custom_call" | custom-call | flops 1000000 | bytes 1000000 | tf_op jit(solution)/shard_map/pallas_call | solution.py:373
  (5 shorter events, 0.0 us)
Async XLA Ops:
  0.6 21.1 %collective-permute-start = (f32[2,2,48,768]{3,2,1,0:T(8,128)}, f32[2,2,48,768]{3,2,1,0:T(8,128)S(1)}, u32[]{:S(2)}, u32[]{:S(2)}) collective-permute-start(f32[2,2,48,768]{3,2,1,0:T(8,128)} %source.1), channel_id=1, source_target_pairs={{16,0},{32,16},{48,32},{64,48},{80,64},{96,80},{112,96},{128,112},... | collective-permute-start | bytes 1769480 | tf_op jit(solution)/shard_map/ppermute | solution.py:345
  1.9 19.8 %collective-permute-start.2 = (f32[2,2,48,768]{3,2,1,0:T(8,128)}, f32[2,2,48,768]{3,2,1,0:T(8,128)S(1)}, u32[]{:S(2)}, u32[]{:S(2)}) collective-permute-start(f32[2,2,48,768]{3,2,1,0:T(8,128)} %source.1), channel_id=1, source_target_pairs={{0,16},{16,32},{32,48},{48,64},{64,80},{80,96},{96,112},{112,128},... | collective-permute-start | bytes 1769480 | tf_op jit(solution)/shard_map/ppermute | solution.py:345
  7.0 23.3 %collective-permute-start.3 = (f32[2,2,48,768]{3,2,1,0:T(8,128)}, f32[2,2,48,768]{3,2,1,0:T(8,128)S(1)}, u32[]{:S(2)}, u32[]{:S(2)}) collective-permute-start(f32[2,2,48,768]{3,2,1,0:T(8,128)} %source.1), channel_id=1, source_target_pairs={{240,256},{496,0},{241,257},{497,1},{242,258},{498,2},{243,259},{4... | collective-permute-start | bytes 1769480 | tf_op jit(solution)/shard_map/ppermute | solution.py:345
  8.3 28.4 %collective-permute-start.1 = (f32[2,2,48,768]{3,2,1,0:T(8,128)}, f32[2,2,48,768]{3,2,1,0:T(8,128)S(1)}, u32[]{:S(2)}, u32[]{:S(2)}) collective-permute-start(f32[2,2,48,768]{3,2,1,0:T(8,128)} %source.1), channel_id=1, source_target_pairs={{0,496},{256,240},{1,497},{257,241},{2,498},{258,242},{3,499},{259... | collective-permute-start | bytes 1769480 | tf_op jit(solution)/shard_map/ppermute | solution.py:345
  31.2 8.9 %collective-permute-start.5 = (f32[192,128]{1,0:T(8,128)S(1)}, f32[192,128]{1,0:T(8,128)S(1)}, u32[]{:S(2)}, u32[]{:S(2)}) collective-permute-start(f32[192,128]{1,0:T(8,128)S(1)} %get-tuple-element.11), channel_id=1, source_target_pairs={{0,496},{16,0},{32,16},{48,32},{64,48},{80,64},{96,80},{112,96},{1... | collective-permute-start | bytes 294920 | tf_op jit(solution)/shard_map/ppermute | solution.py:345
  34.7 5.3 %collective-permute-start.4 = (f32[24,128]{1,0:T(8,128)S(1)}, f32[24,128]{1,0:T(8,128)S(1)}, u32[]{:S(2)}, u32[]{:S(2)}) collective-permute-start(f32[24,128]{1,0:T(8,128)S(1)} %get-tuple-element.10), channel_id=1, source_target_pairs={{0,497},{1,496},{16,1},{17,0},{32,17},{33,16},{48,33},{49,32},{64,... | collective-permute-start | bytes 36872 | tf_op jit(solution)/shard_map/ppermute | solution.py:346
  40.1 12.5 %copy-start.3 = (f32[64,64]{1,0:T(8,128)S(1)}, f32[64,64]{1,0:T(8,128)}, u32[]{:S(2)}) copy-start(f32[64,64]{1,0:T(8,128)} %constant.13.clone.down) | copy-start | bytes 49156
  40.1 12.5 %copy-start.4 = (f32[48,64]{1,0:T(8,128)S(1)}, f32[48,64]{1,0:T(8,128)}, u32[]{:S(2)}) copy-start(f32[48,64]{1,0:T(8,128)} %constant.14.clone.up) | copy-start | bytes 36868
  41.0 1.4 %collective-permute-start.7 = (f32[192,128]{1,0:T(8,128)S(1)}, f32[192,128]{1,0:T(8,128)S(1)}, u32[]{:S(2)}, u32[]{:S(2)}) collective-permute-start(f32[192,128]{1,0:T(8,128)S(1)} %get-tuple-element.14), channel_id=1, source_target_pairs={{240,224},{496,480},{241,225},{497,481},{242,226},{498,482},{243,2... | collective-permute-start | bytes 294920 | tf_op jit(solution)/shard_map/ppermute | solution.py:345
  41.7 0.7 %copy-start.5 = (s32[2,3]{1,0:T(2,128)S(1)}, s32[2,3]{1,0:T(2,128)}, u32[]{:S(2)}) copy-start(s32[2,3]{1,0:T(2,128)} %secondaries.1) | copy-start | bytes 76
  41.7 0.7 %collective-permute-start.6 = (f32[24,128]{1,0:T(8,128)S(1)}, f32[24,128]{1,0:T(8,128)S(1)}, u32[]{:S(2)}, u32[]{:S(2)}) collective-permute-start(f32[24,128]{1,0:T(8,128)S(1)} %get-tuple-element.13), channel_id=1, source_target_pairs={{240,225},{241,224},{496,481},{497,480},{242,227},{243,226},{498,4... | collective-permute-start | bytes 36872 | tf_op jit(solution)/shard_map/ppermute | solution.py:346
  42.4 10.2 %copy-start = (f32[128,256]{1,0:T(8,128)S(1)}, f32[128,256]{1,0:T(8,128)}, u32[]{:S(2)}) copy-start(f32[128,256]{1,0:T(8,128)} %constant.10.clone.forward) | copy-start | bytes 393220
  42.4 10.2 %copy-start.1 = (f32[128,256]{1,0:T(8,128)S(1)}, f32[128,256]{1,0:T(8,128)}, u32[]{:S(2)}) copy-start(f32[128,256]{1,0:T(8,128)} %constant.11.clone.spread) | copy-start | bytes 393220
  42.4 10.2 %copy-start.2 = (f32[128,256]{1,0:T(8,128)S(1)}, f32[128,256]{1,0:T(8,128)}, u32[]{:S(2)}) copy-start(f32[128,256]{1,0:T(8,128)} %constant.12.clone.inverse) | copy-start | bytes 393220
  43.2 8.2 %collective-permute-start.8 = (f32[80,128]{1,0:T(8,128)S(1)}, f32[80,128]{1,0:T(8,128)S(1)}, u32[]{:S(2)}, u32[]{:S(2)}) collective-permute-start(f32[80,128]{1,0:T(8,128)S(1)} %get-tuple-element.16), channel_id=1, source_target_pairs={{2,4},{4,2},{6,8},{8,6},{10,12},{12,10},{3,5},{5,3},{7,9},{9,7},{1... | collective-permute-start | bytes 122888 | tf_op jit(solution)/shard_map/ppermute | solution.py:371
  49.5 3.1 %collective-permute-start.9 = (f32[80,128]{1,0:T(8,128)S(1)}, f32[80,128]{1,0:T(8,128)S(1)}, u32[]{:S(2)}, u32[]{:S(2)}) collective-permute-start(f32[80,128]{1,0:T(8,128)S(1)} %get-tuple-element.17), channel_id=1, source_target_pairs={{0,2},{2,0},{4,6},{6,4},{8,10},{10,8},{12,14},{14,12},{1,3},{3,1},... | collective-permute-start | bytes 122888 | tf_op jit(solution)/shard_map/ppermute | solution.py:370

commit v3 on v2

--- a/solution.py
+++ b/solution.py
@@ -71,7 +71,7 @@
     return [spec(index) for index in range(cols // LANES)]
 
 
-def keep_kernel(source, target, arrived):
+def keep_kernel(secondaries, source, target, slots, arrived):
     copies = [
         pltpu.make_async_copy(
             source.at[:, :, :, pl.ds(tile * LANES, LANES)], target.at[tile], arrived.at[tile]
@@ -80,19 +80,28 @@
     ]
     for copy in copies:
         copy.start()
+    first = 2 * lax.axis_index("date")
+    dates = 2 * lax.axis_size("date")
+    for date in range(2):
+        for link in range(LINKS):
+            slot = (secondaries[date, link] - first + dates) % dates
+            slots[pl.ds(LINKS * date + link, 1), :] = jnp.full((1, LANES), slot, jnp.int32)
     for copy in copies:
         copy.wait()
 
 
-def kept(images):
+def kept(images, secondaries):
     tiles = images.shape[3] // LANES
     return pl.pallas_call(
         keep_kernel,
-        out_shape=pltpu.VMEM((tiles,) + images.shape[:3] + (LANES,), F32),
-        in_specs=[pl.BlockSpec(memory_space=pl.ANY)],
-        out_specs=vmem(),
+        out_shape=(
+            pltpu.VMEM((tiles,) + images.shape[:3] + (LANES,), F32),
+            pltpu.VMEM((8, LANES), jnp.int32),
+        ),
+        in_specs=[smem(), pl.BlockSpec(memory_space=pl.ANY)],
+        out_specs=(vmem(), vmem()),
         scratch_shapes=[pltpu.SemaphoreType.DMA((tiles,))],
-    )(images)
+    )(secondaries, images)
 
 
 def product(a, b):
@@ -134,8 +143,9 @@
             stage[pl.ds(n * half, half), lanes] = value
 
 
-def meet(stage, image, tiles, half, sent, side):
-    fill(stage, image, tiles, half, SENT, (2, 3))
+def meet(stage, image, tiles, half, wanted, *outs):
+    pairs, slots = wanted
+    fill(stage, image, tiles, half, pairs, slots)
     at_left = lax.axis_index("col") == 0
 
     def border(slot):
@@ -149,91 +159,169 @@
     values = [v for a, b in CANDIDATES for v in product(bordered[a], bordered[b])]
     values += [power(bordered[slot]) for slot in range(-2, 4)]
     block = lane_index((half, LANES)) >> 5
-    rows = pl.ds((2 * len(SENT) + 2) * half, half)
+    rows = pl.ds((2 * len(pairs) + len(slots)) * half, half)
     for tile in range(tiles):
         row = jnp.zeros((half, LANES), F32)
         for k, value in enumerate(values[4 * tile : 4 * tile + 4]):
             row = jnp.where(block == k, pltpu.roll(value, STRIP * k, 1) if k else value, row)
         stage[rows, pl.ds(tile * LANES, LANES)] = row
     means = split_dot(stage[...], looks_table(tiles * LANES))
-    end = (2 * len(SENT) + 2) * half
-    sent[...] = means[:end]
-    side[...] = means[end:]
-
-
-def meet_kernel(*refs):
-    own, (sent, side, stage) = refs[0], refs[-3:]
+    at = 0
+    for out in outs:
+        out[...] = means[at : at + out.shape[0]]
+        at += out.shape[0]
+
+
+ALL = (HELD + SENT, (0, 1, 2, 3))
+GOING = (SENT, (2, 3))
+
+
+def near_kernel(*refs):
+    own, (held, sent, side, stage, means) = refs[0], refs[-5:]
     tiles, half = own.shape[0], own.shape[3] // 2
-    before, before_wrap, after = [refs[1 + n * tiles : 1 + (n + 1) * tiles] for n in range(3)]
-    first = lax.axis_index("date") % RUN == 0
-    image = reader(own, {-1: (before, before_wrap, first), 1: (after, None, None)})
-    meet(stage, image, tiles, half, sent, side)
-
-
-def held_kernel(*refs):
-    own, (held, sent, side, stage, second) = refs[0], refs[-5:]
+    after, before = [refs[1 + n * tiles : 1 + (n + 1) * tiles] for n in range(2)]
+
+    @pl.when(lax.axis_index("date") % RUN < RUN - 1)
+    def _():
+        image = reader(own, {-1: (before, None, None), 1: (after, None, None)})
+        meet(stage, image, tiles, half, ALL, means, side)
+        share(means, half, held, sent)
+
+
+def share(means, half, held, sent):
+    kept, going = 2 * len(HELD) * half, 2 * len(SENT) * half
+    held[pl.ds(0, kept), :] = means[pl.ds(0, kept), :]
+    held[pl.ds(kept, 4 * half), :] = means[pl.ds(kept + going, 4 * half), :]
+    sent[pl.ds(0, going), :] = means[pl.ds(kept, going), :]
+    sent[pl.ds(going, 2 * half), :] = means[pl.ds(kept + going + 2 * half, 2 * half), :]
+
+
+def end_kernel(run, own, before, after, *refs):
+    count = 2 if run == 0 else 4
+    outs, (stage, mine, near, arrived) = refs[-4 - count : -4], refs[-4:]
     tiles, half = own.shape[0], own.shape[3] // 2
-    after, after_wrap, before = [refs[1 + n * tiles : 1 + (n + 1) * tiles] for n in range(3)]
-    last = lax.axis_index("date") % RUN == RUN - 1
-    fill(stage, reader(own, {1: (after, after_wrap, last)}), tiles, half, HELD, range(4))
-    held[...] = split_dot(stage[...], looks_table(tiles * LANES))
-
-    @pl.when(last)
+
+    @pl.when(lax.axis_index("date") % RUN == run)
     def _():
-        image = reader(own, {-1: (before, None, None), 1: (after_wrap, None, None)})
-        meet(second, image, tiles, half, sent, side)
-
-
-def on_tiles(kernel, counts, stages, own, *images, behind=()):
+        copies = [pltpu.make_async_copy(own, mine, arrived.at[0, 0])]
+        for n, source in enumerate((before, after)):
+            for tile in range(tiles):
+                lanes = pl.ds(tile * LANES, LANES)
+                copies.append(
+                    pltpu.make_async_copy(source.at[:, :, :, lanes], near.at[n, tile], arrived.at[n + 1, tile])
+                )
+        for copy in copies:
+            copy.start()
+        for copy in copies:
+            copy.wait()
+        blocks = [[near.at[n, tile] for tile in range(tiles)] for n in range(2)]
+        image = reader(mine, {-1: (blocks[0], None, None), 1: (blocks[1], None, None)})
+        if run == 0:
+            meet(stage, image, tiles, half, GOING, *outs)
+        else:
+            held, sent, side, means = outs
+            meet(stage, image, tiles, half, ALL, means, side)
+            share(means, half, held, sent)
+
+
+def planes_of(rows, *counts):
+    return tuple(jax.ShapeDtypeStruct((count * rows // 2, LANES), F32) for count in counts)
+
+
+STAYING, LEAVING = 2 * len(HELD) + 4, 2 * len(SENT) + 2
+BOTH = 2 * len(HELD + SENT) + 4
+
+
+def at_end(run, own, before, after, *behind):
+    rows, cols = after.shape[2:]
+    half, tiles = rows // 2, cols // LANES
+    outs = (LEAVING, 1) if run == 0 else (STAYING, LEAVING, 1)
+    total = LEAVING if run == 0 else BOTH
+    scratch = [
+        pltpu.VMEM(((total + 1) * half, cols), F32),
+        pltpu.VMEM(own.shape, F32),
+        pltpu.VMEM((2,) + own.shape, F32),
+        pltpu.SemaphoreType.DMA((3, tiles)),
+    ]
+    return call(
+        functools.partial(end_kernel, run),
+        planes_of(rows, *outs),
+        3 + len(behind),
+        ([] if run == 0 else [pltpu.VMEM((BOTH * half, LANES), F32)]) + scratch,
+        [pl.BlockSpec(memory_space=pl.ANY)] * (3 + len(behind)),
+    )(own, before, after, *behind)
+
+
+def near(own, *images):
     rows, cols = images[0].shape[2:]
     half = rows // 2
     whole = lambda shape: pl.BlockSpec(shape, lambda i: (0,) * len(shape))
+    outs = planes_of(rows, STAYING, LEAVING, 1)
     return pl.pallas_call(
-        kernel,
+        near_kernel,
         grid=(1,),
-        out_shape=tuple(jax.ShapeDtypeStruct((count * half, LANES), F32) for count in counts),
-        in_specs=[whole(own.shape)] + [spec for image in images for spec in tiled(image)]
-        + [whole(value.shape) for value in behind],
-        out_specs=tuple(whole((count * half, LANES)) for count in counts),
-        scratch_shapes=[pltpu.VMEM((count * half, cols), F32) for count in stages],
+        out_shape=outs,
+        in_specs=[whole(own.shape)] + [spec for image in images for spec in tiled(image)],
+        out_specs=tuple(whole(out.shape) for out in outs),
+        scratch_shapes=[pltpu.VMEM(((BOTH + 1) * half, cols), F32), pltpu.VMEM((BOTH * half, LANES), F32)],
         compiler_params=pltpu.CompilerParams(vmem_limit_bytes=32 * 1024 * 1024),
-    )(own, *[image for image in images for _ in range(cols // LANES)], *behind)
-
-
-def rims_kernel(secondaries, held, side, back, late_side, late_back, picked, chip, across, every):
+    )(own, *[image for image in images for _ in range(cols // LANES)])
+
+
+def rims_kernel(
+    slots,
+    held,
+    last_held,
+    side,
+    back,
+    low_side,
+    low_back,
+    high_side,
+    high_back,
+    picked,
+    chip,
+    across,
+    every,
+):
     at_left = lax.axis_index("col") == 0
     lanes = lane_index((KEEP, LANES))
-    place = jnp.where(at_left, RIGHT, 0)
-    margin = (lanes >= place) & (lanes < place + MARGIN)
-    late = lax.axis_index("date") % RUN == RUN - 2
-    columns = jnp.where(late, late_side[...], side[...])
+    edge = jnp.where(at_left, RIGHT, 0)
+    margin = (lanes >= edge) & (lanes < edge + MARGIN)
+    place = lax.axis_index("date") % RUN
+    from_low, from_high = place == RUN - 1, place == RUN - 2
+    columns = jnp.where(from_low, low_side[...], jnp.where(from_high, high_side[...], side[...]))
     held_at, back_at = 0, 0
     for n in range(PLANES):
         pair = n // 2
         from_back = pair in (3, 6, 7) or n >= PLANES - 2
         if from_back:
             rows = pl.ds(back_at * KEEP, KEEP)
-            value, back_at = jnp.where(late, late_back[rows, :], back[rows, :]), back_at + 1
+            value = jnp.where(from_high, high_back[rows, :], back[rows, :])
+            value, back_at = jnp.where(from_low, low_back[rows, :], value), back_at + 1
         else:
-            value, held_at = held[pl.ds(held_at * KEEP, KEEP), :], held_at + 1
+            rows = pl.ds(held_at * KEEP, KEEP)
+            value, held_at = jnp.where(from_low, last_held[rows, :], held[rows, :]), held_at + 1
         here = MARGIN + MARGIN * n
         right = pltpu.roll(columns, (RIGHT - here) % LANES, 1)
         left = pltpu.roll(columns, -here % LANES, 1)
         every[pl.ds(n * KEEP, KEEP), :] = jnp.where(margin, jnp.where(at_left, right, left), value)
 
-    first = 2 * lax.axis_index("date")
-    dates = 2 * lax.axis_size("date")
     even = lax.axis_index("row") % 2 == 0
-    starts = []
+    plane = lambda n: every[pl.ds(n * KEEP, KEEP), :]
+    chosen = []
     for date in range(2):
         for link in range(LINKS):
-            slot = (secondaries[date, link] - first + dates) % dates
-            pair = 3 * date + slot - 1
-            starts += [2 * pair, 2 * pair + 1, PLANES - 6 + slot]
-    starts += [PLANES - 6 + date for date in range(2)]
-    for n, start in enumerate(starts):
-        at = start * KEEP if isinstance(start, int) else pl.multiple_of(start * KEEP, 8)
-        value = every[pl.ds(at, KEEP), :]
+            slot = jnp.broadcast_to(slots[pl.ds(LINKS * date + link, 1), :], (KEEP, LANES))
+            triples = [
+                (plane(2 * (3 * date + n - 1)), plane(2 * (3 * date + n - 1) + 1), plane(PLANES - 6 + n))
+                for n in range(date + 1, date + 5)
+            ]
+            values = triples[0]
+            for n, triple in zip(range(date + 2, date + 5), triples[1:]):
+                values = [jnp.where(slot == n, v, w) for v, w in zip(triple, values)]
+            chosen += values
+    chosen += [plane(PLANES - 6 + date) for date in range(2)]
+    for n, value in enumerate(chosen):
         picked[pl.ds(n * KEEP, KEEP), :] = value
         top, bottom = value[:MARGIN], value[KEEP - MARGIN :]
         chip[pl.ds(MARGIN * n, MARGIN), :] = jnp.where(even, bottom, top)
@@ -348,24 +436,22 @@
     )
     after, before = along(images, inner(-1)), along(images, inner(1))
     after_wrap, before_wrap = along(images, outer(-1)), along(images, outer(1))
-    own = kept(images)
-    total = 2 * len(SENT) + 2
-    sent, side = on_tiles(meet_kernel, (total, 1), (total + 1,), own, before, before_wrap, after)
-    soon = [(d, (d - 1) % dates) for d in range(dates) if d % RUN < RUN - 1]
-    late = [(d, d - 1) for d in range(dates) if d % RUN == RUN - 1]
-    side, back = across(side, soon), along(sent, soon)
-    keeps = 2 * len(HELD) + 4
-    held, late_sent, late_side = on_tiles(
-        held_kernel, (keeps, total, 1), (keeps, total + 1), own, after, after_wrap, before, behind=(side, back)
-    )
-    late_side, late_back = across(late_side, late), along(late_sent, late)
+    own, slots = kept(images, secondaries)
+    step = lambda wanted: [(d, (d - 1) % dates) for d in range(dates) if wanted(d % RUN)]
+    middle, low, high = step(lambda n: 0 < n < RUN - 1), step(lambda n: n == 0), step(lambda n: n == RUN - 1)
+    held, sent, side = near(own, after, before)
+    side, back = across(side, middle), along(sent, middle)
+    sent, low_side = at_end(0, own, before_wrap, after, side, back, before)
+    low_side, low_back = across(low_side, low), along(sent, low)
+    last_held, sent, high_side = at_end(RUN - 1, own, before, after_wrap, low_side, low_back)
+    high_side, high_back = across(high_side, high), along(sent, high)
 
     planes = 3 * 2 * LINKS + 2
     rim = jax.ShapeDtypeStruct((planes * MARGIN, LANES), F32)
     every = pltpu.VMEM((PLANES * cells_down, LANES), F32)
     picked = jax.ShapeDtypeStruct((planes * cells_down, LANES), F32)
-    picked, chip, across = call(rims_kernel, (picked, rim, rim), 6, [every], [smem()] + [vmem()] * 5)(
-        secondaries, held, side, back, late_side, late_back
+    picked, chip, across = call(rims_kernel, (picked, rim, rim), 9, [every])(
+        slots, held, last_held, side, back, low_side, low_back, high_side, high_back
     )
     chip = lax.ppermute(chip, "row", [(i, i ^ 1) for i in range(count)])
     across = lax.ppermute(across, "row", [(i, ((i + 1) ^ 1) - 1) for i in range(1, count - 1)])

time: 56.2 us -> 51.3 us (0.913)
  waiting for transfers between devices: 13.1 us -> 6.8 us
  Pallas kernels: 6.93 us -> 7.96 us
    ppermute x6 -> x7, waiting for transfers between devices: 8.54 us -> 4.82 us  [body(): along = lambda value, pairs: lax.ppermute(value, 'date', pairs)]
    ppermute x2 -> x3, waiting for transfers between devices: 3.4 us -> 0.81 us  [body(): lax.ppermute(value, ('date', 'col'), [(2 * d + c, 2 * e + (c ^ 1)) for d,...]
    pallas_call x4 -> x5, Pallas kernels: 3.71 us -> 4.75 us  [the longest x1 1.88 us: kept(): pl.pallas_call(keep_kernel, out_shape=(pltpu.VMEM((tiles,) + images.shape...]
    ppermute x1, starting transfers between devices: 6.3 us -> 5.57 us  [body(): lax.ppermute(across, 'row', [(i, (i + 1 ^ 1) - 1) for i in range(1, count...]
    ppermute x2 -> x3, starting transfers between devices: 2.58 us -> 3.24 us  [body(): lax.ppermute(value, ('date', 'col'), [(2 * d + c, 2 * e + (c ^ 1)) for d,...]
    ppermute x6 -> x7, starting transfers between devices: 24.1 us -> 24.5 us  [body(): along = lambda value, pairs: lax.ppermute(value, 'date', pairs)]
  transfers between devices with their start and end apart: 10 -> 12, of which waited for: 3 -> 3; matrix products, arithmetic and copies ran while one was open for 0% -> 0% of each run, Pallas kernels for 4% -> 9%
where the time goes in v3:
time: 51.3 us; the launch traced here: 50.9 us
  starting transfers between devices  35.2 us (69%)
  Pallas kernels  7.96 us (16%)
  waiting for transfers between devices  6.8 us (13%)
  between operations  0.87 us (2%)
    ppermute x7, starting transfers between devices, body(): along = lambda value, pairs: lax.ppermute(value, 'date', pairs)  24.5 us
    ppermute x1, starting transfers between devices, body(): lax.ppermute(across, 'row', [(i, (i + 1 ^ 1) - 1) for i in range(1, count...  5.57 us
    ppermute x7, waiting for transfers between devices, body(): along = lambda value, pairs: lax.ppermute(value, 'date', pairs)  4.82 us
    ppermute x3, starting transfers between devices, body(): lax.ppermute(value, ('date', 'col'), [(2 * d + c, 2 * e + (c ^ 1)) for d,...  3.24 us
    pallas_call x1, Pallas kernels, body(): call(filter_kernel, (out, out), 8, [pltpu.VMEM((planes, PATCH, LANES), F3...  3.22 us
    ppermute x1, starting transfers between devices, body(): chip = lax.ppermute(chip, 'row', [(i, i ^ 1) for i in range(count)])  1.92 us
    pallas_call x1, Pallas kernels, kept(): pl.pallas_call(keep_kernel, out_shape=(pltpu.VMEM((tiles,) + images.shape...  1.88 us
    pallas_call x2, Pallas kernels, at_end(): call(functools.partial(end_kernel, run), planes_of(rows, *outs), 3 + len(...  1.36 us
  transfers between devices with their start and end apart: 12, of which 3 were waited for; matrix products, arithmetic and copies ran while one was open for 0% of the time, Pallas kernels for 9%

profile of v3, /device:TPU:1, one launch (start us, length us, event | category | flops | bytes accessed | tf_op | source)
XLA Modules:
  0.0 50.9 jit_solution(13649477996084546637)
XLA Ops:
  0.6 4.4 %collective-permute-start.1 = (f32[2,2,48,768]{3,2,1,0:T(8,128)}, f32[2,2,48,768]{3,2,1,0:T(8,128)S(1)}, u32[]{:S(2)}, u32[]{:S(2)}) collective-permute-start(f32[2,2,48,768]{3,2,1,0:T(8,128)} %source.1), channel_id=1, source_target_pairs={{0,16},{16,32},{32,48},{48,64},{64,80},{80,96},{96,112},{112,128},... | collective-permute-start | bytes 1769480 | tf_op jit(solution)/shard_map/ppermute | solution.py:433
  5.0 1.3 %collective-permute-start = (f32[2,2,48,768]{3,2,1,0:T(8,128)}, f32[2,2,48,768]{3,2,1,0:T(8,128)S(1)}, u32[]{:S(2)}, u32[]{:S(2)}) collective-permute-start(f32[2,2,48,768]{3,2,1,0:T(8,128)} %source.1), channel_id=1, source_target_pairs={{16,0},{32,16},{48,32},{64,48},{80,64},{96,80},{112,96},{128,112},... | collective-permute-start | bytes 1769480 | tf_op jit(solution)/shard_map/ppermute | solution.py:433
  6.3 1.3 %collective-permute-start.3 = (f32[2,2,48,768]{3,2,1,0:T(8,128)}, f32[2,2,48,768]{3,2,1,0:T(8,128)S(1)}, u32[]{:S(2)}, u32[]{:S(2)}) collective-permute-start(f32[2,2,48,768]{3,2,1,0:T(8,128)} %source.1), channel_id=1, source_target_pairs={{240,256},{496,0},{241,257},{497,1},{242,258},{498,2},{243,259},{4... | collective-permute-start | bytes 1769480 | tf_op jit(solution)/shard_map/ppermute | solution.py:433
  7.6 14.3 %collective-permute-start.2 = (f32[2,2,48,768]{3,2,1,0:T(8,128)}, f32[2,2,48,768]{3,2,1,0:T(8,128)S(1)}, u32[]{:S(2)}, u32[]{:S(2)}) collective-permute-start(f32[2,2,48,768]{3,2,1,0:T(8,128)} %source.1), channel_id=1, source_target_pairs={{0,496},{256,240},{1,497},{257,241},{2,498},{258,242},{3,499},{259... | collective-permute-start | bytes 1769480 | tf_op jit(solution)/shard_map/ppermute | solution.py:433
  21.9 1.9 %shard_map.86 = (f32[6,2,2,48,128]{4,3,2,1,0:T(8,128)S(1)}, s32[8,128]{1,0:T(8,128)S(1)}) custom-call(s32[2,3]{1,0:T(2,128)} %secondaries.1, f32[2,2,48,768]{3,2,1,0:T(8,128)} %source.1), custom_call_target="tpu_custom_call" | custom-call | tf_op jit(solution)/shard_map/pallas_call | solution.py:95
  23.8 0.0 collective-permute-done.1.refs_7_.refs_8_.refs_9_.refs_10_.refs_11_.refs_12_.refs_2_.before
  23.8 1.3 %shard_map.87 = (f32[336,128]{1,0:T(8,128)S(1)}, f32[192,128]{1,0:T(8,128)S(1)}, f32[24,128]{1,0:T(8,128)S(1)}) custom-call(f32[6,2,2,48,128]{4,3,2,1,0:T(8,128)S(1)} %get-tuple-element.16.refs_0_.own, f32[2,2,48,768]{3,2,1,0:T(8,128)S(1)} %collective-permute-done.refs_1_.refs_2_.refs_3_.refs_4_.refs_5_.refs_6_.after, ...), custom_call_target="tpu_custom_call" | custom-call | tf_op jit(solution)/shard_map/pallas_call | solution.py:260
  25.1 1.3 %collective-permute-start.5 = (f32[192,128]{1,0:T(8,128)S(1)}, f32[192,128]{1,0:T(8,128)S(1)}, u32[]{:S(2)}, u32[]{:S(2)}) collective-permute-start(f32[192,128]{1,0:T(8,128)S(1)} %get-tuple-element.19), channel_id=1, source_target_pairs={{16,0},{32,16},{48,32},{64,48},{80,64},{96,80},{112,96},{128,112},... | collective-permute-start | bytes 294920 | tf_op jit(solution)/shard_map/ppermute | solution.py:433
  26.4 1.3 %collective-permute-start.4 = (f32[24,128]{1,0:T(8,128)S(1)}, f32[24,128]{1,0:T(8,128)S(1)}, u32[]{:S(2)}, u32[]{:S(2)}) collective-permute-start(f32[24,128]{1,0:T(8,128)S(1)} %get-tuple-element.18), channel_id=1, source_target_pairs={{16,1},{17,0},{32,17},{33,16},{48,33},{49,32},{64,49},{65,48},{80,... | collective-permute-start | bytes 36872 | tf_op jit(solution)/shard_map/ppermute | solution.py:434
  27.7 4.8 %collective-permute-done.3.before = f32[2,2,48,768]{3,2,1,0:T(8,128)S(1)} collective-permute-done((f32[2,2,48,768]{3,2,1,0:T(8,128)}, f32[2,2,48,768]{3,2,1,0:T(8,128)S(1)}, u32[]{:S(2)}, u32[]{:S(2)}) %collective-permute-start.3) | collective-permute-done | bytes 589856 | tf_op jit(solution)/shard_map/ppermute | solution.py:433
  32.5 0.0 collective-permute-done.4.refs_0_.side
  32.5 0.0 collective-permute-done.5.refs_1_.back
  32.5 1.2 %shard_map.88 = (f32[192,128]{1,0:T(8,128)S(1)}, f32[24,128]{1,0:T(8,128)S(1)}) custom-call(f32[6,2,2,48,128]{4,3,2,1,0:T(8,128)S(1)} %get-tuple-element.16.refs_0_.own, f32[2,2,48,768]{3,2,1,0:T(8,128)S(1)} %collective-permute-done.3.before, f32[2,2,48,768]{3,2,1,0:T(8,128)S(1)} %collective-permute-done.refs_1_.refs_2_.refs_3_.refs_4_.refs_5_.refs_6_.after, ...), custom_call_target="tpu_custom_call" | custom-call | flops 1000000 | bytes 1000000 | tf_op jit(solution)/shard_map/pallas_call | solution.py:246
  33.7 1.3 %collective-permute-start.7 = (f32[192,128]{1,0:T(8,128)S(1)}, f32[192,128]{1,0:T(8,128)S(1)}, u32[]{:S(2)}, u32[]{:S(2)}) collective-permute-start(f32[192,128]{1,0:T(8,128)S(1)} %get-tuple-element.21), channel_id=1, source_target_pairs={{0,496},{256,240},{1,497},{257,241},{2,498},{258,242},{3,499},{259... | collective-permute-start | bytes 294920 | tf_op jit(solution)/shard_map/ppermute | solution.py:433
  35.1 1.3 %collective-permute-start.6 = (f32[24,128]{1,0:T(8,128)S(1)}, f32[24,128]{1,0:T(8,128)S(1)}, u32[]{:S(2)}, u32[]{:S(2)}) collective-permute-start(f32[24,128]{1,0:T(8,128)S(1)} %get-tuple-element.20), channel_id=1, source_target_pairs={{0,497},{1,496},{256,241},{257,240},{2,499},{3,498},{258,243},{259... | collective-permute-start | bytes 36872 | tf_op jit(solution)/shard_map/ppermute | solution.py:434
  36.3 0.0 collective-permute-done.2.after
  36.4 0.8 %collective-permute-done.6.refs_0_.low_side = f32[24,128]{1,0:T(8,128)S(1)} collective-permute-done((f32[24,128]{1,0:T(8,128)S(1)}, f32[24,128]{1,0:T(8,128)S(1)}, u32[]{:S(2)}, u32[]{:S(2)}) %collective-permute-start.6) | collective-permute-done | bytes 12320 | tf_op jit(solution)/shard_map/ppermute | solution.py:434
  37.2 0.0 collective-permute-done.7.refs_1_.low_back
  37.2 0.2 shard_map.89
  37.3 0.7 %collective-permute-start.9 = (f32[192,128]{1,0:T(8,128)S(1)}, f32[192,128]{1,0:T(8,128)S(1)}, u32[]{:S(2)}, u32[]{:S(2)}) collective-permute-start(f32[192,128]{1,0:T(8,128)S(1)} %get-tuple-element.24), channel_id=1, source_target_pairs={{240,224},{496,480},{241,225},{497,481},{242,226},{498,482},{243,2... | collective-permute-start | bytes 294920 | tf_op jit(solution)/shard_map/ppermute | solution.py:433
  38.0 0.7 %collective-permute-start.8 = (f32[24,128]{1,0:T(8,128)S(1)}, f32[24,128]{1,0:T(8,128)S(1)}, u32[]{:S(2)}, u32[]{:S(2)}) collective-permute-start(f32[24,128]{1,0:T(8,128)S(1)} %get-tuple-element.23), channel_id=1, source_target_pairs={{240,225},{241,224},{496,481},{497,480},{242,227},{243,226},{498,4... | collective-permute-start | bytes 36872 | tf_op jit(solution)/shard_map/ppermute | solution.py:434
  38.7 0.0 collective-permute-done.8.high_side
  38.7 0.0 copy-start
  38.7 0.0 copy-start.1
  38.7 0.0 copy-start.2
  38.7 0.0 copy-start.3
  38.8 0.0 copy-start.4
  38.8 0.2 shard_map.90
  39.0 5.6 %collective-permute-start.10 = (f32[80,128]{1,0:T(8,128)S(1)}, f32[80,128]{1,0:T(8,128)S(1)}, u32[]{:S(2)}, u32[]{:S(2)}) collective-permute-start(f32[80,128]{1,0:T(8,128)S(1)} %get-tuple-element.26), channel_id=1, source_target_pairs={{2,4},{4,2},{6,8},{8,6},{10,12},{12,10},{3,5},{5,3},{7,9},{9,7},{1... | collective-permute-start | bytes 122888 | tf_op jit(solution)/shard_map/ppermute | solution.py:457
  44.6 1.9 %collective-permute-start.11 = (f32[80,128]{1,0:T(8,128)S(1)}, f32[80,128]{1,0:T(8,128)S(1)}, u32[]{:S(2)}, u32[]{:S(2)}) collective-permute-start(f32[80,128]{1,0:T(8,128)S(1)} %get-tuple-element.27), channel_id=1, source_target_pairs={{0,2},{2,0},{4,6},{6,4},{8,10},{10,8},{12,14},{14,12},{1,3},{3,1},... | collective-permute-start | bytes 122888 | tf_op jit(solution)/shard_map/ppermute | solution.py:456
  46.5 1.2 %collective-permute-done.11.chip = f32[80,128]{1,0:T(8,128)S(1)} collective-permute-done((f32[80,128]{1,0:T(8,128)S(1)}, f32[80,128]{1,0:T(8,128)S(1)}, u32[]{:S(2)}, u32[]{:S(2)}) %collective-permute-start.11) | collective-permute-done | bytes 40992 | tf_op jit(solution)/shard_map/ppermute | solution.py:456
  47.7 3.2 %shard_map.91 = (f32[2,3,2,24,96]{4,3,2,1,0:T(8,128)}, f32[2,3,2,24,96]{4,3,2,1,0:T(8,128)}) custom-call(f32[480,128]{1,0:T(8,128)S(1)} %get-tuple-element.25.picked, f32[80,128]{1,0:T(8,128)S(1)} %collective-permute-done.10.across, f32[80,128]{1,0:T(8,128)S(1)} %collective-permute-done.11.chip, f32[128,256]{1,0:T(8,128)S(1)} %copy-done.2, ...), custom_call_target="tpu_custom_call" | custom-call | flops 1000000 | bytes 1000000 | tf_op jit(solution)/shard_map/pallas_call | solution.py:459
  (8 shorter events, 0.0 us)
Async XLA Ops:
  0.6 23.2 %collective-permute-start.1 = (f32[2,2,48,768]{3,2,1,0:T(8,128)}, f32[2,2,48,768]{3,2,1,0:T(8,128)S(1)}, u32[]{:S(2)}, u32[]{:S(2)}) collective-permute-start(f32[2,2,48,768]{3,2,1,0:T(8,128)} %source.1), channel_id=1, source_target_pairs={{0,16},{16,32},{32,48},{48,64},{64,80},{80,96},{96,112},{112,128},... | collective-permute-start | bytes 1769480 | tf_op jit(solution)/shard_map/ppermute | solution.py:433
  5.0 18.8 %collective-permute-start = (f32[2,2,48,768]{3,2,1,0:T(8,128)}, f32[2,2,48,768]{3,2,1,0:T(8,128)S(1)}, u32[]{:S(2)}, u32[]{:S(2)}) collective-permute-start(f32[2,2,48,768]{3,2,1,0:T(8,128)} %source.1), channel_id=1, source_target_pairs={{16,0},{32,16},{48,32},{64,48},{80,64},{96,80},{112,96},{128,112},... | collective-permute-start | bytes 1769480 | tf_op jit(solution)/shard_map/ppermute | solution.py:433
  6.3 26.2 %collective-permute-start.3 = (f32[2,2,48,768]{3,2,1,0:T(8,128)}, f32[2,2,48,768]{3,2,1,0:T(8,128)S(1)}, u32[]{:S(2)}, u32[]{:S(2)}) collective-permute-start(f32[2,2,48,768]{3,2,1,0:T(8,128)} %source.1), channel_id=1, source_target_pairs={{240,256},{496,0},{241,257},{497,1},{242,258},{498,2},{243,259},{4... | collective-permute-start | bytes 1769480 | tf_op jit(solution)/shard_map/ppermute | solution.py:433
  7.6 28.7 %collective-permute-start.2 = (f32[2,2,48,768]{3,2,1,0:T(8,128)}, f32[2,2,48,768]{3,2,1,0:T(8,128)S(1)}, u32[]{:S(2)}, u32[]{:S(2)}) collective-permute-start(f32[2,2,48,768]{3,2,1,0:T(8,128)} %source.1), channel_id=1, source_target_pairs={{0,496},{256,240},{1,497},{257,241},{2,498},{258,242},{3,499},{259... | collective-permute-start | bytes 1769480 | tf_op jit(solution)/shard_map/ppermute | solution.py:433
  25.1 7.4 %collective-permute-start.5 = (f32[192,128]{1,0:T(8,128)S(1)}, f32[192,128]{1,0:T(8,128)S(1)}, u32[]{:S(2)}, u32[]{:S(2)}) collective-permute-start(f32[192,128]{1,0:T(8,128)S(1)} %get-tuple-element.19), channel_id=1, source_target_pairs={{16,0},{32,16},{48,32},{64,48},{80,64},{96,80},{112,96},{128,112},... | collective-permute-start | bytes 294920 | tf_op jit(solution)/shard_map/ppermute | solution.py:433
  26.4 6.1 %collective-permute-start.4 = (f32[24,128]{1,0:T(8,128)S(1)}, f32[24,128]{1,0:T(8,128)S(1)}, u32[]{:S(2)}, u32[]{:S(2)}) collective-permute-start(f32[24,128]{1,0:T(8,128)S(1)} %get-tuple-element.18), channel_id=1, source_target_pairs={{16,1},{17,0},{32,17},{33,16},{48,33},{49,32},{64,49},{65,48},{80,... | collective-permute-start | bytes 36872 | tf_op jit(solution)/shard_map/ppermute | solution.py:434
  33.7 3.4 %collective-permute-start.7 = (f32[192,128]{1,0:T(8,128)S(1)}, f32[192,128]{1,0:T(8,128)S(1)}, u32[]{:S(2)}, u32[]{:S(2)}) collective-permute-start(f32[192,128]{1,0:T(8,128)S(1)} %get-tuple-element.21), channel_id=1, source_target_pairs={{0,496},{256,240},{1,497},{257,241},{2,498},{258,242},{3,499},{259... | collective-permute-start | bytes 294920 | tf_op jit(solution)/shard_map/ppermute | solution.py:433
  35.1 2.1 %collective-permute-start.6 = (f32[24,128]{1,0:T(8,128)S(1)}, f32[24,128]{1,0:T(8,128)S(1)}, u32[]{:S(2)}, u32[]{:S(2)}) collective-permute-start(f32[24,128]{1,0:T(8,128)S(1)} %get-tuple-element.20), channel_id=1, source_target_pairs={{0,497},{1,496},{256,241},{257,240},{2,499},{3,498},{258,243},{259... | collective-permute-start | bytes 36872 | tf_op jit(solution)/shard_map/ppermute | solution.py:434
  37.3 1.4 %collective-permute-start.9 = (f32[192,128]{1,0:T(8,128)S(1)}, f32[192,128]{1,0:T(8,128)S(1)}, u32[]{:S(2)}, u32[]{:S(2)}) collective-permute-start(f32[192,128]{1,0:T(8,128)S(1)} %get-tuple-element.24), channel_id=1, source_target_pairs={{240,224},{496,480},{241,225},{497,481},{242,226},{498,482},{243,2... | collective-permute-start | bytes 294920 | tf_op jit(solution)/shard_map/ppermute | solution.py:433
  38.0 0.7 %collective-permute-start.8 = (f32[24,128]{1,0:T(8,128)S(1)}, f32[24,128]{1,0:T(8,128)S(1)}, u32[]{:S(2)}, u32[]{:S(2)}) collective-permute-start(f32[24,128]{1,0:T(8,128)S(1)} %get-tuple-element.23), channel_id=1, source_target_pairs={{240,225},{241,224},{496,481},{497,480},{242,227},{243,226},{498,4... | collective-permute-start | bytes 36872 | tf_op jit(solution)/shard_map/ppermute | solution.py:434
  38.7 9.0 %copy-start = (f32[128,256]{1,0:T(8,128)S(1)}, f32[128,256]{1,0:T(8,128)}, u32[]{:S(2)}) copy-start(f32[128,256]{1,0:T(8,128)} %constant.12.clone.inverse) | copy-start | bytes 393220
  38.7 9.0 %copy-start.1 = (f32[128,256]{1,0:T(8,128)S(1)}, f32[128,256]{1,0:T(8,128)}, u32[]{:S(2)}) copy-start(f32[128,256]{1,0:T(8,128)} %constant.11.clone.spread) | copy-start | bytes 393220
  38.7 9.0 %copy-start.2 = (f32[128,256]{1,0:T(8,128)S(1)}, f32[128,256]{1,0:T(8,128)}, u32[]{:S(2)}) copy-start(f32[128,256]{1,0:T(8,128)} %constant.10.clone.forward) | copy-start | bytes 393220
  38.7 8.9 %copy-start.3 = (f32[64,64]{1,0:T(8,128)S(1)}, f32[64,64]{1,0:T(8,128)}, u32[]{:S(2)}) copy-start(f32[64,64]{1,0:T(8,128)} %constant.13.clone.down) | copy-start | bytes 49156
  38.8 8.9 %copy-start.4 = (f32[48,64]{1,0:T(8,128)S(1)}, f32[48,64]{1,0:T(8,128)}, u32[]{:S(2)}) copy-start(f32[48,64]{1,0:T(8,128)} %constant.14.clone.up) | copy-start | bytes 36868
  39.0 7.5 %collective-permute-start.10 = (f32[80,128]{1,0:T(8,128)S(1)}, f32[80,128]{1,0:T(8,128)S(1)}, u32[]{:S(2)}, u32[]{:S(2)}) collective-permute-start(f32[80,128]{1,0:T(8,128)S(1)} %get-tuple-element.26), channel_id=1, source_target_pairs={{2,4},{4,2},{6,8},{8,6},{10,12},{12,10},{3,5},{5,3},{7,9},{9,7},{1... | collective-permute-start | bytes 122888 | tf_op jit(solution)/shard_map/ppermute | solution.py:457
  44.6 3.1 %collective-permute-start.11 = (f32[80,128]{1,0:T(8,128)S(1)}, f32[80,128]{1,0:T(8,128)S(1)}, u32[]{:S(2)}, u32[]{:S(2)}) collective-permute-start(f32[80,128]{1,0:T(8,128)S(1)} %get-tuple-element.27), channel_id=1, source_target_pairs={{0,2},{2,0},{4,6},{6,4},{8,10},{10,8},{12,14},{14,12},{1,3},{3,1},... | collective-permute-start | bytes 122888 | tf_op jit(solution)/shard_map/ppermute | solution.py:456

commit v4 on v3

--- a/solution.py
+++ b/solution.py
@@ -217,7 +217,9 @@
         blocks = [[near.at[n, tile] for tile in range(tiles)] for n in range(2)]
         image = reader(mine, {-1: (blocks[0], None, None), 1: (blocks[1], None, None)})
         if run == 0:
-            meet(stage, image, tiles, half, GOING, *outs)
+            sent, side = outs
+            side[pl.ds(half, side.shape[0] - half), :] = jnp.zeros((side.shape[0] - half, LANES), F32)
+            meet(stage, image, tiles, half, GOING, sent, side.at[pl.ds(0, half), :])
         else:
             held, sent, side, means = outs
             meet(stage, image, tiles, half, ALL, means, side)
@@ -235,7 +237,7 @@
 def at_end(run, own, before, after, *behind):
     rows, cols = after.shape[2:]
     half, tiles = rows // 2, cols // LANES
-    outs = (LEAVING, 1) if run == 0 else (STAYING, LEAVING, 1)
+    outs = (LEAVING, 8) if run == 0 else (STAYING, LEAVING, 1)
     total = LEAVING if run == 0 else BOTH
     scratch = [
         pltpu.VMEM(((total + 1) * half, cols), F32),
@@ -268,14 +270,18 @@
     )(own, *[image for image in images for _ in range(cols // LANES)])
 
 
+def merge_kernel(side, back, low_side, low_back, new_side, new_back):
+    from_low = lax.axis_index("date") % RUN == RUN - 1
+    new_side[...] = jnp.where(from_low, low_side[pl.ds(0, side.shape[0]), :], side[...])
+    new_back[...] = jnp.where(from_low, low_back[...], back[...])
+
+
 def rims_kernel(
     slots,
     held,
     last_held,
     side,
     back,
-    low_side,
-    low_back,
     high_side,
     high_back,
     picked,
@@ -289,15 +295,14 @@
     margin = (lanes >= edge) & (lanes < edge + MARGIN)
     place = lax.axis_index("date") % RUN
     from_low, from_high = place == RUN - 1, place == RUN - 2
-    columns = jnp.where(from_low, low_side[...], jnp.where(from_high, high_side[...], side[...]))
+    columns = jnp.where(from_high, high_side[...], side[...])
     held_at, back_at = 0, 0
     for n in range(PLANES):
         pair = n // 2
         from_back = pair in (3, 6, 7) or n >= PLANES - 2
         if from_back:
             rows = pl.ds(back_at * KEEP, KEEP)
-            value = jnp.where(from_high, high_back[rows, :], back[rows, :])
-            value, back_at = jnp.where(from_low, low_back[rows, :], value), back_at + 1
+            value, back_at = jnp.where(from_high, high_back[rows, :], back[rows, :]), back_at + 1
         else:
             rows = pl.ds(held_at * KEEP, KEEP)
             value, held_at = jnp.where(from_low, last_held[rows, :], held[rows, :]), held_at + 1
@@ -352,11 +357,37 @@
     down = np.block([[cosine, sine], [-sine, cosine]])
     kept = slice(MARGIN, MARGIN + KEEP)
     up = np.block([[cosine[kept], -sine[kept]], [sine[kept], cosine[kept]]]) / PATCH
-    return [np.asarray(t, np.float32) for t in (forward, spread, inverse, down, up)]
-
-
-def exact_dot(a, b):
-    return jnp.dot(a, b, preferred_element_type=F32, precision=lax.Precision.HIGHEST)
+
+    def thrice(table, axis):
+        high = table.astype(np.float32).astype(BF16)
+        low = (table - high.astype(np.float64)).astype(np.float32).astype(BF16)
+        return np.concatenate([high, low, high], axis=axis)
+
+    twice = np.concatenate([spread, spread], axis=0).astype(np.float32).astype(BF16)
+    return [thrice(forward, 0), twice, thrice(inverse, 0), thrice(down, 1), thrice(up, 1)]
+
+
+def parts(values):
+    high = values.astype(BF16)
+    return high, (values - high.astype(F32)).astype(BF16)
+
+
+def narrow_dot(a, b):
+    return jnp.dot(a, b, preferred_element_type=F32)
+
+
+def right_dot(values, table):
+    high, low = parts(values)
+    return narrow_dot(jnp.concatenate([high, high, low], axis=1), table)
+
+
+def left_dot(table, values):
+    high, low = parts(values)
+    return narrow_dot(table, jnp.concatenate([high, high, low], axis=0))
+
+
+def sum_dot(values, table):
+    return narrow_dot(jnp.concatenate(parts(values), axis=1), table)
 
 
 def filter_kernel(picked, across, chip, forward, spread, inverse, down, up, filtered, coherent, pad):
@@ -384,7 +415,7 @@
     reals = jnp.concatenate([pad[3 * p] for p in range(pairs)], axis=0)
     imags = jnp.concatenate([pad[3 * p + 1] for p in range(pairs)], axis=0)
     size = pairs * PATCH
-    across_cols = exact_dot(jnp.concatenate([reals, imags], axis=0), forward[...])
+    across_cols = right_dot(jnp.concatenate([reals, imags], axis=0), forward[...])
     col_real = across_cols[:size, :LANES] - across_cols[size:, LANES:]
     col_imag = across_cols[size:, :LANES] + across_cols[:size, LANES:]
     rows_of = lambda v, p, count: v[p * count : (p + 1) * count]
@@ -395,28 +426,28 @@
         ],
         axis=1,
     )
-    spectrum = exact_dot(down[...], stacked)
+    spectrum = left_dot(down[...], stacked)
     real, imag = spectrum[:PATCH], spectrum[PATCH:]
     power = real * real + imag * imag
     lanes_of = lambda v, p: v[:, p * LANES : (p + 1) * LANES]
     tall = lambda v: jnp.concatenate([lanes_of(v, p) for p in range(pairs)], axis=0)
-    sums = exact_dot(tall(power), spread[...])
+    sums = sum_dot(tall(power), spread[...])
     weights = []
     for p in range(pairs):
         near = rows_of(sums, p, PATCH)[:, :LANES]
         level = jnp.sum(rows_of(sums, p, PATCH)[:, LANES:], axis=0, keepdims=True) * (1.0 / (PATCH * PATCH))
         smooth = (near + pltpu.roll(near, 1, 0) + pltpu.roll(near, PATCH - 1, 0)) * (1.0 / 9.0)
         weights.append(jnp.sqrt(jnp.sqrt(smooth + level + 1e-06)))
-    totals = exact_dot(jnp.concatenate(weights, axis=0), spread[:, LANES:])
+    totals = sum_dot(jnp.concatenate(weights, axis=0), spread[:, LANES:])
     scaled = []
     for p in range(pairs):
         total = jnp.sum(rows_of(totals, p, PATCH), axis=0, keepdims=True)
         scaled.append(weights[p] * ((PATCH * PATCH) / total))
     weight = jnp.concatenate(scaled, axis=1)
-    lifted = exact_dot(up[...], jnp.concatenate([real * weight, imag * weight], axis=0))
+    lifted = left_dot(up[...], jnp.concatenate([real * weight, imag * weight], axis=0))
     low, high = lifted[:KEEP], lifted[KEEP:]
     size = pairs * KEEP
-    result = exact_dot(jnp.concatenate([tall(low), tall(high)], axis=0), inverse[...])
+    result = right_dot(jnp.concatenate([tall(low), tall(high)], axis=0), inverse[...])
     out_real = result[:size, :LANES] - result[size:, LANES:]
     out_imag = result[size:, :LANES] + result[:size, LANES:]
     for p in range(pairs):
@@ -442,16 +473,18 @@
     held, sent, side = near(own, after, before)
     side, back = across(side, middle), along(sent, middle)
     sent, low_side = at_end(0, own, before_wrap, after, side, back, before)
+    formed = low_side
     low_side, low_back = across(low_side, low), along(sent, low)
-    last_held, sent, high_side = at_end(RUN - 1, own, before, after_wrap, low_side, low_back)
+    last_held, sent, high_side = at_end(RUN - 1, own, before, after_wrap, formed)
     high_side, high_back = across(high_side, high), along(sent, high)
+    side, back = call(merge_kernel, planes_of(rows, 1, LEAVING), 4)(side, back, low_side, low_back)
 
     planes = 3 * 2 * LINKS + 2
     rim = jax.ShapeDtypeStruct((planes * MARGIN, LANES), F32)
     every = pltpu.VMEM((PLANES * cells_down, LANES), F32)
     picked = jax.ShapeDtypeStruct((planes * cells_down, LANES), F32)
-    picked, chip, across = call(rims_kernel, (picked, rim, rim), 9, [every])(
-        slots, held, last_held, side, back, low_side, low_back, high_side, high_back
+    picked, chip, across = call(rims_kernel, (picked, rim, rim), 7, [every])(
+        slots, held, last_held, side, back, high_side, high_back
     )
     chip = lax.ppermute(chip, "row", [(i, i ^ 1) for i in range(count)])
     across = lax.ppermute(across, "row", [(i, ((i + 1) ^ 1) - 1) for i in range(1, count - 1)])

time: 51.3 us -> 49.2 us (0.959)
  Pallas kernels: 7.96 us -> 6.64 us
  waiting for transfers between devices: 6.8 us -> 6.06 us
    pallas_call x1, Pallas kernels: 3.22 us -> 1.85 us  [body(): call(filter_kernel, (out, out), 8, [pltpu.VMEM((planes, PATCH, LANES), F3...]
    ppermute x3, waiting for transfers between devices: 0.81 us -> 0.07 us  [body(): lax.ppermute(value, ('date', 'col'), [(2 * d + c, 2 * e + (c ^ 1)) for d,...]
where the time goes in v4:
time: 49.2 us; the launch traced here: 48.9 us
  starting transfers between devices  35.3 us (72%)
  Pallas kernels  6.64 us (13%)
  waiting for transfers between devices  6.06 us (12%)
  between operations  0.88 us (2%)
    ppermute x7, starting transfers between devices, body(): along = lambda value, pairs: lax.ppermute(value, 'date', pairs)  24.5 us
    ppermute x1, starting transfers between devices, body(): lax.ppermute(across, 'row', [(i, (i + 1 ^ 1) - 1) for i in range(1, count...  5.58 us
    ppermute x7, waiting for transfers between devices, body(): along = lambda value, pairs: lax.ppermute(value, 'date', pairs)  4.82 us
    ppermute x3, starting transfers between devices, body(): lax.ppermute(value, ('date', 'col'), [(2 * d + c, 2 * e + (c ^ 1)) for d,...  3.25 us
    ppermute x1, starting transfers between devices, body(): chip = lax.ppermute(chip, 'row', [(i, i ^ 1) for i in range(count)])  1.92 us
    pallas_call x1, Pallas kernels, kept(): pl.pallas_call(keep_kernel, out_shape=(pltpu.VMEM((tiles,) + images.shape...  1.88 us
    pallas_call x1, Pallas kernels, body(): call(filter_kernel, (out, out), 8, [pltpu.VMEM((planes, PATCH, LANES), F3...  1.85 us
    pallas_call x2, Pallas kernels, at_end(): call(functools.partial(end_kernel, run), planes_of(rows, *outs), 3 + len(...  1.38 us
  transfers between devices with their start and end apart: 12, of which 3 were waited for; matrix products, arithmetic and copies ran while one was open for 0% of the time, Pallas kernels for 9%

profile of v4, /device:TPU:1, one launch (start us, length us, event | category | flops | bytes accessed | tf_op | source)
XLA Modules:
  0.0 48.9 jit_solution(10287234740778394364)
XLA Ops:
  0.6 4.4 %collective-permute-start.1 = (f32[2,2,48,768]{3,2,1,0:T(8,128)}, f32[2,2,48,768]{3,2,1,0:T(8,128)S(1)}, u32[]{:S(2)}, u32[]{:S(2)}) collective-permute-start(f32[2,2,48,768]{3,2,1,0:T(8,128)} %source.1), channel_id=1, source_target_pairs={{0,16},{16,32},{32,48},{48,64},{64,80},{80,96},{96,112},{112,128},... | collective-permute-start | bytes 1769480 | tf_op jit(solution)/shard_map/ppermute | solution.py:464
  5.0 1.3 %collective-permute-start = (f32[2,2,48,768]{3,2,1,0:T(8,128)}, f32[2,2,48,768]{3,2,1,0:T(8,128)S(1)}, u32[]{:S(2)}, u32[]{:S(2)}) collective-permute-start(f32[2,2,48,768]{3,2,1,0:T(8,128)} %source.1), channel_id=1, source_target_pairs={{16,0},{32,16},{48,32},{64,48},{80,64},{96,80},{112,96},{128,112},... | collective-permute-start | bytes 1769480 | tf_op jit(solution)/shard_map/ppermute | solution.py:464
  6.3 1.3 %collective-permute-start.3 = (f32[2,2,48,768]{3,2,1,0:T(8,128)}, f32[2,2,48,768]{3,2,1,0:T(8,128)S(1)}, u32[]{:S(2)}, u32[]{:S(2)}) collective-permute-start(f32[2,2,48,768]{3,2,1,0:T(8,128)} %source.1), channel_id=1, source_target_pairs={{240,256},{496,0},{241,257},{497,1},{242,258},{498,2},{243,259},{4... | collective-permute-start | bytes 1769480 | tf_op jit(solution)/shard_map/ppermute | solution.py:464
  7.6 14.3 %collective-permute-start.2 = (f32[2,2,48,768]{3,2,1,0:T(8,128)}, f32[2,2,48,768]{3,2,1,0:T(8,128)S(1)}, u32[]{:S(2)}, u32[]{:S(2)}) collective-permute-start(f32[2,2,48,768]{3,2,1,0:T(8,128)} %source.1), channel_id=1, source_target_pairs={{0,496},{256,240},{1,497},{257,241},{2,498},{258,242},{3,499},{259... | collective-permute-start | bytes 1769480 | tf_op jit(solution)/shard_map/ppermute | solution.py:464
  21.9 1.9 %shard_map.86 = (f32[6,2,2,48,128]{4,3,2,1,0:T(8,128)S(1)}, s32[8,128]{1,0:T(8,128)S(1)}) custom-call(s32[2,3]{1,0:T(2,128)} %secondaries.1, f32[2,2,48,768]{3,2,1,0:T(8,128)} %source.1), custom_call_target="tpu_custom_call" | custom-call | tf_op jit(solution)/shard_map/pallas_call | solution.py:95
  23.8 0.0 collective-permute-done.1.refs_7_.refs_8_.refs_9_.refs_10_.refs_11_.refs_12_.refs_2_.before
  23.8 0.0 collective-permute-done.refs_1_.refs_2_.refs_3_.refs_4_.refs_5_.refs_6_.after
  23.8 1.3 %shard_map.87 = (f32[336,128]{1,0:T(8,128)S(1)}, f32[192,128]{1,0:T(8,128)S(1)}, f32[24,128]{1,0:T(8,128)S(1)}) custom-call(f32[6,2,2,48,128]{4,3,2,1,0:T(8,128)S(1)} %get-tuple-element.18.refs_0_.own, f32[2,2,48,768]{3,2,1,0:T(8,128)S(1)} %collective-permute-done.refs_1_.refs_2_.refs_3_.refs_4_.refs_5_.refs_6_.after, ...), custom_call_target="tpu_custom_call" | custom-call | tf_op jit(solution)/shard_map/pallas_call | solution.py:262
  25.1 1.3 %collective-permute-start.5 = (f32[192,128]{1,0:T(8,128)S(1)}, f32[192,128]{1,0:T(8,128)S(1)}, u32[]{:S(2)}, u32[]{:S(2)}) collective-permute-start(f32[192,128]{1,0:T(8,128)S(1)} %get-tuple-element.21), channel_id=1, source_target_pairs={{16,0},{32,16},{48,32},{64,48},{80,64},{96,80},{112,96},{128,112},... | collective-permute-start | bytes 294920 | tf_op jit(solution)/shard_map/ppermute | solution.py:464
  26.4 1.3 %collective-permute-start.4 = (f32[24,128]{1,0:T(8,128)S(1)}, f32[24,128]{1,0:T(8,128)S(1)}, u32[]{:S(2)}, u32[]{:S(2)}) collective-permute-start(f32[24,128]{1,0:T(8,128)S(1)} %get-tuple-element.20), channel_id=1, source_target_pairs={{16,1},{17,0},{32,17},{33,16},{48,33},{49,32},{64,49},{65,48},{80,... | collective-permute-start | bytes 36872 | tf_op jit(solution)/shard_map/ppermute | solution.py:465
  27.7 4.8 %collective-permute-done.3.before = f32[2,2,48,768]{3,2,1,0:T(8,128)S(1)} collective-permute-done((f32[2,2,48,768]{3,2,1,0:T(8,128)}, f32[2,2,48,768]{3,2,1,0:T(8,128)S(1)}, u32[]{:S(2)}, u32[]{:S(2)}) %collective-permute-start.3) | collective-permute-done | bytes 589856 | tf_op jit(solution)/shard_map/ppermute | solution.py:464
  32.5 0.0 collective-permute-done.4.refs_0_.side
  32.5 0.0 collective-permute-done.5.refs_1_.back
  32.5 1.2 %shard_map.88 = (f32[192,128]{1,0:T(8,128)S(1)}, f32[192,128]{1,0:T(8,128)S(1)}) custom-call(f32[6,2,2,48,128]{4,3,2,1,0:T(8,128)S(1)} %get-tuple-element.18.refs_0_.own, f32[2,2,48,768]{3,2,1,0:T(8,128)S(1)} %collective-permute-done.3.before, f32[2,2,48,768]{3,2,1,0:T(8,128)S(1)} %collective-permute-done.refs_1_.refs_2_.refs_3_.refs_4_.refs_5_.refs_6_.after, ...), custom_call_target="tpu_custom_call" | custom-call | flops 1000000 | bytes 1000000 | tf_op jit(solution)/shard_map/pallas_call | solution.py:248
  33.7 1.3 %collective-permute-start.7 = (f32[192,128]{1,0:T(8,128)S(1)}, f32[192,128]{1,0:T(8,128)S(1)}, u32[]{:S(2)}, u32[]{:S(2)}) collective-permute-start(f32[192,128]{1,0:T(8,128)S(1)} %get-tuple-element.24), channel_id=1, source_target_pairs={{0,496},{256,240},{1,497},{257,241},{2,498},{258,242},{3,499},{259... | collective-permute-start | bytes 294920 | tf_op jit(solution)/shard_map/ppermute | solution.py:464
  35.0 1.3 %collective-permute-start.6 = (f32[192,128]{1,0:T(8,128)S(1)}, f32[192,128]{1,0:T(8,128)S(1)}, u32[]{:S(2)}, u32[]{:S(2)}) collective-permute-start(f32[192,128]{1,0:T(8,128)S(1)} %get-tuple-element.22.refs_0_), channel_id=1, source_target_pairs={{0,497},{1,496},{256,241},{257,240},{2,499},{3,498},{258,243},{259... | collective-permute-start | bytes 294920 | tf_op jit(solution)/shard_map/ppermute | solution.py:465
  36.4 0.0 collective-permute-done.2.after
  36.4 0.2 shard_map.89
  36.6 0.7 %collective-permute-start.9 = (f32[192,128]{1,0:T(8,128)S(1)}, f32[192,128]{1,0:T(8,128)S(1)}, u32[]{:S(2)}, u32[]{:S(2)}) collective-permute-start(f32[192,128]{1,0:T(8,128)S(1)} %get-tuple-element.28), channel_id=1, source_target_pairs={{240,224},{496,480},{241,225},{497,481},{242,226},{498,482},{243,2... | collective-permute-start | bytes 294920 | tf_op jit(solution)/shard_map/ppermute | solution.py:464
  37.2 0.7 %collective-permute-start.8 = (f32[24,128]{1,0:T(8,128)S(1)}, f32[24,128]{1,0:T(8,128)S(1)}, u32[]{:S(2)}, u32[]{:S(2)}) collective-permute-start(f32[24,128]{1,0:T(8,128)S(1)} %get-tuple-element.27), channel_id=1, source_target_pairs={{240,225},{241,224},{496,481},{497,480},{242,227},{243,226},{498,4... | collective-permute-start | bytes 36872 | tf_op jit(solution)/shard_map/ppermute | solution.py:465
  37.9 0.0 collective-permute-done.7.low_back
  37.9 0.1 collective-permute-done.6.low_side
  38.0 0.0 collective-permute-done.9.high_back
  38.0 0.0 copy-start
  38.0 0.0 copy-start.1
  38.0 0.0 copy-start.2
  38.1 0.0 copy-start.3
  38.1 0.2 shard_map.91
  38.3 5.6 %collective-permute-start.10 = (f32[80,128]{1,0:T(8,128)S(1)}, f32[80,128]{1,0:T(8,128)S(1)}, u32[]{:S(2)}, u32[]{:S(2)}) collective-permute-start(f32[80,128]{1,0:T(8,128)S(1)} %get-tuple-element.30), channel_id=1, source_target_pairs={{2,4},{4,2},{6,8},{8,6},{10,12},{12,10},{3,5},{5,3},{7,9},{9,7},{1... | collective-permute-start | bytes 122888 | tf_op jit(solution)/shard_map/ppermute | solution.py:490
  43.9 1.9 %collective-permute-start.11 = (f32[80,128]{1,0:T(8,128)S(1)}, f32[80,128]{1,0:T(8,128)S(1)}, u32[]{:S(2)}, u32[]{:S(2)}) collective-permute-start(f32[80,128]{1,0:T(8,128)S(1)} %get-tuple-element.31), channel_id=1, source_target_pairs={{0,2},{2,0},{4,6},{6,4},{8,10},{10,8},{12,14},{14,12},{1,3},{3,1},... | collective-permute-start | bytes 122888 | tf_op jit(solution)/shard_map/ppermute | solution.py:489
  45.8 1.2 %collective-permute-done.11.chip = f32[80,128]{1,0:T(8,128)S(1)} collective-permute-done((f32[80,128]{1,0:T(8,128)S(1)}, f32[80,128]{1,0:T(8,128)S(1)}, u32[]{:S(2)}, u32[]{:S(2)}) %collective-permute-start.11) | collective-permute-done | bytes 40992 | tf_op jit(solution)/shard_map/ppermute | solution.py:489
  47.0 1.9 %shard_map.92 = (f32[2,3,2,24,96]{4,3,2,1,0:T(8,128)}, f32[2,3,2,24,96]{4,3,2,1,0:T(8,128)}) custom-call(f32[480,128]{1,0:T(8,128)S(1)} %get-tuple-element.29.picked, f32[80,128]{1,0:T(8,128)S(1)} %collective-permute-done.10.across, f32[80,128]{1,0:T(8,128)S(1)} %collective-permute-done.11.chip, bf16[384,256]{1,0:T(8,128)(2,1)S(1)} %copy-done.1, ...), custom_call_target="tpu_custom_call" | custom-call | flops 1000000 | bytes 1000000 | tf_op jit(solution)/shard_map/pallas_call | solution.py:492
  (9 shorter events, 0.0 us)
Async XLA Ops:
  0.6 23.2 %collective-permute-start.1 = (f32[2,2,48,768]{3,2,1,0:T(8,128)}, f32[2,2,48,768]{3,2,1,0:T(8,128)S(1)}, u32[]{:S(2)}, u32[]{:S(2)}) collective-permute-start(f32[2,2,48,768]{3,2,1,0:T(8,128)} %source.1), channel_id=1, source_target_pairs={{0,16},{16,32},{32,48},{48,64},{64,80},{80,96},{96,112},{112,128},... | collective-permute-start | bytes 1769480 | tf_op jit(solution)/shard_map/ppermute | solution.py:464
  5.0 18.8 %collective-permute-start = (f32[2,2,48,768]{3,2,1,0:T(8,128)}, f32[2,2,48,768]{3,2,1,0:T(8,128)S(1)}, u32[]{:S(2)}, u32[]{:S(2)}) collective-permute-start(f32[2,2,48,768]{3,2,1,0:T(8,128)} %source.1), channel_id=1, source_target_pairs={{16,0},{32,16},{48,32},{64,48},{80,64},{96,80},{112,96},{128,112},... | collective-permute-start | bytes 1769480 | tf_op jit(solution)/shard_map/ppermute | solution.py:464
  6.3 26.2 %collective-permute-start.3 = (f32[2,2,48,768]{3,2,1,0:T(8,128)}, f32[2,2,48,768]{3,2,1,0:T(8,128)S(1)}, u32[]{:S(2)}, u32[]{:S(2)}) collective-permute-start(f32[2,2,48,768]{3,2,1,0:T(8,128)} %source.1), channel_id=1, source_target_pairs={{240,256},{496,0},{241,257},{497,1},{242,258},{498,2},{243,259},{4... | collective-permute-start | bytes 1769480 | tf_op jit(solution)/shard_map/ppermute | solution.py:464
  7.6 28.7 %collective-permute-start.2 = (f32[2,2,48,768]{3,2,1,0:T(8,128)}, f32[2,2,48,768]{3,2,1,0:T(8,128)S(1)}, u32[]{:S(2)}, u32[]{:S(2)}) collective-permute-start(f32[2,2,48,768]{3,2,1,0:T(8,128)} %source.1), channel_id=1, source_target_pairs={{0,496},{256,240},{1,497},{257,241},{2,498},{258,242},{3,499},{259... | collective-permute-start | bytes 1769480 | tf_op jit(solution)/shard_map/ppermute | solution.py:464
  25.1 7.4 %collective-permute-start.5 = (f32[192,128]{1,0:T(8,128)S(1)}, f32[192,128]{1,0:T(8,128)S(1)}, u32[]{:S(2)}, u32[]{:S(2)}) collective-permute-start(f32[192,128]{1,0:T(8,128)S(1)} %get-tuple-element.21), channel_id=1, source_target_pairs={{16,0},{32,16},{48,32},{64,48},{80,64},{96,80},{112,96},{128,112},... | collective-permute-start | bytes 294920 | tf_op jit(solution)/shard_map/ppermute | solution.py:464
  26.4 6.1 %collective-permute-start.4 = (f32[24,128]{1,0:T(8,128)S(1)}, f32[24,128]{1,0:T(8,128)S(1)}, u32[]{:S(2)}, u32[]{:S(2)}) collective-permute-start(f32[24,128]{1,0:T(8,128)S(1)} %get-tuple-element.20), channel_id=1, source_target_pairs={{16,1},{17,0},{32,17},{33,16},{48,33},{49,32},{64,49},{65,48},{80,... | collective-permute-start | bytes 36872 | tf_op jit(solution)/shard_map/ppermute | solution.py:465
  33.7 4.2 %collective-permute-start.7 = (f32[192,128]{1,0:T(8,128)S(1)}, f32[192,128]{1,0:T(8,128)S(1)}, u32[]{:S(2)}, u32[]{:S(2)}) collective-permute-start(f32[192,128]{1,0:T(8,128)S(1)} %get-tuple-element.24), channel_id=1, source_target_pairs={{0,496},{256,240},{1,497},{257,241},{2,498},{258,242},{3,499},{259... | collective-permute-start | bytes 294920 | tf_op jit(solution)/shard_map/ppermute | solution.py:464
  35.0 2.9 %collective-permute-start.6 = (f32[192,128]{1,0:T(8,128)S(1)}, f32[192,128]{1,0:T(8,128)S(1)}, u32[]{:S(2)}, u32[]{:S(2)}) collective-permute-start(f32[192,128]{1,0:T(8,128)S(1)} %get-tuple-element.22.refs_0_), channel_id=1, source_target_pairs={{0,497},{1,496},{256,241},{257,240},{2,499},{3,498},{258,243},{259... | collective-permute-start | bytes 294920 | tf_op jit(solution)/shard_map/ppermute | solution.py:465
  36.6 1.5 %collective-permute-start.9 = (f32[192,128]{1,0:T(8,128)S(1)}, f32[192,128]{1,0:T(8,128)S(1)}, u32[]{:S(2)}, u32[]{:S(2)}) collective-permute-start(f32[192,128]{1,0:T(8,128)S(1)} %get-tuple-element.28), channel_id=1, source_target_pairs={{240,224},{496,480},{241,225},{497,481},{242,226},{498,482},{243,2... | collective-permute-start | bytes 294920 | tf_op jit(solution)/shard_map/ppermute | solution.py:464
  37.2 0.8 %collective-permute-start.8 = (f32[24,128]{1,0:T(8,128)S(1)}, f32[24,128]{1,0:T(8,128)S(1)}, u32[]{:S(2)}, u32[]{:S(2)}) collective-permute-start(f32[24,128]{1,0:T(8,128)S(1)} %get-tuple-element.27), channel_id=1, source_target_pairs={{240,225},{241,224},{496,481},{497,480},{242,227},{243,226},{498,4... | collective-permute-start | bytes 36872 | tf_op jit(solution)/shard_map/ppermute | solution.py:465
  38.0 9.0 %copy-start.4 = (bf16[48,192]{1,0:T(8,128)(2,1)S(1)}, bf16[48,192]{1,0:T(8,128)(2,1)}, u32[]{:S(2)}) copy-start(bf16[48,192]{1,0:T(8,128)(2,1)} %constant.14.clone.up) | copy-start | bytes 55300
  38.0 9.0 %copy-start = (bf16[384,256]{1,0:T(8,128)(2,1)S(1)}, bf16[384,256]{1,0:T(8,128)(2,1)}, u32[]{:S(2)}) copy-start(bf16[384,256]{1,0:T(8,128)(2,1)} %constant.12.clone.inverse) | copy-start | bytes 589828
  38.0 9.0 %copy-start.1 = (bf16[384,256]{1,0:T(8,128)(2,1)S(1)}, bf16[384,256]{1,0:T(8,128)(2,1)}, u32[]{:S(2)}) copy-start(bf16[384,256]{1,0:T(8,128)(2,1)} %constant.10.clone.forward) | copy-start | bytes 589828
  38.0 8.9 %copy-start.2 = (bf16[256,256]{1,0:T(8,128)(2,1)S(1)}, bf16[256,256]{1,0:T(8,128)(2,1)}, u32[]{:S(2)}) copy-start(bf16[256,256]{1,0:T(8,128)(2,1)} %constant.11.clone.spread) | copy-start | bytes 393220
  38.1 8.9 %copy-start.3 = (bf16[64,192]{1,0:T(8,128)(2,1)S(1)}, bf16[64,192]{1,0:T(8,128)(2,1)}, u32[]{:S(2)}) copy-start(bf16[64,192]{1,0:T(8,128)(2,1)} %constant.13.clone.down) | copy-start | bytes 73732
  38.3 7.5 %collective-permute-start.10 = (f32[80,128]{1,0:T(8,128)S(1)}, f32[80,128]{1,0:T(8,128)S(1)}, u32[]{:S(2)}, u32[]{:S(2)}) collective-permute-start(f32[80,128]{1,0:T(8,128)S(1)} %get-tuple-element.30), channel_id=1, source_target_pairs={{2,4},{4,2},{6,8},{8,6},{10,12},{12,10},{3,5},{5,3},{7,9},{9,7},{1... | collective-permute-start | bytes 122888 | tf_op jit(solution)/shard_map/ppermute | solution.py:490
  43.9 3.1 %collective-permute-start.11 = (f32[80,128]{1,0:T(8,128)S(1)}, f32[80,128]{1,0:T(8,128)S(1)}, u32[]{:S(2)}, u32[]{:S(2)}) collective-permute-start(f32[80,128]{1,0:T(8,128)S(1)} %get-tuple-element.31), channel_id=1, source_target_pairs={{0,2},{2,0},{4,6},{6,4},{8,10},{10,8},{12,14},{14,12},{1,3},{3,1},... | collective-permute-start | bytes 122888 | tf_op jit(solution)/shard_map/ppermute | solution.py:489

commit v5 on v4

--- a/solution.py
+++ b/solution.py
@@ -179,7 +179,7 @@
 def near_kernel(*refs):
     own, (held, sent, side, stage, means) = refs[0], refs[-5:]
     tiles, half = own.shape[0], own.shape[3] // 2
-    after, before = [refs[1 + n * tiles : 1 + (n + 1) * tiles] for n in range(2)]
+    before, after = [refs[1 + n * tiles : 1 + (n + 1) * tiles] for n in range(2)]
 
     @pl.when(lax.axis_index("date") % RUN < RUN - 1)
     def _():
@@ -268,6 +268,11 @@
         scratch_shapes=[pltpu.VMEM(((BOTH + 1) * half, cols), F32), pltpu.VMEM((BOTH * half, LANES), F32)],
         compiler_params=pltpu.CompilerParams(vmem_limit_bytes=32 * 1024 * 1024),
     )(own, *[image for image in images for _ in range(cols // LANES)])
+
+
+def arrived_kernel(side, back, new_side, new_back):
+    new_side[...] = side[pl.ds(0, new_side.shape[0]), :]
+    new_back[...] = back[...]
 
 
 def merge_kernel(side, back, low_side, low_back, new_side, new_back):
@@ -465,18 +470,21 @@
     across = lambda value, pairs: lax.ppermute(
         value, ("date", "col"), [(2 * d + c, 2 * e + (c ^ 1)) for d, e in pairs for c in range(2)]
     )
-    after, before = along(images, inner(-1)), along(images, inner(1))
+    up_from = lambda wanted: [(d, d + 1) for d in range(dates) if wanted(d % RUN)]
+    after, before = along(images, inner(-1)), along(images, up_from(lambda n: n < RUN - 2))
     after_wrap, before_wrap = along(images, outer(-1)), along(images, outer(1))
+    before_last = along(images, up_from(lambda n: n == RUN - 2))
     own, slots = kept(images, secondaries)
     step = lambda wanted: [(d, (d - 1) % dates) for d in range(dates) if wanted(d % RUN)]
     middle, low, high = step(lambda n: 0 < n < RUN - 1), step(lambda n: n == 0), step(lambda n: n == RUN - 1)
-    held, sent, side = near(own, after, before)
+    held, sent, side = near(own, before, after)
     side, back = across(side, middle), along(sent, middle)
-    sent, low_side = at_end(0, own, before_wrap, after, side, back, before)
+    sent, low_side = at_end(0, own, before_wrap, after, side, before)
     formed = low_side
     low_side, low_back = across(low_side, low), along(sent, low)
-    last_held, sent, high_side = at_end(RUN - 1, own, before, after_wrap, formed)
+    last_held, sent, high_side = at_end(RUN - 1, own, before_last, after_wrap, formed)
     high_side, high_back = across(high_side, high), along(sent, high)
+    side, back = call(arrived_kernel, planes_of(rows, 1, LEAVING), 2)(side, back)
     side, back = call(merge_kernel, planes_of(rows, 1, LEAVING), 4)(side, back, low_side, low_back)
 
     planes = 3 * 2 * LINKS + 2

time: 49.2 us -> 48.5 us (0.986)
  starting transfers between devices: 35.3 us -> 34.3 us
    ppermute x1, starting transfers between devices: 5.58 us -> 4.65 us  [body(): lax.ppermute(across, 'row', [(i, (i + 1 ^ 1) - 1) for i in range(1, count...]
    ppermute x7 -> x8, waiting for transfers between devices: 4.82 us -> 5.05 us  [body(): along = lambda value, pairs: lax.ppermute(value, 'date', pairs)]
    ppermute x7 -> x8, starting transfers between devices: 24.5 us -> 24.4 us  [body(): along = lambda value, pairs: lax.ppermute(value, 'date', pairs)]
  transfers between devices with their start and end apart: 12 -> 13, of which waited for: 3 -> 3; matrix products, arithmetic and copies ran while one was open for 0% -> 0% of each run, Pallas kernels for 9% -> 10%
where the time goes in v5:
time: 48.5 us; the launch traced here: 48.1 us
  starting transfers between devices  34.3 us (71%)
  Pallas kernels  6.64 us (14%)
  waiting for transfers between devices  6.24 us (13%)
  between operations  0.91 us (2%)
    ppermute x8, starting transfers between devices, body(): along = lambda value, pairs: lax.ppermute(value, 'date', pairs)  24.4 us
    ppermute x8, waiting for transfers between devices, body(): along = lambda value, pairs: lax.ppermute(value, 'date', pairs)  5.05 us
    ppermute x1, starting transfers between devices, body(): lax.ppermute(across, 'row', [(i, (i + 1 ^ 1) - 1) for i in range(1, count...  4.65 us
    ppermute x3, starting transfers between devices, body(): lax.ppermute(value, ('date', 'col'), [(2 * d + c, 2 * e + (c ^ 1)) for d,...  3.25 us
    ppermute x1, starting transfers between devices, body(): chip = lax.ppermute(chip, 'row', [(i, i ^ 1) for i in range(count)])  1.92 us
    pallas_call x1, Pallas kernels, kept(): pl.pallas_call(keep_kernel, out_shape=(pltpu.VMEM((tiles,) + images.shape...  1.88 us
    pallas_call x1, Pallas kernels, body(): call(filter_kernel, (out, out), 8, [pltpu.VMEM((planes, PATCH, LANES), F3...  1.85 us
    pallas_call x2, Pallas kernels, at_end(): call(functools.partial(end_kernel, run), planes_of(rows, *outs), 3 + len(...  1.38 us
  transfers between devices with their start and end apart: 13, of which 3 were waited for; matrix products, arithmetic and copies ran while one was open for 0% of the time, Pallas kernels for 10%

profile of v5, /device:TPU:1, one launch (start us, length us, event | category | flops | bytes accessed | tf_op | source)
XLA Modules:
  0.0 48.1 jit_solution(7291096696468009900)
XLA Ops:
  0.6 4.4 %collective-permute-start = (f32[2,2,48,768]{3,2,1,0:T(8,128)}, f32[2,2,48,768]{3,2,1,0:T(8,128)S(1)}, u32[]{:S(2)}, u32[]{:S(2)}) collective-permute-start(f32[2,2,48,768]{3,2,1,0:T(8,128)} %source.1), channel_id=1, source_target_pairs={{0,16},{16,32},{32,48},{48,64},{64,80},{80,96},{96,112},{112,128},... | collective-permute-start | bytes 1769480 | tf_op jit(solution)/shard_map/ppermute | solution.py:469
  5.0 1.3 %collective-permute-start.1 = (f32[2,2,48,768]{3,2,1,0:T(8,128)}, f32[2,2,48,768]{3,2,1,0:T(8,128)S(1)}, u32[]{:S(2)}, u32[]{:S(2)}) collective-permute-start(f32[2,2,48,768]{3,2,1,0:T(8,128)} %source.1), channel_id=1, source_target_pairs={{16,0},{32,16},{48,32},{64,48},{80,64},{96,80},{112,96},{128,112},... | collective-permute-start | bytes 1769480 | tf_op jit(solution)/shard_map/ppermute | solution.py:469
  6.3 1.3 %collective-permute-start.4 = (f32[2,2,48,768]{3,2,1,0:T(8,128)}, f32[2,2,48,768]{3,2,1,0:T(8,128)S(1)}, u32[]{:S(2)}, u32[]{:S(2)}) collective-permute-start(f32[2,2,48,768]{3,2,1,0:T(8,128)} %source.1), channel_id=1, source_target_pairs={{240,256},{496,0},{241,257},{497,1},{242,258},{498,2},{243,259},{4... | collective-permute-start | bytes 1769480 | tf_op jit(solution)/shard_map/ppermute | solution.py:469
  7.6 0.7 %collective-permute-start.2 = (f32[2,2,48,768]{3,2,1,0:T(8,128)}, f32[2,2,48,768]{3,2,1,0:T(8,128)S(1)}, u32[]{:S(2)}, u32[]{:S(2)}) collective-permute-start(f32[2,2,48,768]{3,2,1,0:T(8,128)} %source.1), channel_id=1, source_target_pairs={{224,240},{480,496},{225,241},{481,497},{226,242},{482,498},{227,2... | collective-permute-start | bytes 1769480 | tf_op jit(solution)/shard_map/ppermute | solution.py:469
  8.4 13.5 %collective-permute-start.3 = (f32[2,2,48,768]{3,2,1,0:T(8,128)}, f32[2,2,48,768]{3,2,1,0:T(8,128)S(1)}, u32[]{:S(2)}, u32[]{:S(2)}) collective-permute-start(f32[2,2,48,768]{3,2,1,0:T(8,128)} %source.1), channel_id=1, source_target_pairs={{0,496},{256,240},{1,497},{257,241},{2,498},{258,242},{3,499},{259... | collective-permute-start | bytes 1769480 | tf_op jit(solution)/shard_map/ppermute | solution.py:469
  21.9 1.9 %shard_map.86 = (f32[6,2,2,48,128]{4,3,2,1,0:T(8,128)S(1)}, s32[8,128]{1,0:T(8,128)S(1)}) custom-call(s32[2,3]{1,0:T(2,128)} %secondaries.1, f32[2,2,48,768]{3,2,1,0:T(8,128)} %source.1), custom_call_target="tpu_custom_call" | custom-call | tf_op jit(solution)/shard_map/pallas_call | solution.py:95
  23.8 0.0 collective-permute-done.1.refs_7_.refs_8_.refs_9_.refs_10_.refs_11_.refs_12_.after
  23.8 1.3 %shard_map.87 = (f32[336,128]{1,0:T(8,128)S(1)}, f32[192,128]{1,0:T(8,128)S(1)}, f32[24,128]{1,0:T(8,128)S(1)}) custom-call(f32[6,2,2,48,128]{4,3,2,1,0:T(8,128)S(1)} %get-tuple-element.20.refs_0_.own, f32[2,2,48,768]{3,2,1,0:T(8,128)S(1)} %collective-permute-done.refs_1_.refs_2_.refs_3_.refs_4_.refs_5_.refs_6_, ...), custom_call_target="tpu_custom_call" | custom-call | tf_op jit(solution)/shard_map/pallas_call | solution.py:262
  25.1 1.3 %collective-permute-start.5 = (f32[24,128]{1,0:T(8,128)S(1)}, f32[24,128]{1,0:T(8,128)S(1)}, u32[]{:S(2)}, u32[]{:S(2)}) collective-permute-start(f32[24,128]{1,0:T(8,128)S(1)} %get-tuple-element.22), channel_id=1, source_target_pairs={{16,1},{17,0},{32,17},{33,16},{48,33},{49,32},{64,49},{65,48},{80,... | collective-permute-start | bytes 36872 | tf_op jit(solution)/shard_map/ppermute | solution.py:470
  26.4 1.3 %collective-permute-start.6 = (f32[192,128]{1,0:T(8,128)S(1)}, f32[192,128]{1,0:T(8,128)S(1)}, u32[]{:S(2)}, u32[]{:S(2)}) collective-permute-start(f32[192,128]{1,0:T(8,128)S(1)} %get-tuple-element.25), channel_id=1, source_target_pairs={{16,0},{32,16},{48,32},{64,48},{80,64},{96,80},{112,96},{128,112},... | collective-permute-start | bytes 294920 | tf_op jit(solution)/shard_map/ppermute | solution.py:469
  27.7 3.8 %collective-permute-done.4.before = f32[2,2,48,768]{3,2,1,0:T(8,128)S(1)} collective-permute-done((f32[2,2,48,768]{3,2,1,0:T(8,128)}, f32[2,2,48,768]{3,2,1,0:T(8,128)S(1)}, u32[]{:S(2)}, u32[]{:S(2)}) %collective-permute-start.4) | collective-permute-done | bytes 589856 | tf_op jit(solution)/shard_map/ppermute | solution.py:469
  31.5 0.0 collective-permute-done.5.refs_0_.side
  31.5 1.2 %shard_map.88 = (f32[192,128]{1,0:T(8,128)S(1)}, f32[192,128]{1,0:T(8,128)S(1)}) custom-call(f32[6,2,2,48,128]{4,3,2,1,0:T(8,128)S(1)} %get-tuple-element.20.refs_0_.own, f32[2,2,48,768]{3,2,1,0:T(8,128)S(1)} %collective-permute-done.4.before, f32[2,2,48,768]{3,2,1,0:T(8,128)S(1)} %collective-permute-done.1.refs_7_.refs_8_.refs_9_.refs_10_.refs_11_.refs_12_.after, ...), custom_call_target="tpu_custom_call" | custom-call | flops 1000000 | bytes 1000000 | tf_op jit(solution)/shard_map/pallas_call | solution.py:248
  32.7 1.3 %collective-permute-start.7 = (f32[192,128]{1,0:T(8,128)S(1)}, f32[192,128]{1,0:T(8,128)S(1)}, u32[]{:S(2)}, u32[]{:S(2)}) collective-permute-start(f32[192,128]{1,0:T(8,128)S(1)} %get-tuple-element.23.refs_0_), channel_id=1, source_target_pairs={{0,497},{1,496},{256,241},{257,240},{2,499},{3,498},{258,243},{259... | collective-permute-start | bytes 294920 | tf_op jit(solution)/shard_map/ppermute | solution.py:470
  34.0 1.3 %collective-permute-start.8 = (f32[192,128]{1,0:T(8,128)S(1)}, f32[192,128]{1,0:T(8,128)S(1)}, u32[]{:S(2)}, u32[]{:S(2)}) collective-permute-start(f32[192,128]{1,0:T(8,128)S(1)} %get-tuple-element.28), channel_id=1, source_target_pairs={{0,496},{256,240},{1,497},{257,241},{2,498},{258,242},{3,499},{259... | collective-permute-start | bytes 294920 | tf_op jit(solution)/shard_map/ppermute | solution.py:469
  35.3 0.0 collective-permute-done.2.before
  35.3 0.2 shard_map.89
  35.5 0.7 %collective-permute-start.10 = (f32[192,128]{1,0:T(8,128)S(1)}, f32[192,128]{1,0:T(8,128)S(1)}, u32[]{:S(2)}, u32[]{:S(2)}) collective-permute-start(f32[192,128]{1,0:T(8,128)S(1)} %get-tuple-element.32), channel_id=1, source_target_pairs={{240,224},{496,480},{241,225},{497,481},{242,226},{498,482},{243,2... | collective-permute-start | bytes 294920 | tf_op jit(solution)/shard_map/ppermute | solution.py:469
  36.2 0.7 %collective-permute-start.9 = (f32[24,128]{1,0:T(8,128)S(1)}, f32[24,128]{1,0:T(8,128)S(1)}, u32[]{:S(2)}, u32[]{:S(2)}) collective-permute-start(f32[24,128]{1,0:T(8,128)S(1)} %get-tuple-element.31), channel_id=1, source_target_pairs={{240,225},{241,224},{496,481},{497,480},{242,227},{243,226},{498,4... | collective-permute-start | bytes 36872 | tf_op jit(solution)/shard_map/ppermute | solution.py:470
  36.9 1.2 %collective-permute-done.8.low_back = f32[192,128]{1,0:T(8,128)S(1)} collective-permute-done((f32[192,128]{1,0:T(8,128)S(1)}, f32[192,128]{1,0:T(8,128)S(1)}, u32[]{:S(2)}, u32[]{:S(2)}) %collective-permute-start.8) | collective-permute-done | bytes 98336 | tf_op jit(solution)/shard_map/ppermute | solution.py:469
  38.2 0.0 collective-permute-done.9.high_side
  38.2 0.0 collective-permute-done.10.high_back
  38.2 0.0 copy-start
  38.2 0.0 copy-start.1
  38.2 0.0 copy-start.2
  38.2 0.0 copy-start.3
  38.2 0.2 shard_map.92
  38.4 4.7 %collective-permute-start.11 = (f32[80,128]{1,0:T(8,128)S(1)}, f32[80,128]{1,0:T(8,128)S(1)}, u32[]{:S(2)}, u32[]{:S(2)}) collective-permute-start(f32[80,128]{1,0:T(8,128)S(1)} %get-tuple-element.34), channel_id=1, source_target_pairs={{2,4},{4,2},{6,8},{8,6},{10,12},{12,10},{3,5},{5,3},{7,9},{9,7},{1... | collective-permute-start | bytes 122888 | tf_op jit(solution)/shard_map/ppermute | solution.py:498
  43.1 1.9 %collective-permute-start.12 = (f32[80,128]{1,0:T(8,128)S(1)}, f32[80,128]{1,0:T(8,128)S(1)}, u32[]{:S(2)}, u32[]{:S(2)}) collective-permute-start(f32[80,128]{1,0:T(8,128)S(1)} %get-tuple-element.35), channel_id=1, source_target_pairs={{0,2},{2,0},{4,6},{6,4},{8,10},{10,8},{12,14},{14,12},{1,3},{3,1},... | collective-permute-start | bytes 122888 | tf_op jit(solution)/shard_map/ppermute | solution.py:497
  45.0 0.0 collective-permute-done.11.across
  45.0 1.2 %collective-permute-done.12.chip = f32[80,128]{1,0:T(8,128)S(1)} collective-permute-done((f32[80,128]{1,0:T(8,128)S(1)}, f32[80,128]{1,0:T(8,128)S(1)}, u32[]{:S(2)}, u32[]{:S(2)}) %collective-permute-start.12) | collective-permute-done | bytes 40992 | tf_op jit(solution)/shard_map/ppermute | solution.py:497
  46.2 1.9 %shard_map.93 = (f32[2,3,2,24,96]{4,3,2,1,0:T(8,128)}, f32[2,3,2,24,96]{4,3,2,1,0:T(8,128)}) custom-call(f32[480,128]{1,0:T(8,128)S(1)} %get-tuple-element.33.picked, f32[80,128]{1,0:T(8,128)S(1)} %collective-permute-done.11.across, f32[80,128]{1,0:T(8,128)S(1)} %collective-permute-done.12.chip, bf16[384,256]{1,0:T(8,128)(2,1)S(1)} %copy-done, ...), custom_call_target="tpu_custom_call" | custom-call | flops 1000000 | bytes 1000000 | tf_op jit(solution)/shard_map/pallas_call | solution.py:500
  (12 shorter events, 0.1 us)
Async XLA Ops:
  0.6 23.1 %collective-permute-start = (f32[2,2,48,768]{3,2,1,0:T(8,128)}, f32[2,2,48,768]{3,2,1,0:T(8,128)S(1)}, u32[]{:S(2)}, u32[]{:S(2)}) collective-permute-start(f32[2,2,48,768]{3,2,1,0:T(8,128)} %source.1), channel_id=1, source_target_pairs={{0,16},{16,32},{32,48},{48,64},{64,80},{80,96},{96,112},{112,128},... | collective-permute-start | bytes 1769480 | tf_op jit(solution)/shard_map/ppermute | solution.py:469
  5.0 18.7 %collective-permute-start.1 = (f32[2,2,48,768]{3,2,1,0:T(8,128)}, f32[2,2,48,768]{3,2,1,0:T(8,128)S(1)}, u32[]{:S(2)}, u32[]{:S(2)}) collective-permute-start(f32[2,2,48,768]{3,2,1,0:T(8,128)} %source.1), channel_id=1, source_target_pairs={{16,0},{32,16},{48,32},{64,48},{80,64},{96,80},{112,96},{128,112},... | collective-permute-start | bytes 1769480 | tf_op jit(solution)/shard_map/ppermute | solution.py:469
  6.3 25.2 %collective-permute-start.4 = (f32[2,2,48,768]{3,2,1,0:T(8,128)}, f32[2,2,48,768]{3,2,1,0:T(8,128)S(1)}, u32[]{:S(2)}, u32[]{:S(2)}) collective-permute-start(f32[2,2,48,768]{3,2,1,0:T(8,128)} %source.1), channel_id=1, source_target_pairs={{240,256},{496,0},{241,257},{497,1},{242,258},{498,2},{243,259},{4... | collective-permute-start | bytes 1769480 | tf_op jit(solution)/shard_map/ppermute | solution.py:469
  7.6 27.7 %collective-permute-start.2 = (f32[2,2,48,768]{3,2,1,0:T(8,128)}, f32[2,2,48,768]{3,2,1,0:T(8,128)S(1)}, u32[]{:S(2)}, u32[]{:S(2)}) collective-permute-start(f32[2,2,48,768]{3,2,1,0:T(8,128)} %source.1), channel_id=1, source_target_pairs={{224,240},{480,496},{225,241},{481,497},{226,242},{482,498},{227,2... | collective-permute-start | bytes 1769480 | tf_op jit(solution)/shard_map/ppermute | solution.py:469
  8.4 27.0 %collective-permute-start.3 = (f32[2,2,48,768]{3,2,1,0:T(8,128)}, f32[2,2,48,768]{3,2,1,0:T(8,128)S(1)}, u32[]{:S(2)}, u32[]{:S(2)}) collective-permute-start(f32[2,2,48,768]{3,2,1,0:T(8,128)} %source.1), channel_id=1, source_target_pairs={{0,496},{256,240},{1,497},{257,241},{2,498},{258,242},{3,499},{259... | collective-permute-start | bytes 1769480 | tf_op jit(solution)/shard_map/ppermute | solution.py:469
  25.1 6.4 %collective-permute-start.5 = (f32[24,128]{1,0:T(8,128)S(1)}, f32[24,128]{1,0:T(8,128)S(1)}, u32[]{:S(2)}, u32[]{:S(2)}) collective-permute-start(f32[24,128]{1,0:T(8,128)S(1)} %get-tuple-element.22), channel_id=1, source_target_pairs={{16,1},{17,0},{32,17},{33,16},{48,33},{49,32},{64,49},{65,48},{80,... | collective-permute-start | bytes 36872 | tf_op jit(solution)/shard_map/ppermute | solution.py:470
  26.4 10.5 %collective-permute-start.6 = (f32[192,128]{1,0:T(8,128)S(1)}, f32[192,128]{1,0:T(8,128)S(1)}, u32[]{:S(2)}, u32[]{:S(2)}) collective-permute-start(f32[192,128]{1,0:T(8,128)S(1)} %get-tuple-element.25), channel_id=1, source_target_pairs={{16,0},{32,16},{48,32},{64,48},{80,64},{96,80},{112,96},{128,112},... | collective-permute-start | bytes 294920 | tf_op jit(solution)/shard_map/ppermute | solution.py:469
  32.7 4.2 %collective-permute-start.7 = (f32[192,128]{1,0:T(8,128)S(1)}, f32[192,128]{1,0:T(8,128)S(1)}, u32[]{:S(2)}, u32[]{:S(2)}) collective-permute-start(f32[192,128]{1,0:T(8,128)S(1)} %get-tuple-element.23.refs_0_), channel_id=1, source_target_pairs={{0,497},{1,496},{256,241},{257,240},{2,499},{3,498},{258,243},{259... | collective-permute-start | bytes 294920 | tf_op jit(solution)/shard_map/ppermute | solution.py:470
  34.0 4.1 %collective-permute-start.8 = (f32[192,128]{1,0:T(8,128)S(1)}, f32[192,128]{1,0:T(8,128)S(1)}, u32[]{:S(2)}, u32[]{:S(2)}) collective-permute-start(f32[192,128]{1,0:T(8,128)S(1)} %get-tuple-element.28), channel_id=1, source_target_pairs={{0,496},{256,240},{1,497},{257,241},{2,498},{258,242},{3,499},{259... | collective-permute-start | bytes 294920 | tf_op jit(solution)/shard_map/ppermute | solution.py:469
  35.5 2.6 %collective-permute-start.10 = (f32[192,128]{1,0:T(8,128)S(1)}, f32[192,128]{1,0:T(8,128)S(1)}, u32[]{:S(2)}, u32[]{:S(2)}) collective-permute-start(f32[192,128]{1,0:T(8,128)S(1)} %get-tuple-element.32), channel_id=1, source_target_pairs={{240,224},{496,480},{241,225},{497,481},{242,226},{498,482},{243,2... | collective-permute-start | bytes 294920 | tf_op jit(solution)/shard_map/ppermute | solution.py:469
  36.2 2.0 %collective-permute-start.9 = (f32[24,128]{1,0:T(8,128)S(1)}, f32[24,128]{1,0:T(8,128)S(1)}, u32[]{:S(2)}, u32[]{:S(2)}) collective-permute-start(f32[24,128]{1,0:T(8,128)S(1)} %get-tuple-element.31), channel_id=1, source_target_pairs={{240,225},{241,224},{496,481},{497,480},{242,227},{243,226},{498,4... | collective-permute-start | bytes 36872 | tf_op jit(solution)/shard_map/ppermute | solution.py:470
  38.1 8.1 %copy-start.4 = (bf16[48,192]{1,0:T(8,128)(2,1)S(1)}, bf16[48,192]{1,0:T(8,128)(2,1)}, u32[]{:S(2)}) copy-start(bf16[48,192]{1,0:T(8,128)(2,1)} %constant.14.clone.up) | copy-start | bytes 55300
  38.2 8.0 %copy-start = (bf16[384,256]{1,0:T(8,128)(2,1)S(1)}, bf16[384,256]{1,0:T(8,128)(2,1)}, u32[]{:S(2)}) copy-start(bf16[384,256]{1,0:T(8,128)(2,1)} %constant.10.clone.forward) | copy-start | bytes 589828
  38.2 8.0 %copy-start.1 = (bf16[384,256]{1,0:T(8,128)(2,1)S(1)}, bf16[384,256]{1,0:T(8,128)(2,1)}, u32[]{:S(2)}) copy-start(bf16[384,256]{1,0:T(8,128)(2,1)} %constant.12.clone.inverse) | copy-start | bytes 589828
  38.2 8.0 %copy-start.2 = (bf16[256,256]{1,0:T(8,128)(2,1)S(1)}, bf16[256,256]{1,0:T(8,128)(2,1)}, u32[]{:S(2)}) copy-start(bf16[256,256]{1,0:T(8,128)(2,1)} %constant.11.clone.spread) | copy-start | bytes 393220
  38.2 8.0 %copy-start.3 = (bf16[64,192]{1,0:T(8,128)(2,1)S(1)}, bf16[64,192]{1,0:T(8,128)(2,1)}, u32[]{:S(2)}) copy-start(bf16[64,192]{1,0:T(8,128)(2,1)} %constant.13.clone.down) | copy-start | bytes 73732
  38.4 6.6 %collective-permute-start.11 = (f32[80,128]{1,0:T(8,128)S(1)}, f32[80,128]{1,0:T(8,128)S(1)}, u32[]{:S(2)}, u32[]{:S(2)}) collective-permute-start(f32[80,128]{1,0:T(8,128)S(1)} %get-tuple-element.34), channel_id=1, source_target_pairs={{2,4},{4,2},{6,8},{8,6},{10,12},{12,10},{3,5},{5,3},{7,9},{9,7},{1... | collective-permute-start | bytes 122888 | tf_op jit(solution)/shard_map/ppermute | solution.py:498
  43.1 3.1 %collective-permute-start.12 = (f32[80,128]{1,0:T(8,128)S(1)}, f32[80,128]{1,0:T(8,128)S(1)}, u32[]{:S(2)}, u32[]{:S(2)}) collective-permute-start(f32[80,128]{1,0:T(8,128)S(1)} %get-tuple-element.35), channel_id=1, source_target_pairs={{0,2},{2,0},{4,6},{6,4},{8,10},{10,8},{12,14},{14,12},{1,3},{3,1},... | collective-permute-start | bytes 122888 | tf_op jit(solution)/shard_map/ppermute | solution.py:497

commit v6 on v5

--- a/solution.py
+++ b/solution.py
@@ -143,7 +143,36 @@
             stage[pl.ds(n * half, half), lanes] = value
 
 
-def meet(stage, image, tiles, half, wanted, *outs):
+def pack(planes):
+    lanes = lane_index(planes[0].shape)
+    packed = []
+    for n in range(0, len(planes), 4):
+        shifts = (-MARGIN, 3 * STRIP - MARGIN, 2 * STRIP - MARGIN, STRIP - MARGIN)
+        a, b, c, d = [pltpu.roll(v, shift % LANES, 1) for v, shift in zip(planes[n : n + 4], shifts)]
+        packed += [jnp.where(lanes < (3 - k) * STRIP, v, w) for k, (v, w) in enumerate(((a, b), (b, c), (c, d)))]
+    return packed
+
+
+def unpack(packed):
+    lanes = lane_index(packed[0].shape)
+    cells = (lanes >= MARGIN) & (lanes < RIGHT)
+    planes = []
+    for n in range(0, len(packed), 3):
+        first, second, third = packed[n : n + 3]
+        b = jnp.where(lanes >= 3 * STRIP, first, second)
+        c = jnp.where(lanes >= 2 * STRIP, second, third)
+        shifts = (MARGIN, MARGIN - 3 * STRIP, MARGIN - 2 * STRIP, MARGIN - STRIP)
+        moved = [pltpu.roll(v, shift % LANES, 1) for v, shift in zip((first, b, c, third), shifts)]
+        planes += [jnp.where(cells, v, 0.0) for v in moved]
+    return planes
+
+
+def store(target, planes):
+    for n, value in enumerate(planes):
+        target[pl.ds(n * KEEP, KEEP), :] = value
+
+
+def meet(stage, image, tiles, half, wanted, target, side):
     pairs, slots = wanted
     fill(stage, image, tiles, half, pairs, slots)
     at_left = lax.axis_index("col") == 0
@@ -166,10 +195,12 @@
             row = jnp.where(block == k, pltpu.roll(value, STRIP * k, 1) if k else value, row)
         stage[rows, pl.ds(tile * LANES, LANES)] = row
     means = split_dot(stage[...], looks_table(tiles * LANES))
-    at = 0
-    for out in outs:
-        out[...] = means[at : at + out.shape[0]]
-        at += out.shape[0]
+    count = 2 * len(pairs) + len(slots)
+    if wanted is GOING:
+        store(target, pack([means[n * half : (n + 1) * half] for n in range(count)]))
+    else:
+        target[...] = means[: count * half]
+    side[...] = means[count * half :]
 
 
 ALL = (HELD + SENT, (0, 1, 2, 3))
@@ -192,8 +223,9 @@
     kept, going = 2 * len(HELD) * half, 2 * len(SENT) * half
     held[pl.ds(0, kept), :] = means[pl.ds(0, kept), :]
     held[pl.ds(kept, 4 * half), :] = means[pl.ds(kept + going, 4 * half), :]
-    sent[pl.ds(0, going), :] = means[pl.ds(kept, going), :]
-    sent[pl.ds(going, 2 * half), :] = means[pl.ds(kept + going + 2 * half, 2 * half), :]
+    starts = [kept + n * half for n in range(2 * len(SENT))]
+    starts += [kept + going + n * half for n in (2, 3)]
+    store(sent, pack([means[pl.ds(start, half), :] for start in starts]))
 
 
 def end_kernel(run, own, before, after, *refs):
@@ -231,13 +263,14 @@
 
 
 STAYING, LEAVING = 2 * len(HELD) + 4, 2 * len(SENT) + 2
+PACKED = LEAVING * 3 // 4
 BOTH = 2 * len(HELD + SENT) + 4
 
 
 def at_end(run, own, before, after, *behind):
     rows, cols = after.shape[2:]
     half, tiles = rows // 2, cols // LANES
-    outs = (LEAVING, 8) if run == 0 else (STAYING, LEAVING, 1)
+    outs = (PACKED, PACKED) if run == 0 else (STAYING, PACKED, 1)
     total = LEAVING if run == 0 else BOTH
     scratch = [
         pltpu.VMEM(((total + 1) * half, cols), F32),
@@ -258,7 +291,7 @@
     rows, cols = images[0].shape[2:]
     half = rows // 2
     whole = lambda shape: pl.BlockSpec(shape, lambda i: (0,) * len(shape))
-    outs = planes_of(rows, STAYING, LEAVING, 1)
+    outs = planes_of(rows, STAYING, PACKED, 1)
     return pl.pallas_call(
         near_kernel,
         grid=(1,),
@@ -301,13 +334,14 @@
     place = lax.axis_index("date") % RUN
     from_low, from_high = place == RUN - 1, place == RUN - 2
     columns = jnp.where(from_high, high_side[...], side[...])
+    rows = [pl.ds(n * KEEP, KEEP) for n in range(back.shape[0] // KEEP)]
+    returned = unpack([jnp.where(from_high, high_back[r, :], back[r, :]) for r in rows])
     held_at, back_at = 0, 0
     for n in range(PLANES):
         pair = n // 2
         from_back = pair in (3, 6, 7) or n >= PLANES - 2
         if from_back:
-            rows = pl.ds(back_at * KEEP, KEEP)
-            value, back_at = jnp.where(from_high, high_back[rows, :], back[rows, :]), back_at + 1
+            value, back_at = returned[back_at], back_at + 1
         else:
             rows = pl.ds(held_at * KEEP, KEEP)
             value, held_at = jnp.where(from_low, last_held[rows, :], held[rows, :]), held_at + 1
@@ -484,8 +518,8 @@
     low_side, low_back = across(low_side, low), along(sent, low)
     last_held, sent, high_side = at_end(RUN - 1, own, before_last, after_wrap, formed)
     high_side, high_back = across(high_side, high), along(sent, high)
-    side, back = call(arrived_kernel, planes_of(rows, 1, LEAVING), 2)(side, back)
-    side, back = call(merge_kernel, planes_of(rows, 1, LEAVING), 4)(side, back, low_side, low_back)
+    side, back = call(arrived_kernel, planes_of(rows, 1, PACKED), 2)(side, back)
+    side, back = call(merge_kernel, planes_of(rows, 1, PACKED), 4)(side, back, low_side, low_back)
 
     planes = 3 * 2 * LINKS + 2
     rim = jax.ShapeDtypeStruct((planes * MARGIN, LANES), F32)

time: 48.5 us -> 47.7 us (0.984)
  waiting for transfers between devices: 6.24 us -> 5.02 us
    ppermute x8, waiting for transfers between devices: 5.05 us -> 3.83 us  [body(): along = lambda value, pairs: lax.ppermute(value, 'date', pairs)]
  transfers between devices with their start and end apart: 13 -> 13, of which waited for: 3 -> 2; matrix products, arithmetic and copies ran while one was open for 0% -> 0% of each run, Pallas kernels for 10% -> 10%
where the time goes in v6:
time: 47.7 us; the launch traced here: 47.3 us
  starting transfers between devices  34.6 us (73%)
  Pallas kernels  6.77 us (14%)
  waiting for transfers between devices  5.02 us (11%)
  between operations  0.9 us (2%)
    ppermute x8, starting transfers between devices, body(): along = lambda value, pairs: lax.ppermute(value, 'date', pairs)  24.4 us
    ppermute x1, starting transfers between devices, body(): lax.ppermute(across, 'row', [(i, (i + 1 ^ 1) - 1) for i in range(1, count...  5.01 us
    ppermute x8, waiting for transfers between devices, body(): along = lambda value, pairs: lax.ppermute(value, 'date', pairs)  3.83 us
    ppermute x3, starting transfers between devices, body(): lax.ppermute(value, ('date', 'col'), [(2 * d + c, 2 * e + (c ^ 1)) for d,...  3.25 us
    ppermute x1, starting transfers between devices, body(): chip = lax.ppermute(chip, 'row', [(i, i ^ 1) for i in range(count)])  1.92 us
    pallas_call x1, Pallas kernels, kept(): pl.pallas_call(keep_kernel, out_shape=(pltpu.VMEM((tiles,) + images.shape...  1.88 us
    pallas_call x1, Pallas kernels, body(): call(filter_kernel, (out, out), 8, [pltpu.VMEM((planes, PATCH, LANES), F3...  1.85 us
    pallas_call x2, Pallas kernels, at_end(): call(functools.partial(end_kernel, run), planes_of(rows, *outs), 3 + len(...  1.44 us
  transfers between devices with their start and end apart: 13, of which 2 were waited for; matrix products, arithmetic and copies ran while one was open for 0% of the time, Pallas kernels for 10%

profile of v6, /device:TPU:1, one launch (start us, length us, event | category | flops | bytes accessed | tf_op | source)
XLA Modules:
  0.0 47.3 jit_solution(15805675709457340384)
XLA Ops:
  0.6 4.4 %collective-permute-start = (f32[2,2,48,768]{3,2,1,0:T(8,128)}, f32[2,2,48,768]{3,2,1,0:T(8,128)S(1)}, u32[]{:S(2)}, u32[]{:S(2)}) collective-permute-start(f32[2,2,48,768]{3,2,1,0:T(8,128)} %source.1), channel_id=1, source_target_pairs={{0,16},{16,32},{32,48},{48,64},{64,80},{80,96},{96,112},{112,128},... | collective-permute-start | bytes 1769480 | tf_op jit(solution)/shard_map/ppermute | solution.py:503
  5.0 1.3 %collective-permute-start.1 = (f32[2,2,48,768]{3,2,1,0:T(8,128)}, f32[2,2,48,768]{3,2,1,0:T(8,128)S(1)}, u32[]{:S(2)}, u32[]{:S(2)}) collective-permute-start(f32[2,2,48,768]{3,2,1,0:T(8,128)} %source.1), channel_id=1, source_target_pairs={{16,0},{32,16},{48,32},{64,48},{80,64},{96,80},{112,96},{128,112},... | collective-permute-start | bytes 1769480 | tf_op jit(solution)/shard_map/ppermute | solution.py:503
  6.3 1.3 %collective-permute-start.4 = (f32[2,2,48,768]{3,2,1,0:T(8,128)}, f32[2,2,48,768]{3,2,1,0:T(8,128)S(1)}, u32[]{:S(2)}, u32[]{:S(2)}) collective-permute-start(f32[2,2,48,768]{3,2,1,0:T(8,128)} %source.1), channel_id=1, source_target_pairs={{240,256},{496,0},{241,257},{497,1},{242,258},{498,2},{243,259},{4... | collective-permute-start | bytes 1769480 | tf_op jit(solution)/shard_map/ppermute | solution.py:503
  7.6 0.7 %collective-permute-start.2 = (f32[2,2,48,768]{3,2,1,0:T(8,128)}, f32[2,2,48,768]{3,2,1,0:T(8,128)S(1)}, u32[]{:S(2)}, u32[]{:S(2)}) collective-permute-start(f32[2,2,48,768]{3,2,1,0:T(8,128)} %source.1), channel_id=1, source_target_pairs={{224,240},{480,496},{225,241},{481,497},{226,242},{482,498},{227,2... | collective-permute-start | bytes 1769480 | tf_op jit(solution)/shard_map/ppermute | solution.py:503
  8.4 13.5 %collective-permute-start.3 = (f32[2,2,48,768]{3,2,1,0:T(8,128)}, f32[2,2,48,768]{3,2,1,0:T(8,128)S(1)}, u32[]{:S(2)}, u32[]{:S(2)}) collective-permute-start(f32[2,2,48,768]{3,2,1,0:T(8,128)} %source.1), channel_id=1, source_target_pairs={{0,496},{256,240},{1,497},{257,241},{2,498},{258,242},{3,499},{259... | collective-permute-start | bytes 1769480 | tf_op jit(solution)/shard_map/ppermute | solution.py:503
  21.9 1.9 %shard_map.86 = (f32[6,2,2,48,128]{4,3,2,1,0:T(8,128)S(1)}, s32[8,128]{1,0:T(8,128)S(1)}) custom-call(s32[2,3]{1,0:T(2,128)} %secondaries.1, f32[2,2,48,768]{3,2,1,0:T(8,128)} %source.1), custom_call_target="tpu_custom_call" | custom-call | tf_op jit(solution)/shard_map/pallas_call | solution.py:95
  23.7 0.0 collective-permute-done.refs_1_.refs_2_.refs_3_.refs_4_.refs_5_.refs_6_
  23.8 0.0 collective-permute-done.1.refs_7_.refs_8_.refs_9_.refs_10_.refs_11_.refs_12_.after
  23.8 1.4 %shard_map.87 = (f32[336,128]{1,0:T(8,128)S(1)}, f32[144,128]{1,0:T(8,128)S(1)}, f32[24,128]{1,0:T(8,128)S(1)}) custom-call(f32[6,2,2,48,128]{4,3,2,1,0:T(8,128)S(1)} %get-tuple-element.20.refs_0_.own, f32[2,2,48,768]{3,2,1,0:T(8,128)S(1)} %collective-permute-done.refs_1_.refs_2_.refs_3_.refs_4_.refs_5_.refs_6_, ...), custom_call_target="tpu_custom_call" | custom-call | tf_op jit(solution)/shard_map/pallas_call | solution.py:295
  25.1 1.3 %collective-permute-start.5 = (f32[24,128]{1,0:T(8,128)S(1)}, f32[24,128]{1,0:T(8,128)S(1)}, u32[]{:S(2)}, u32[]{:S(2)}) collective-permute-start(f32[24,128]{1,0:T(8,128)S(1)} %get-tuple-element.22), channel_id=1, source_target_pairs={{16,1},{17,0},{32,17},{33,16},{48,33},{49,32},{64,49},{65,48},{80,... | collective-permute-start | bytes 36872 | tf_op jit(solution)/shard_map/ppermute | solution.py:504
  26.4 1.3 %collective-permute-start.6 = (f32[144,128]{1,0:T(8,128)S(1)}, f32[144,128]{1,0:T(8,128)S(1)}, u32[]{:S(2)}, u32[]{:S(2)}) collective-permute-start(f32[144,128]{1,0:T(8,128)S(1)} %get-tuple-element.25), channel_id=1, source_target_pairs={{16,0},{32,16},{48,32},{64,48},{80,64},{96,80},{112,96},{128,112},... | collective-permute-start | bytes 221192 | tf_op jit(solution)/shard_map/ppermute | solution.py:503
  27.7 3.8 %collective-permute-done.4.before = f32[2,2,48,768]{3,2,1,0:T(8,128)S(1)} collective-permute-done((f32[2,2,48,768]{3,2,1,0:T(8,128)}, f32[2,2,48,768]{3,2,1,0:T(8,128)S(1)}, u32[]{:S(2)}, u32[]{:S(2)}) %collective-permute-start.4) | collective-permute-done | bytes 589856 | tf_op jit(solution)/shard_map/ppermute | solution.py:503
  31.5 1.3 %shard_map.88 = (f32[144,128]{1,0:T(8,128)S(1)}, f32[144,128]{1,0:T(8,128)S(1)}) custom-call(f32[6,2,2,48,128]{4,3,2,1,0:T(8,128)S(1)} %get-tuple-element.20.refs_0_.own, f32[2,2,48,768]{3,2,1,0:T(8,128)S(1)} %collective-permute-done.4.before, f32[2,2,48,768]{3,2,1,0:T(8,128)S(1)} %collective-permute-done.1.refs_7_.refs_8_.refs_9_.refs_10_.refs_11_.refs_12_.after, ...), custom_call_target="tpu_custom_call" | custom-call | flops 1000000 | bytes 1000000 | tf_op jit(solution)/shard_map/pallas_call | solution.py:281
  32.8 1.3 %collective-permute-start.7 = (f32[144,128]{1,0:T(8,128)S(1)}, f32[144,128]{1,0:T(8,128)S(1)}, u32[]{:S(2)}, u32[]{:S(2)}) collective-permute-start(f32[144,128]{1,0:T(8,128)S(1)} %get-tuple-element.23.refs_0_), channel_id=1, source_target_pairs={{0,497},{1,496},{256,241},{257,240},{2,499},{3,498},{258,243},{259... | collective-permute-start | bytes 221192 | tf_op jit(solution)/shard_map/ppermute | solution.py:504
  34.1 1.3 %collective-permute-start.8 = (f32[144,128]{1,0:T(8,128)S(1)}, f32[144,128]{1,0:T(8,128)S(1)}, u32[]{:S(2)}, u32[]{:S(2)}) collective-permute-start(f32[144,128]{1,0:T(8,128)S(1)} %get-tuple-element.28), channel_id=1, source_target_pairs={{0,496},{256,240},{1,497},{257,241},{2,498},{258,242},{3,499},{259... | collective-permute-start | bytes 221192 | tf_op jit(solution)/shard_map/ppermute | solution.py:503
  35.4 0.0 collective-permute-done.3.after
  35.4 0.2 shard_map.89
  35.6 0.7 %collective-permute-start.10 = (f32[144,128]{1,0:T(8,128)S(1)}, f32[144,128]{1,0:T(8,128)S(1)}, u32[]{:S(2)}, u32[]{:S(2)}) collective-permute-start(f32[144,128]{1,0:T(8,128)S(1)} %get-tuple-element.32), channel_id=1, source_target_pairs={{240,224},{496,480},{241,225},{497,481},{242,226},{498,482},{243,2... | collective-permute-start | bytes 221192 | tf_op jit(solution)/shard_map/ppermute | solution.py:503
  36.3 0.7 %collective-permute-start.9 = (f32[24,128]{1,0:T(8,128)S(1)}, f32[24,128]{1,0:T(8,128)S(1)}, u32[]{:S(2)}, u32[]{:S(2)}) collective-permute-start(f32[24,128]{1,0:T(8,128)S(1)} %get-tuple-element.31), channel_id=1, source_target_pairs={{240,225},{241,224},{496,481},{497,480},{242,227},{243,226},{498,4... | collective-permute-start | bytes 36872 | tf_op jit(solution)/shard_map/ppermute | solution.py:504
  36.9 0.0 collective-permute-done.6.back
  37.0 0.0 collective-permute-done.7.low_side
  37.0 0.0 collective-permute-done.8.low_back
  37.0 0.0 collective-permute-done.9.high_side
  37.1 0.0 copy-start
  37.1 0.0 copy-start.1
  37.1 0.0 copy-start.2
  37.1 0.2 shard_map.92
  37.3 5.0 %collective-permute-start.11 = (f32[80,128]{1,0:T(8,128)S(1)}, f32[80,128]{1,0:T(8,128)S(1)}, u32[]{:S(2)}, u32[]{:S(2)}) collective-permute-start(f32[80,128]{1,0:T(8,128)S(1)} %get-tuple-element.34), channel_id=1, source_target_pairs={{2,4},{4,2},{6,8},{8,6},{10,12},{12,10},{3,5},{5,3},{7,9},{9,7},{1... | collective-permute-start | bytes 122888 | tf_op jit(solution)/shard_map/ppermute | solution.py:532
  42.3 1.9 %collective-permute-start.12 = (f32[80,128]{1,0:T(8,128)S(1)}, f32[80,128]{1,0:T(8,128)S(1)}, u32[]{:S(2)}, u32[]{:S(2)}) collective-permute-start(f32[80,128]{1,0:T(8,128)S(1)} %get-tuple-element.35), channel_id=1, source_target_pairs={{0,2},{2,0},{4,6},{6,4},{8,10},{10,8},{12,14},{14,12},{1,3},{3,1},... | collective-permute-start | bytes 122888 | tf_op jit(solution)/shard_map/ppermute | solution.py:531
  44.3 0.0 collective-permute-done.11.across
  44.3 1.2 %collective-permute-done.12.chip = f32[80,128]{1,0:T(8,128)S(1)} collective-permute-done((f32[80,128]{1,0:T(8,128)S(1)}, f32[80,128]{1,0:T(8,128)S(1)}, u32[]{:S(2)}, u32[]{:S(2)}) %collective-permute-start.12) | collective-permute-done | bytes 40992 | tf_op jit(solution)/shard_map/ppermute | solution.py:531
  45.5 1.8 %shard_map.93 = (f32[2,3,2,24,96]{4,3,2,1,0:T(8,128)}, f32[2,3,2,24,96]{4,3,2,1,0:T(8,128)}) custom-call(f32[480,128]{1,0:T(8,128)S(1)} %get-tuple-element.33.picked, f32[80,128]{1,0:T(8,128)S(1)} %collective-permute-done.11.across, f32[80,128]{1,0:T(8,128)S(1)} %collective-permute-done.12.chip, bf16[384,256]{1,0:T(8,128)(2,1)S(1)} %copy-done, ...), custom_call_target="tpu_custom_call" | custom-call | flops 1000000 | bytes 1000000 | tf_op jit(solution)/shard_map/pallas_call | solution.py:534
  (12 shorter events, 0.0 us)
Async XLA Ops:
  0.6 23.1 %collective-permute-start = (f32[2,2,48,768]{3,2,1,0:T(8,128)}, f32[2,2,48,768]{3,2,1,0:T(8,128)S(1)}, u32[]{:S(2)}, u32[]{:S(2)}) collective-permute-start(f32[2,2,48,768]{3,2,1,0:T(8,128)} %source.1), channel_id=1, source_target_pairs={{0,16},{16,32},{32,48},{48,64},{64,80},{80,96},{96,112},{112,128},... | collective-permute-start | bytes 1769480 | tf_op jit(solution)/shard_map/ppermute | solution.py:503
  5.0 18.7 %collective-permute-start.1 = (f32[2,2,48,768]{3,2,1,0:T(8,128)}, f32[2,2,48,768]{3,2,1,0:T(8,128)S(1)}, u32[]{:S(2)}, u32[]{:S(2)}) collective-permute-start(f32[2,2,48,768]{3,2,1,0:T(8,128)} %source.1), channel_id=1, source_target_pairs={{16,0},{32,16},{48,32},{64,48},{80,64},{96,80},{112,96},{128,112},... | collective-permute-start | bytes 1769480 | tf_op jit(solution)/shard_map/ppermute | solution.py:503
  6.3 25.2 %collective-permute-start.4 = (f32[2,2,48,768]{3,2,1,0:T(8,128)}, f32[2,2,48,768]{3,2,1,0:T(8,128)S(1)}, u32[]{:S(2)}, u32[]{:S(2)}) collective-permute-start(f32[2,2,48,768]{3,2,1,0:T(8,128)} %source.1), channel_id=1, source_target_pairs={{240,256},{496,0},{241,257},{497,1},{242,258},{498,2},{243,259},{4... | collective-permute-start | bytes 1769480 | tf_op jit(solution)/shard_map/ppermute | solution.py:503
  7.6 27.7 %collective-permute-start.2 = (f32[2,2,48,768]{3,2,1,0:T(8,128)}, f32[2,2,48,768]{3,2,1,0:T(8,128)S(1)}, u32[]{:S(2)}, u32[]{:S(2)}) collective-permute-start(f32[2,2,48,768]{3,2,1,0:T(8,128)} %source.1), channel_id=1, source_target_pairs={{224,240},{480,496},{225,241},{481,497},{226,242},{482,498},{227,2... | collective-permute-start | bytes 1769480 | tf_op jit(solution)/shard_map/ppermute | solution.py:503
  8.4 27.0 %collective-permute-start.3 = (f32[2,2,48,768]{3,2,1,0:T(8,128)}, f32[2,2,48,768]{3,2,1,0:T(8,128)S(1)}, u32[]{:S(2)}, u32[]{:S(2)}) collective-permute-start(f32[2,2,48,768]{3,2,1,0:T(8,128)} %source.1), channel_id=1, source_target_pairs={{0,496},{256,240},{1,497},{257,241},{2,498},{258,242},{3,499},{259... | collective-permute-start | bytes 1769480 | tf_op jit(solution)/shard_map/ppermute | solution.py:503
  25.1 6.4 %collective-permute-start.5 = (f32[24,128]{1,0:T(8,128)S(1)}, f32[24,128]{1,0:T(8,128)S(1)}, u32[]{:S(2)}, u32[]{:S(2)}) collective-permute-start(f32[24,128]{1,0:T(8,128)S(1)} %get-tuple-element.22), channel_id=1, source_target_pairs={{16,1},{17,0},{32,17},{33,16},{48,33},{49,32},{64,49},{65,48},{80,... | collective-permute-start | bytes 36872 | tf_op jit(solution)/shard_map/ppermute | solution.py:504
  26.4 10.5 %collective-permute-start.6 = (f32[144,128]{1,0:T(8,128)S(1)}, f32[144,128]{1,0:T(8,128)S(1)}, u32[]{:S(2)}, u32[]{:S(2)}) collective-permute-start(f32[144,128]{1,0:T(8,128)S(1)} %get-tuple-element.25), channel_id=1, source_target_pairs={{16,0},{32,16},{48,32},{64,48},{80,64},{96,80},{112,96},{128,112},... | collective-permute-start | bytes 221192 | tf_op jit(solution)/shard_map/ppermute | solution.py:503
  32.8 4.2 %collective-permute-start.7 = (f32[144,128]{1,0:T(8,128)S(1)}, f32[144,128]{1,0:T(8,128)S(1)}, u32[]{:S(2)}, u32[]{:S(2)}) collective-permute-start(f32[144,128]{1,0:T(8,128)S(1)} %get-tuple-element.23.refs_0_), channel_id=1, source_target_pairs={{0,497},{1,496},{256,241},{257,240},{2,499},{3,498},{258,243},{259... | collective-permute-start | bytes 221192 | tf_op jit(solution)/shard_map/ppermute | solution.py:504
  34.1 2.9 %collective-permute-start.8 = (f32[144,128]{1,0:T(8,128)S(1)}, f32[144,128]{1,0:T(8,128)S(1)}, u32[]{:S(2)}, u32[]{:S(2)}) collective-permute-start(f32[144,128]{1,0:T(8,128)S(1)} %get-tuple-element.28), channel_id=1, source_target_pairs={{0,496},{256,240},{1,497},{257,241},{2,498},{258,242},{3,499},{259... | collective-permute-start | bytes 221192 | tf_op jit(solution)/shard_map/ppermute | solution.py:503
  35.6 1.5 %collective-permute-start.10 = (f32[144,128]{1,0:T(8,128)S(1)}, f32[144,128]{1,0:T(8,128)S(1)}, u32[]{:S(2)}, u32[]{:S(2)}) collective-permute-start(f32[144,128]{1,0:T(8,128)S(1)} %get-tuple-element.32), channel_id=1, source_target_pairs={{240,224},{496,480},{241,225},{497,481},{242,226},{498,482},{243,2... | collective-permute-start | bytes 221192 | tf_op jit(solution)/shard_map/ppermute | solution.py:503
  36.3 0.8 %collective-permute-start.9 = (f32[24,128]{1,0:T(8,128)S(1)}, f32[24,128]{1,0:T(8,128)S(1)}, u32[]{:S(2)}, u32[]{:S(2)}) collective-permute-start(f32[24,128]{1,0:T(8,128)S(1)} %get-tuple-element.31), channel_id=1, source_target_pairs={{240,225},{241,224},{496,481},{497,480},{242,227},{243,226},{498,4... | collective-permute-start | bytes 36872 | tf_op jit(solution)/shard_map/ppermute | solution.py:504
  37.0 8.4 %copy-start.3 = (bf16[64,192]{1,0:T(8,128)(2,1)S(1)}, bf16[64,192]{1,0:T(8,128)(2,1)}, u32[]{:S(2)}) copy-start(bf16[64,192]{1,0:T(8,128)(2,1)} %constant.13.clone.down) | copy-start | bytes 73732
  37.0 8.4 %copy-start.4 = (bf16[48,192]{1,0:T(8,128)(2,1)S(1)}, bf16[48,192]{1,0:T(8,128)(2,1)}, u32[]{:S(2)}) copy-start(bf16[48,192]{1,0:T(8,128)(2,1)} %constant.14.clone.up) | copy-start | bytes 55300
  37.1 8.4 %copy-start = (bf16[384,256]{1,0:T(8,128)(2,1)S(1)}, bf16[384,256]{1,0:T(8,128)(2,1)}, u32[]{:S(2)}) copy-start(bf16[384,256]{1,0:T(8,128)(2,1)} %constant.10.clone.forward) | copy-start | bytes 589828
  37.1 8.4 %copy-start.1 = (bf16[384,256]{1,0:T(8,128)(2,1)S(1)}, bf16[384,256]{1,0:T(8,128)(2,1)}, u32[]{:S(2)}) copy-start(bf16[384,256]{1,0:T(8,128)(2,1)} %constant.12.clone.inverse) | copy-start | bytes 589828
  37.1 8.4 %copy-start.2 = (bf16[256,256]{1,0:T(8,128)(2,1)S(1)}, bf16[256,256]{1,0:T(8,128)(2,1)}, u32[]{:S(2)}) copy-start(bf16[256,256]{1,0:T(8,128)(2,1)} %constant.11.clone.spread) | copy-start | bytes 393220
  37.3 6.9 %collective-permute-start.11 = (f32[80,128]{1,0:T(8,128)S(1)}, f32[80,128]{1,0:T(8,128)S(1)}, u32[]{:S(2)}, u32[]{:S(2)}) collective-permute-start(f32[80,128]{1,0:T(8,128)S(1)} %get-tuple-element.34), channel_id=1, source_target_pairs={{2,4},{4,2},{6,8},{8,6},{10,12},{12,10},{3,5},{5,3},{7,9},{9,7},{1... | collective-permute-start | bytes 122888 | tf_op jit(solution)/shard_map/ppermute | solution.py:532
  42.3 3.1 %collective-permute-start.12 = (f32[80,128]{1,0:T(8,128)S(1)}, f32[80,128]{1,0:T(8,128)S(1)}, u32[]{:S(2)}, u32[]{:S(2)}) collective-permute-start(f32[80,128]{1,0:T(8,128)S(1)} %get-tuple-element.35), channel_id=1, source_target_pairs={{0,2},{2,0},{4,6},{6,4},{8,10},{10,8},{12,14},{14,12},{1,3},{3,1},... | collective-permute-start | bytes 122888 | tf_op jit(solution)/shard_map/ppermute | solution.py:531
